TPU v7x, 32 devices: a whole 2x2x4 slice. The times are simulated.
32 devices in a mesh: fsdp: 4 (over x, core), seq: 8 (over z, y).
Axes of the slice: x: 2, y: 2, z: 4, core: 2. Of those that a mesh axis runs over, the one named last changes fastest.
Arguments:
- tokens: bfloat16 [4096, 2048], P(('fsdp', 'seq')), may hold values from -6 to 6
- positions: int32 [4096], P(('fsdp', 'seq')), may hold values from 0 to 1023
- doc_start: int32 [4096], P(('fsdp', 'seq')), may hold values from 0 to 63, as said below
- cotangent: bfloat16 [4096, 2048], P(('fsdp', 'seq')), may hold values from -6 to 6
- w_query: bfloat16 [2048, 2048], P(('fsdp', 'seq')), may hold values from -0.1875 to 0.1875
- w_key: bfloat16 [2048, 256], P(('fsdp', 'seq')), may hold values from -0.125 to 0.125
- w_value: bfloat16 [2048, 256], P(('fsdp', 'seq')), may hold values from -0.125 to 0.125
- w_out: bfloat16 [2048, 2048], P(None, ('fsdp', 'seq')), may hold values from -1.5 to 1.5
- attn_gain: bfloat16 [2048], P(('fsdp', 'seq')), may hold values from 0.5 to 1.5
- w_gate: bfloat16 [2048, 5632], P(('fsdp', 'seq')), may hold values from -0.125 to 0.125
- w_up: bfloat16 [2048, 5632], P(('fsdp', 'seq')), may hold values from -0.125 to 0.125
- w_down: bfloat16 [5632, 2048], P(('fsdp', 'seq')), may hold values from -0.078125 to 0.078125
- mlp_gain: bfloat16 [2048], P(('fsdp', 'seq')), may hold values from 0.5 to 1.5
Outputs:
- output: bfloat16 [4096, 2048], P(('fsdp', 'seq'))
- input_grad: float32 [4096, 2048], P(('fsdp', 'seq'))
- grad_query: float32 [2048, 2048], P(('fsdp', 'seq'))
- grad_key: float32 [2048, 256], P(('fsdp', 'seq'))
- grad_value: float32 [2048, 256], P(('fsdp', 'seq'))
- grad_out: float32 [2048, 2048], P(None, ('fsdp', 'seq'))
- grad_attn_gain: float32 [2048], P(('fsdp', 'seq'))
- grad_gate: float32 [2048, 5632], P(('fsdp', 'seq'))
- grad_up: float32 [2048, 5632], P(('fsdp', 'seq'))
- grad_down: float32 [5632, 2048], P(('fsdp', 'seq'))
- grad_mlp_gain: float32 [2048], P(('fsdp', 'seq'))
Inputs may be any that keep to these rules, and one draw needn't show every extreme that they name: `doc_start`: within each sequence of 1024 rows the value is 0 up to a cut c with 1 <= c <= 63 and c from row c to the sequence's end; in one sequence c = 63.
All inputs are finite; a program needn't handle non-finite values.
Results may differ from a plain program's by a relative error of at most 0.017.
Values may be sent and summed in bfloat16 or wider, within the bound.
A program may use at most 384 MiB of HBM per device.

v0:
```python
import jax
import jax.numpy as jnp
from jax import lax
from jax.sharding import PartitionSpec as P

HEADS = 32
KV_HEADS = 4
HEAD_DIM = 64


EPSILON = 1e-05
MASKED = -1e30


def dot_plain(matrix_a, matrix_b):
    return jnp.dot(matrix_a, matrix_b, preferred_element_type=jnp.float32)


def dot_right_t(matrix_a, matrix_b):
    return lax.dot_general(
        matrix_a, matrix_b, (((1,), (1,)), ((), ())), preferred_element_type=jnp.float32
    )


def dot_left_t(matrix_a, matrix_b):
    return lax.dot_general(
        matrix_a, matrix_b, (((0,), (0,)), ((), ())), preferred_element_type=jnp.float32
    )


def norm_forward(values, gain_vec):
    inverse = lax.rsqrt(jnp.mean(values * values, axis=-1, keepdims=True) + EPSILON)
    normed = values * inverse
    return ((normed * gain_vec).astype(jnp.bfloat16), normed, inverse)


def norm_backward(gradient, normed, inverse, gain_vec):
    scaled = gradient * gain_vec
    return inverse * (scaled - normed * jnp.mean(scaled * normed, axis=-1, keepdims=True))


def rope_tables(positions, head_dim):
    half_dim = head_dim // 2
    frequency = 10000.0 ** (-2.0 * jnp.arange(half_dim, dtype=jnp.float32) / head_dim)
    angles = positions.astype(jnp.float32)[:, None] * frequency[None, :]
    cos_table = jnp.concatenate([jnp.cos(angles), jnp.cos(angles)], axis=-1)[:, None, :]
    sin_table = jnp.concatenate([jnp.sin(angles), jnp.sin(angles)], axis=-1)[:, None, :]
    return (cos_table, sin_table)


def rope_apply(values, cos_table, sin_table):
    half_dim = values.shape[-1] // 2
    turned = jnp.concatenate([-values[..., half_dim:], values[..., :half_dim]], axis=-1)
    return values * cos_table + turned * sin_table


def rope_reverse(gradient, cos_table, sin_table):
    half_dim = gradient.shape[-1] // 2
    scaled = gradient * sin_table
    return gradient * cos_table + jnp.concatenate(
        [scaled[..., half_dim:], -scaled[..., :half_dim]], axis=-1
    )


def shards(
    tokens,
    positions,
    doc_start,
    cotangent,
    w_query,
    w_key,
    w_value,
    w_out,
    attn_gain,
    w_gate,
    w_up,
    w_down,
    mlp_gain,
):
    row_count = tokens.shape[0]
    seq_index = lax.axis_index("seq")
    key_count = row_count * lax.axis_size("seq")
    block_len = min(512, key_count)
    group_size = HEADS // KV_HEADS
    kv_width = KV_HEADS * HEAD_DIM
    query_width = HEADS * HEAD_DIM
    score_scale = HEAD_DIM ** (-0.5)
    head_shape = (KV_HEADS, group_size, row_count)
    query_rows = seq_index * row_count + jnp.arange(row_count, dtype=jnp.int32)
    block_count = ((seq_index + 1) * row_count + block_len - 1) // block_len
    query_full, key_full, value_full, out_full, attn_full = (
        lax.all_gather(w_query, ("fsdp", "seq"), axis=0, tiled=True),
        lax.all_gather(w_key, ("fsdp", "seq"), axis=0, tiled=True),
        lax.all_gather(w_value, ("fsdp", "seq"), axis=0, tiled=True),
        lax.all_gather(w_out, ("fsdp", "seq"), axis=1, tiled=True),
        lax.all_gather(attn_gain, ("fsdp", "seq"), axis=0, tiled=True),
    )
    inputs_f = tokens.astype(jnp.float32)
    attn_in, attn_normed, attn_inverse = norm_forward(inputs_f, attn_full.astype(jnp.float32))
    cos_table, sin_table = rope_tables(positions, HEAD_DIM)
    query_pre = dot_plain(attn_in, query_full)
    key_pre = dot_plain(attn_in, key_full)
    value_pre = dot_plain(attn_in, value_full)
    query_low = rope_apply(
        query_pre.reshape(row_count, HEADS, HEAD_DIM), cos_table, sin_table
    ).astype(jnp.bfloat16)
    key_low = (
        rope_apply(key_pre.reshape(row_count, KV_HEADS, HEAD_DIM), cos_table, sin_table)
        .astype(jnp.bfloat16)
        .reshape(row_count, kv_width)
    )
    value_low = value_pre.astype(jnp.bfloat16)
    key_all, value_all = (
        lax.all_gather(key_low, "seq", axis=0, tiled=True),
        lax.all_gather(value_low, "seq", axis=0, tiled=True),
    )
    query_heads = query_low.reshape(row_count, KV_HEADS, group_size, HEAD_DIM).transpose(1, 2, 0, 3)

    def key_tile_at(step_idx):
        first_row = step_idx * block_len
        key_tile = lax.dynamic_slice_in_dim(key_all, first_row, block_len, 0).reshape(
            block_len, KV_HEADS, HEAD_DIM
        )
        value_tile = lax.dynamic_slice_in_dim(value_all, first_row, block_len, 0).reshape(
            block_len, KV_HEADS, HEAD_DIM
        )
        scores = (
            jnp.einsum("kgrd,jkd->kgrj", query_heads, key_tile, preferred_element_type=jnp.float32)
            * score_scale
        )
        columns = first_row + jnp.arange(block_len, dtype=jnp.int32)
        allowed = (columns[None, :] >= doc_start[:, None]) & (
            columns[None, :] <= query_rows[:, None]
        )
        scores = jnp.where(allowed[None, None], scores, MASKED)
        return (key_tile, value_tile, scores, allowed)

    def stats_step(step_idx, running):
        highest, exp_total = running
        key_tile, value_tile, scores, allowed = key_tile_at(step_idx)
        new_high = jnp.maximum(highest, jnp.max(scores, axis=-1))
        terms = jnp.where(allowed[None, None], jnp.exp(scores - new_high[..., None]), 0.0)
        exp_total = exp_total * jnp.exp(highest - new_high) + jnp.sum(terms, axis=-1)
        return (new_high, exp_total)

    highest, exp_total = lax.fori_loop(
        0,
        block_count,
        stats_step,
        (jnp.full(head_shape, MASKED, jnp.float32), jnp.zeros(head_shape, jnp.float32)),
    )
    log_total = highest + jnp.log(exp_total)

    def value_step(step_idx, context_sum):
        key_tile, value_tile, scores, allowed = key_tile_at(step_idx)
        weights_low = jnp.exp(scores - log_total[..., None]).astype(jnp.bfloat16)
        return context_sum + jnp.einsum(
            "kgrj,jkd->kgrd", weights_low, value_tile, preferred_element_type=jnp.float32
        )

    context_heads = lax.fori_loop(
        0,
        block_count,
        value_step,
        jnp.zeros((KV_HEADS, group_size, row_count, HEAD_DIM), jnp.float32),
    )
    context_low = (
        context_heads.transpose(2, 0, 1, 3).reshape(row_count, query_width).astype(jnp.bfloat16)
    )
    mid_f = inputs_f + dot_plain(context_low, out_full)
    gate_full, up_full, down_full, mlp_full = (
        lax.all_gather(w_gate, ("fsdp", "seq"), axis=0, tiled=True),
        lax.all_gather(w_up, ("fsdp", "seq"), axis=0, tiled=True),
        lax.all_gather(w_down, ("fsdp", "seq"), axis=0, tiled=True),
        lax.all_gather(mlp_gain, ("fsdp", "seq"), axis=0, tiled=True),
    )
    mlp_in, mlp_normed, mlp_inverse = norm_forward(mid_f, mlp_full.astype(jnp.float32))
    gate_pre = dot_plain(mlp_in, gate_full)
    up_pre = dot_plain(mlp_in, up_full)
    sigmoid_gate = jax.nn.sigmoid(gate_pre)
    hidden_low = (gate_pre * sigmoid_gate * up_pre).astype(jnp.bfloat16)
    output = (mid_f + dot_plain(hidden_low, down_full)).astype(jnp.bfloat16)
    gate_back, up_back, down_back, mlp_back = (
        lax.all_gather(w_gate, ("fsdp", "seq"), axis=0, tiled=True),
        lax.all_gather(w_up, ("fsdp", "seq"), axis=0, tiled=True),
        lax.all_gather(w_down, ("fsdp", "seq"), axis=0, tiled=True),
        lax.all_gather(mlp_gain, ("fsdp", "seq"), axis=0, tiled=True),
    )
    query_back, key_back, value_back, out_back, attn_back = (
        lax.all_gather(w_query, ("fsdp", "seq"), axis=0, tiled=True),
        lax.all_gather(w_key, ("fsdp", "seq"), axis=0, tiled=True),
        lax.all_gather(w_value, ("fsdp", "seq"), axis=0, tiled=True),
        lax.all_gather(w_out, ("fsdp", "seq"), axis=1, tiled=True),
        lax.all_gather(attn_gain, ("fsdp", "seq"), axis=0, tiled=True),
    )
    upstream = cotangent.astype(jnp.float32)
    down_part = dot_left_t(hidden_low, cotangent)
    hidden_grad = dot_right_t(cotangent, down_back)
    gate_grad = (
        hidden_grad * up_pre * sigmoid_gate * (1.0 + gate_pre * (1.0 - sigmoid_gate))
    ).astype(jnp.bfloat16)
    up_grad = (hidden_grad * gate_pre * sigmoid_gate).astype(jnp.bfloat16)
    mlp_in_grad = dot_right_t(gate_grad, gate_back) + dot_right_t(up_grad, up_back)
    gate_part = dot_left_t(mlp_in, gate_grad)
    up_part = dot_left_t(mlp_in, up_grad)
    mlp_gain_part = jnp.sum(mlp_in_grad * mlp_normed, axis=0)
    grad_gate, grad_up, grad_down, grad_mlp_gain = (
        lax.psum_scatter(gate_part, ("fsdp", "seq"), scatter_dimension=0, tiled=True),
        lax.psum_scatter(up_part, ("fsdp", "seq"), scatter_dimension=0, tiled=True),
        lax.psum_scatter(down_part, ("fsdp", "seq"), scatter_dimension=0, tiled=True),
        lax.psum_scatter(mlp_gain_part, ("fsdp", "seq"), scatter_dimension=0, tiled=True),
    )
    mid_grad = upstream + norm_backward(
        mlp_in_grad, mlp_normed, mlp_inverse, mlp_back.astype(jnp.float32)
    )
    mid_low = mid_grad.astype(jnp.bfloat16)
    out_part = dot_left_t(context_low, mid_low)
    context_grad = dot_right_t(mid_low, out_back).astype(jnp.bfloat16)
    dout_heads = context_grad.reshape(row_count, KV_HEADS, group_size, HEAD_DIM).transpose(
        1, 2, 0, 3
    )
    row_delta = jnp.sum(dout_heads.astype(jnp.float32) * context_heads, axis=-1)

    def grad_step(step_idx, running):
        query_grad, key_grads, value_grads = running
        key_tile, value_tile, scores, allowed = key_tile_at(step_idx)
        weights_f = jnp.exp(scores - log_total[..., None])
        weights_low = weights_f.astype(jnp.bfloat16)
        value_part = jnp.einsum(
            "kgrj,kgrd->jkd", weights_low, dout_heads, preferred_element_type=jnp.float32
        )
        weight_grad = jnp.einsum(
            "kgrd,jkd->kgrj", dout_heads, value_tile, preferred_element_type=jnp.float32
        )
        score_grad = (weights_f * (weight_grad - row_delta[..., None])).astype(jnp.bfloat16)
        query_grad = (
            query_grad
            + jnp.einsum("kgrj,jkd->kgrd", score_grad, key_tile, preferred_element_type=jnp.float32)
            * score_scale
        )
        key_part = (
            jnp.einsum(
                "kgrj,kgrd->jkd", score_grad, query_heads, preferred_element_type=jnp.float32
            )
            * score_scale
        )
        first_row = step_idx * block_len
        key_grads = lax.dynamic_update_slice_in_dim(
            key_grads,
            lax.dynamic_slice_in_dim(key_grads, first_row, block_len, 0)
            + key_part.reshape(block_len, kv_width),
            first_row,
            0,
        )
        value_grads = lax.dynamic_update_slice_in_dim(
            value_grads,
            lax.dynamic_slice_in_dim(value_grads, first_row, block_len, 0)
            + value_part.reshape(block_len, kv_width),
            first_row,
            0,
        )
        return (query_grad, key_grads, value_grads)

    query_grad, key_grads, value_grads = lax.fori_loop(
        0,
        block_count,
        grad_step,
        (
            jnp.zeros((KV_HEADS, group_size, row_count, HEAD_DIM), jnp.float32),
            jnp.zeros((key_count, kv_width), jnp.float32),
            jnp.zeros((key_count, kv_width), jnp.float32),
        ),
    )
    key_local, value_local = (
        lax.psum_scatter(
            key_grads.astype(jnp.bfloat16), "seq", scatter_dimension=0, tiled=True
        ).astype(jnp.float32),
        lax.psum_scatter(
            value_grads.astype(jnp.bfloat16), "seq", scatter_dimension=0, tiled=True
        ).astype(jnp.float32),
    )
    query_rot_grad = query_grad.transpose(2, 0, 1, 3).reshape(row_count, HEADS, HEAD_DIM)
    query_pre_grad = (
        rope_reverse(query_rot_grad, cos_table, sin_table)
        .reshape(row_count, query_width)
        .astype(jnp.bfloat16)
    )
    key_pre_grad = (
        rope_reverse(key_local.reshape(row_count, KV_HEADS, HEAD_DIM), cos_table, sin_table)
        .reshape(row_count, kv_width)
        .astype(jnp.bfloat16)
    )
    value_pre_grad = value_local.astype(jnp.bfloat16)
    attn_in_grad = (
        dot_right_t(query_pre_grad, query_back)
        + dot_right_t(key_pre_grad, key_back)
        + dot_right_t(value_pre_grad, value_back)
    )
    query_part = dot_left_t(attn_in, query_pre_grad)
    key_wpart = dot_left_t(attn_in, key_pre_grad)
    value_wpart = dot_left_t(attn_in, value_pre_grad)
    attn_gain_part = jnp.sum(attn_in_grad * attn_normed, axis=0)
    grad_query, grad_key, grad_value, grad_out, grad_attn_gain = (
        lax.psum_scatter(query_part, ("fsdp", "seq"), scatter_dimension=0, tiled=True),
        lax.psum_scatter(key_wpart, ("fsdp", "seq"), scatter_dimension=0, tiled=True),
        lax.psum_scatter(value_wpart, ("fsdp", "seq"), scatter_dimension=0, tiled=True),
        lax.psum_scatter(out_part, ("fsdp", "seq"), scatter_dimension=1, tiled=True),
        lax.psum_scatter(attn_gain_part, ("fsdp", "seq"), scatter_dimension=0, tiled=True),
    )
    input_grad = mid_grad + norm_backward(
        attn_in_grad, attn_normed, attn_inverse, attn_back.astype(jnp.float32)
    )
    return (
        output,
        input_grad,
        grad_query,
        grad_key,
        grad_value,
        grad_out,
        grad_attn_gain,
        grad_gate,
        grad_up,
        grad_down,
        grad_mlp_gain,
    )


def solution(mesh):
    in_specs = (
        P(("fsdp", "seq"), None),
        P(("fsdp", "seq")),
        P(("fsdp", "seq")),
        P(("fsdp", "seq"), None),
        P(("fsdp", "seq"), None),
        P(("fsdp", "seq"), None),
        P(("fsdp", "seq"), None),
        P(None, ("fsdp", "seq")),
        P(("fsdp", "seq")),
        P(("fsdp", "seq"), None),
        P(("fsdp", "seq"), None),
        P(("fsdp", "seq"), None),
        P(("fsdp", "seq")),
    )
    out_specs = (
        P(("fsdp", "seq"), None),
        P(("fsdp", "seq"), None),
        P(("fsdp", "seq"), None),
        P(("fsdp", "seq"), None),
        P(("fsdp", "seq"), None),
        P(None, ("fsdp", "seq")),
        P(("fsdp", "seq")),
        P(("fsdp", "seq"), None),
        P(("fsdp", "seq"), None),
        P(("fsdp", "seq"), None),
        P(("fsdp", "seq")),
    )
    return jax.shard_map(shards, mesh=mesh, in_specs=in_specs, out_specs=out_specs, check_vma=False)
```

profile of v0, /device:TPU:31, one launch (start us, length us, event | category | flops | bytes accessed | tf_op | source)
XLA Modules:
  0.0 4833.5 jit_solution(17736795928979614994)
XLA Ops:
  13.7 38.4 all-reduce.5
  53.0 1.2 fusion.42
  54.3 10.0 all-gather.8.cloned.1.call-done
  64.3 1.7 fusion.61
  66.3 25.5 all_gather.44
  92.1 28.1 all-gather.12.cloned.1.call-done
  120.1 1.6 convolution_convert_fusion.1
  121.7 26.0 all_gather.47
  148.0 52.5 %all-gather.10.cloned.1.call-done = bf16[2048,2048]{1,0:T(8,128)(2,1)} async-done(((bf16[64,2048]{1,0:T(8,128)(2,1)}), bf16[2048,2048]{1,0:T(8,128)(2,1)}) %all-gather.10.cloned.1.call-update) | async-done | bytes 8388624 | tf_op jit(solution)/shard_map/all_gather | solution.py:92
  200.5 6.8 fusion.59
  207.7 7.5 while.39
  207.9 1.3 fusion.146
  209.2 2.2 select_reduce_fusion.2
  211.6 1.3 fusion.146
  213.0 2.2 select_reduce_fusion.2
  215.3 9.5 while.40
  216.7 3.6 fusion.151
  221.2 3.6 fusion.151
  225.8 53.5 %all-gather.14.cloned.1.call-done = bf16[2048,2048]{0,1:T(8,128)(2,1)} async-done(((bf16[2048,64]{0,1:T(8,128)(2,1)}), bf16[2048,2048]{0,1:T(8,128)(2,1)}) %all-gather.14.cloned.1.call-update) | async-done | bytes 8388624 | tf_op jit(solution)/shard_map/all_gather | solution.py:95
  279.3 6.5 multiply_reduce_fusion.3
  287.0 137.8 %all-gather.16.cloned.1.call-done = bf16[2048,5632]{1,0:T(8,128)(2,1)} async-done(((bf16[64,5632]{1,0:T(8,128)(2,1)}), bf16[2048,5632]{1,0:T(8,128)(2,1)}) %all-gather.16.cloned.1.call-update) | async-done | bytes 23068688 | tf_op jit(solution)/shard_map/all_gather | solution.py:172
  424.8 12.5 fusion.66
  437.3 133.1 %all-gather.18.cloned.1.call-done = bf16[2048,5632]{1,0:T(8,128)(2,1)} async-done(((bf16[64,5632]{1,0:T(8,128)(2,1)}), bf16[2048,5632]{1,0:T(8,128)(2,1)}) %all-gather.18.cloned.1.call-update) | async-done | bytes 23068688 | tf_op jit(solution)/shard_map/all_gather | solution.py:173
  570.4 12.5 fusion.67
  582.9 133.3 %all-gather.20.cloned.1.call-done = bf16[5632,2048]{1,0:T(8,128)(2,1)} async-done(((bf16[176,2048]{1,0:T(8,128)(2,1)}), bf16[5632,2048]{1,0:T(8,128)(2,1)}) %all-gather.20.cloned.1.call-update) | async-done | bytes 23068688 | tf_op jit(solution)/shard_map/all_gather | solution.py:174
  716.1 15.6 multiply_convert_fusion
  731.7 13.0 fusion.68
  744.8 14.0 multiply_reduce_fusion
  758.8 1.7 multiply_add_fusion.1
  761.4 5.6 convolution_convert_fusion
  767.0 2.0 copy.66
  769.0 1.2 multiply_reduce_fusion.1
  771.5 1.1 broadcast.224.clone
  772.6 20.9 while.41
  772.6 1.3 fusion.162
  774.2 2.8 fusion.163
  777.9 1.9 fusion.165
  779.8 1.4 fusion.166
  782.9 1.3 fusion.162
  784.4 2.8 fusion.163
  788.2 1.9 fusion.165
  790.1 1.4 fusion.166
  793.5 1.3 convert_element_type.111
  795.9 1.3 convert_element_type.114
  798.3 56.7 %reduce-scatter.28.cloned.1.call-done = bf16[128,256]{1,0:T(8,128)(2,1)} async-done(((bf16[1024,256]{1,0:T(8,128)(2,1)}), bf16[128,256]{1,0:T(8,128)(2,1)}) %reduce-scatter.28.cloned.1.call-update) | async-done | bytes 65552
  856.1 1.9 fusion.54
  858.1 61.6 %reduce-scatter.30.cloned.1.call-done = bf16[128,256]{1,0:T(8,128)(2,1)} async-done(((bf16[1024,256]{1,0:T(8,128)(2,1)}), bf16[128,256]{1,0:T(8,128)(2,1)}) %reduce-scatter.30.cloned.1.call-update) | async-done | bytes 65552
  919.7 2.7 fusion.52
  923.0 8.3 fusion.56
  931.3 1.2 copy-done.4
  932.6 8.2 fusion.48
  941.8 19.2 fusion.70
  961.3 19.2 fusion.71
  981.6 19.2 fusion.72
  1000.9 6.5 fusion.69
  1007.4 11.8 fusion.31
  1020.4 41.4 all-reduce.4
  1062.9 1.3 fusion.40
  1064.3 132.2 %reduce-scatter.18.cloned.1.call-done = f32[64,256]{1,0:T(8,128)} async-done(((f32[2048,256]{1,0:T(8,128)}), f32[64,256]{1,0:T(8,128)}) %reduce-scatter.18.cloned.1.call-update) | async-done | bytes 65552 | tf_op jit(solution)/shard_map/reduce_scatter | solution.py:306
  1196.5 359.8 %reduce-scatter.14.cloned.1.call-done = f32[64,2048]{1,0:T(8,128)} async-done(((f32[2048,2048]{1,0:T(8,128)}), f32[64,2048]{1,0:T(8,128)}) %reduce-scatter.14.cloned.1.call-update) | async-done | bytes 524304 | tf_op jit(solution)/shard_map/reduce_scatter | solution.py:304
  1556.2 360.2 %reduce-scatter.20.cloned.1.call-done = f32[2048,64]{0,1:T(8,128)} async-done(((f32[2048,2048]{0,1:T(8,128)}), f32[2048,64]{0,1:T(8,128)}) %reduce-scatter.20.cloned.1.call-update) | async-done | bytes 524304 | tf_op jit(solution)/shard_map/reduce_scatter | solution.py:307
  1916.5 970.1 %reduce-scatter.22.cloned.1.call-done = f32[64,5632]{1,0:T(8,128)} async-done(((f32[2048,5632]{1,0:T(8,128)}), f32[64,5632]{1,0:T(8,128)}) %reduce-scatter.22.cloned.1.call-update) | async-done | bytes 1441808 | tf_op jit(solution)/shard_map/reduce_scatter | solution.py:208
  2886.6 970.1 %reduce-scatter.24.cloned.1.call-done = f32[64,5632]{1,0:T(8,128)} async-done(((f32[2048,5632]{1,0:T(8,128)}), f32[64,5632]{1,0:T(8,128)}) %reduce-scatter.24.cloned.1.call-update) | async-done | bytes 1441808 | tf_op jit(solution)/shard_map/reduce_scatter | solution.py:209
  3856.7 970.1 %reduce-scatter.26.cloned.1.call-done = f32[176,2048]{1,0:T(8,128)} async-done(((f32[5632,2048]{1,0:T(8,128)}), f32[176,2048]{1,0:T(8,128)}) %reduce-scatter.26.cloned.1.call-update) | async-done | bytes 1441808 | tf_op jit(solution)/shard_map/reduce_scatter | solution.py:210
  (187 shorter events, 28.8 us)
Async XLA Ops:
  7.2 113.0 %copy-start = (bf16[128,2048]{1,0:T(8,128)(2,1)S(1)}, bf16[128,2048]{1,0:T(8,128)(2,1)}, u32[]{:S(2)}) copy-start(bf16[128,2048]{1,0:T(8,128)(2,1)} %param.19) | copy-start | bytes 1572868
  7.2 57.1 %all-gather.8.cloned.1.call-start = ((), (), s32[]{:S(2)}) async-start(), calls=%async_computation.9 | async-start | bytes 1081344 | tf_op jit(solution)/shard_map/all_gather | solution.py:93
  7.9 112.2 %all-gather.12.cloned.1.call-start = ((), (), s32[]{:S(2)}) async-start(), calls=%async_computation.11 | async-start | bytes 1081344 | tf_op jit(solution)/shard_map/all_gather | solution.py:94
  8.7 191.8 %all-gather.10.cloned.1.call-start = ((), (), s32[]{:S(2)}) async-start(), calls=%async_computation.10 | async-start | bytes 8650752 | tf_op jit(solution)/shard_map/all_gather | solution.py:92
  9.4 269.9 %all-gather.14.cloned.1.call-start = ((), (), s32[]{:S(2)}) async-start(), calls=%async_computation.12 | async-start | bytes 8650752 | tf_op jit(solution)/shard_map/all_gather | solution.py:95
  10.0 414.8 %all-gather.16.cloned.1.call-start = ((), (), s32[]{:S(2)}) async-start(), calls=%async_computation.13 | async-start | bytes 23789568 | tf_op jit(solution)/shard_map/all_gather | solution.py:172
  10.6 559.8 %all-gather.18.cloned.1.call-start = ((), (), s32[]{:S(2)}) async-start(), calls=%async_computation.14 | async-start | bytes 23789568 | tf_op jit(solution)/shard_map/all_gather | solution.py:173
  11.1 705.0 %all-gather.20.cloned.1.call-start = ((), (), s32[]{:S(2)}) async-start(), calls=%async_computation.15 | async-start | bytes 23789568 | tf_op jit(solution)/shard_map/all_gather | solution.py:174
  11.9 843.1 %reduce-scatter.28.cloned.1.call-start = ((), (), s32[]{:S(2)}) async-start(), calls=%async_computation.23 | async-start | bytes 589824
  52.0 155.2 %copy-start.23 = (f32[2048]{0:T(1024)}, f32[2048]{0:T(1024)S(1)}, u32[]{:S(2)}) copy-start(f32[2048]{0:T(1024)S(1)} %convert_element_type.91) | copy-start | bytes 24580
  52.9 154.5 %copy-start.21 = (f32[128,64]{0,1:T(8,128)}, f32[128,64]{0,1:T(8,128)S(1)}, u32[]{:S(2)}) copy-start(f32[128,64]{0,1:T(8,128)S(1)} %pad_maximum_fusion.2) | copy-start | bytes 98308
  53.0 154.3 %copy-start.19 = (f32[128,64]{0,1:T(8,128)}, f32[128,64]{0,1:T(8,128)S(1)}, u32[]{:S(2)}) copy-start(f32[128,64]{0,1:T(8,128)S(1)} %pad_maximum_fusion.3) | copy-start | bytes 98308
  54.3 153.0 %copy-start.28 = (f32[128]{0:T(128)}, f32[128]{0:T(128)S(1)}, u32[]{:S(2)}) copy-start(f32[128]{0:T(128)S(1)} %add_rsqrt_fusion.1) | copy-start | bytes 1540
  121.7 85.9 %copy-start.26 = (s32[128]{0:T(128)S(1)}, s32[128]{0:T(128)}, u32[]{:S(2)}) copy-start(s32[128]{0:T(128)} %param.21) | copy-start | bytes 1540
  224.8 54.5 %copy-start.11 = (f32[4,8,128,64]{2,3,1,0:T(8,128)}, f32[4,8,128,64]{2,3,1,0:T(8,128)S(1)}, u32[]{:S(2)}) copy-start(f32[4,8,128,64]{2,3,1,0:T(8,128)S(1)} %get-tuple-element.175) | copy-start | bytes 3145732
  285.8 472.9 %copy-start.1 = (f32[128,2048]{1,0:T(8,128)}, f32[128,2048]{1,0:T(8,128)S(1)}, u32[]{:S(2)}) copy-start(f32[128,2048]{1,0:T(8,128)S(1)} %get-tuple-element.429) | copy-start | bytes 3145732
  731.7 13.0 copy-start.10
  760.5 1.0 copy-start.3
  761.4 7.6 copy-start.12
  772.6 83.4 %copy-start.20 = (f32[128,64]{0,1:T(8,128)S(1)}, f32[128,64]{0,1:T(8,128)}, u32[]{:S(2)}) copy-start(f32[128,64]{0,1:T(8,128)} %copy-done.19) | copy-start | bytes 98308
  772.6 83.5 %copy-start.22 = (f32[128,64]{0,1:T(8,128)S(1)}, f32[128,64]{0,1:T(8,128)}, u32[]{:S(2)}) copy-start(f32[128,64]{0,1:T(8,128)} %copy-done.21) | copy-start | bytes 98308
  772.6 83.5 %copy-start.24 = (f32[2048]{0:T(1024)S(1)}, f32[2048]{0:T(1024)}, u32[]{:S(2)}) copy-start(f32[2048]{0:T(1024)} %copy-done.23) | copy-start | bytes 24580
  772.6 83.5 %copy-start.29 = (f32[128]{0:T(128)S(1)}, f32[128]{0:T(128)}, u32[]{:S(2)}) copy-start(f32[128]{0:T(128)} %copy-done.28) | copy-start | bytes 1540
  772.6 1.5 copy-start.16
  777.9 3.4 copy-start.5
  777.9 3.4 copy-start.7
  781.5 1.0 copy-start.6
  781.5 1.3 copy-start.8
  782.9 1.5 copy-start.16
  788.1 3.4 copy-start.5
  788.2 3.4 copy-start.7
  791.8 1.0 copy-start.6
  791.8 1.3 copy-start.8
  795.9 123.8 %reduce-scatter.30.cloned.1.call-start = ((), (), s32[]{:S(2)}) async-start(), calls=%async_computation.24 | async-start | bytes 589824
  798.2 266.1 %reduce-scatter.16.cloned.1.call-start = ((), (), s32[]{:S(2)}) async-start(), calls=%async_computation.17 | async-start | bytes 2162688 | tf_op jit(solution)/shard_map/reduce_scatter | solution.py:305
  858.0 338.5 %reduce-scatter.18.cloned.1.call-start = ((), (), s32[]{:S(2)}) async-start(), calls=%async_computation.18 | async-start | bytes 2162688 | tf_op jit(solution)/shard_map/reduce_scatter | solution.py:306
  922.4 633.8 %reduce-scatter.14.cloned.1.call-start = ((), (), s32[]{:S(2)}) async-start(), calls=%async_computation.16 | async-start | bytes 17301504 | tf_op jit(solution)/shard_map/reduce_scatter | solution.py:304
  931.2 1.2 copy-start.4
  931.2 1.4 copy-start.14
  931.2 985.2 %reduce-scatter.20.cloned.1.call-start = ((), (), s32[]{:S(2)}) async-start(), calls=%async_computation.19 | async-start | bytes 17301504 | tf_op jit(solution)/shard_map/reduce_scatter | solution.py:307
  940.8 1.0 copy-start.9
  940.8 1945.8 %reduce-scatter.22.cloned.1.call-start = ((), (), s32[]{:S(2)}) async-start(), calls=%async_computation.20 | async-start | bytes 47579136 | tf_op jit(solution)/shard_map/reduce_scatter | solution.py:208
  961.1 2895.6 %reduce-scatter.24.cloned.1.call-start = ((), (), s32[]{:S(2)}) async-start(), calls=%async_computation.21 | async-start | bytes 47579136 | tf_op jit(solution)/shard_map/reduce_scatter | solution.py:209
  980.5 1.0 copy-start.15
  980.5 3846.2 %reduce-scatter.26.cloned.1.call-start = ((), (), s32[]{:S(2)}) async-start(), calls=%async_computation.22 | async-start | bytes 47579136 | tf_op jit(solution)/shard_map/reduce_scatter | solution.py:210
  1000.8 6.5 copy-start.2
  1000.8 6.5 copy-start.13
  1007.3 11.9 copy-start.17
  1007.3 12.3 copy-start.18
  1007.4 12.3 copy-start.25
  1007.4 13.0 copy-start.27
Sparse Core Ops, SparseCore 0:
  11.1 53.1 all-gather.7
  67.4 52.7 all-gather.11
  123.1 77.2 all-gather.9
  203.3 75.9 all-gather.13
  282.1 142.6 all-gather.15
  427.6 142.7 all-gather.17
  573.3 142.7 all-gather.19
  796.0 58.9 reduce-scatter.27
  858.7 60.9 reduce-scatter.29
  922.4 136.6 reduce-scatter.15
  1062.1 134.3 reduce-scatter.17
  1199.2 357.0 reduce-scatter.13
  1559.1 357.3 reduce-scatter.19
  1919.2 967.3 reduce-scatter.21
  2889.3 967.3 reduce-scatter.23
  3859.4 967.3 reduce-scatter.25
where the time goes:
time: 4840 us; the launch traced here: 4830 us
  waiting for transfers between devices  4430 us (92%)
  matrix products  214 us (4%)
  blocking collectives  131 us (3%)
    reduce_scatter x1, waiting for transfers between devices, shards(): lax.psum_scatter(gate_part, ('fsdp', 'seq'), scatter_dimension=0, tiled=T...  970 us
    reduce_scatter x1, waiting for transfers between devices, shards(): lax.psum_scatter(down_part, ('fsdp', 'seq'), scatter_dimension=0, tiled=T...  970 us
    reduce_scatter x1, waiting for transfers between devices, shards(): lax.psum_scatter(up_part, ('fsdp', 'seq'), scatter_dimension=0, tiled=True)  970 us
    reduce_scatter x1, waiting for transfers between devices, shards(): lax.psum_scatter(out_part, ('fsdp', 'seq'), scatter_dimension=1, tiled=True)  360 us
    reduce_scatter x1, waiting for transfers between devices, shards(): lax.psum_scatter(query_part, ('fsdp', 'seq'), scatter_dimension=0, tiled=...  360 us
    all_gather x1, waiting for transfers between devices, shards(): lax.all_gather(w_gate, ('fsdp', 'seq'), axis=0, tiled=True)  138 us
    all_gather x1, waiting for transfers between devices, shards(): lax.all_gather(w_down, ('fsdp', 'seq'), axis=0, tiled=True)  133 us
    all_gather x1, waiting for transfers between devices, shards(): lax.all_gather(w_up, ('fsdp', 'seq'), axis=0, tiled=True)  133 us
  transfers between devices with their start and end apart: 16, of which 15 were waited for; matrix products, arithmetic and copies ran while one was open for 4% of the time, Pallas kernels for 0%

commit v1 on v0

v1 whole, which is shorter than its diff:
```python
import jax
import jax.numpy as jnp
from jax import lax
from jax.sharding import Mesh
from jax.sharding import PartitionSpec as P

HEADS = 32
KV_HEADS = 4
HEAD_DIM = 64
EPSILON = 1e-05
MASKED = -1e30
ALL = ("x", "core", "z", "y")
TEAM = ("z", "core")
DATA = ("x", "y")
BF = jnp.bfloat16
F32 = jnp.float32


def dot_plain(a, b):
    return jnp.dot(a, b, preferred_element_type=F32)


def dot_right_t(a, b):
    return lax.dot_general(a, b, (((1,), (1,)), ((), ())), preferred_element_type=F32)


def dot_left_t(a, b):
    return lax.dot_general(a, b, (((0,), (0,)), ((), ())), preferred_element_type=F32)


def team_gather(rows):
    return lax.all_gather(rows, TEAM, axis=0, tiled=True)


def team_sum_scatter(partial):
    team = lax.axis_size(TEAM)
    blocks = partial.reshape(team, partial.shape[0] // team, partial.shape[1])
    arrived = lax.all_to_all(blocks, TEAM, 0, 0, tiled=False)
    return jnp.sum(arrived.astype(F32), axis=0)


def team_exchange(blocks):
    return lax.all_to_all(blocks, TEAM, 0, 0, tiled=False)


def weights_gather(blocks):
    z, c = lax.axis_size("z"), lax.axis_size("core")
    rows, cols = blocks.shape[1:]
    got = lax.all_gather(blocks, DATA, axis=0)
    x, y = lax.axis_size("x"), lax.axis_size("y")
    got = got.reshape(x, y, z, c, rows, cols).transpose(0, 3, 2, 1, 4, 5)
    return got.reshape(x * c * z * y * rows, cols)


def grads_scatter(partial):
    x, y, z, c = (lax.axis_size(a) for a in ("x", "y", "z", "core"))
    cols = partial.shape[1]
    rows = partial.shape[0] // (x * y * z * c)
    parts = partial.astype(BF).reshape(x, c, z, y, rows, cols).transpose(0, 3, 2, 1, 4, 5)
    parts = parts.reshape(x * y, z * c * rows, cols)
    arrived = lax.all_to_all(parts, DATA, 0, 0, tiled=False)
    return jnp.sum(arrived.astype(F32), axis=0).reshape(z * c, rows, cols)


def turn(values):
    half = values.shape[-1] // 2
    return jnp.concatenate([-values[..., half:], values[..., :half]], axis=-1)


def rope_apply(values, cos_table, sin_table):
    return values * cos_table + turn(values) * sin_table


def rope_reverse(gradient, cos_table, sin_table):
    half = gradient.shape[-1] // 2
    scaled = gradient * sin_table
    return gradient * cos_table + jnp.concatenate(
        [scaled[..., half:], -scaled[..., :half]], axis=-1
    )


def shards(
    tokens, positions, doc_start, cotangent, w_query, w_key, w_value, w_out,
    attn_gain, w_gate, w_up, w_down, mlp_gain,
):
    nx, nc, nz, ny = (lax.axis_size(a) for a in ALL)
    team = nz * nc
    rows, width = tokens.shape
    own = w_query.shape[0]
    heads = HEADS // team
    qcols = heads * HEAD_DIM
    kv_rep = team // KV_HEADS
    ff = w_gate.shape[1]
    piece = w_down.shape[0]
    ffcols = piece * nx * ny
    y_at = lax.axis_index("y")
    core_at = lax.axis_index("core")
    scale = HEAD_DIM ** (-0.5)

    gain_a = attn_gain.astype(F32)[:, None]
    gain_m = mlp_gain.astype(F32)[:, None]

    def by_heads(w):
        return w.reshape(own, team, -1).transpose(1, 0, 2)

    def by_kv(w):
        return jnp.repeat(w.reshape(own, KV_HEADS, HEAD_DIM).transpose(1, 0, 2), kv_rep, axis=0)

    def scaled(w, gain):
        return (w.astype(F32) * gain).astype(BF)

    def by_ff(w):
        w = w.reshape(own, nx, nc, nz, ny, piece).transpose(3, 2, 0, 1, 4, 5)
        return w.reshape(team, own, ffcols)

    attn_blocks = jnp.concatenate(
        [
            by_heads(scaled(w_query, gain_a)),
            by_kv(scaled(w_key, gain_a)),
            by_kv(scaled(w_value, gain_a)),
            by_heads(w_out.T),
        ],
        axis=-1,
    )
    mlp_blocks = jnp.concatenate([by_ff(scaled(w_gate, gain_m)), by_ff(scaled(w_up, gain_m))], axis=-1)
    w_attn = weights_gather(team_exchange(attn_blocks))
    w_qkv = w_attn[:, : qcols + 2 * HEAD_DIM]
    w_out_t = w_attn[:, qcols + 2 * HEAD_DIM :]

    xf = tokens.astype(F32)
    inv1 = lax.rsqrt(jnp.mean(xf * xf, axis=-1, keepdims=True) + EPSILON)
    n1 = xf * inv1
    half = HEAD_DIM // 2
    frequency = 10000.0 ** (-2.0 * jnp.arange(half, dtype=F32) / HEAD_DIM)
    angles = positions.astype(F32)[:, None] * frequency[None, :]
    table = jnp.concatenate(
        [
            jnp.cos(angles),
            jnp.sin(angles),
            jnp.broadcast_to(doc_start.astype(F32)[:, None], (rows, HEAD_DIM)),
        ],
        axis=-1,
    )
    n1g = team_gather(n1.astype(BF))
    tab = team_gather(table)
    cos_t = jnp.concatenate([tab[:, :half], tab[:, :half]], axis=-1)
    sin_t = jnp.concatenate([tab[:, half : 2 * half], tab[:, half : 2 * half]], axis=-1)
    starts = tab[:, 2 * half].astype(jnp.int32).reshape(nz, nc, rows)

    qkv = dot_plain(n1g, w_qkv)
    total = team * rows
    q = rope_apply(
        qkv[:, :qcols].reshape(total, heads, HEAD_DIM), cos_t[:, None], sin_t[:, None]
    ).astype(BF)
    k = rope_apply(qkv[:, qcols : qcols + HEAD_DIM], cos_t, sin_t).astype(BF)
    v = qkv[:, qcols + HEAD_DIM :].astype(BF)

    kv_own = jnp.concatenate([k, v], axis=-1).reshape(nz, nc, rows, 2 * HEAD_DIM)
    kv_all = lax.all_gather(kv_own, "y", axis=0).transpose(2, 1, 0, 3, 4)
    kv_all = kv_all.reshape(nc, nz * ny * rows, 2 * HEAD_DIM)
    k_all, v_all = kv_all[..., :HEAD_DIM], kv_all[..., HEAD_DIM:]
    qh = q.reshape(nz, nc, rows, heads, HEAD_DIM).transpose(0, 1, 3, 2, 4)

    def block_scores(z):
        keys = (z + 1) * ny * rows
        s = jnp.einsum("chrd,ckd->chrk", qh[z], k_all[:, :keys], preferred_element_type=F32) * scale
        row_at = (z * ny + y_at) * rows + jnp.arange(rows, dtype=jnp.int32)
        cols = jnp.arange(keys, dtype=jnp.int32)
        allowed = (cols[None, None, :] >= starts[z][:, :, None]) & (
            cols[None, None, :] <= row_at[None, :, None]
        )
        s = jnp.where(allowed[:, None], s, MASKED)
        top = jnp.max(s, axis=-1, keepdims=True)
        e = jnp.exp(s - top)
        return e / jnp.sum(e, axis=-1, keepdims=True), keys

    contexts = []
    for z in range(nz):
        p, keys = block_scores(z)
        contexts.append(
            jnp.einsum("chrk,ckd->chrd", p.astype(BF), v_all[:, :keys], preferred_element_type=F32)
        )
    context = jnp.stack(contexts)
    ob = context.transpose(0, 1, 3, 2, 4).reshape(total, qcols).astype(BF)

    mid_f = xf + team_sum_scatter(dot_right_t(ob, w_out_t).astype(BF))
    inv2 = lax.rsqrt(jnp.mean(mid_f * mid_f, axis=-1, keepdims=True) + EPSILON)
    n2 = mid_f * inv2
    n2g = team_gather(n2.astype(BF))

    w_mlp = weights_gather(team_exchange(mlp_blocks))
    w_dn = lax.all_gather(w_down, DATA, axis=0, tiled=True)
    gt = dot_plain(n2g, w_mlp[:, :ffcols])
    up = dot_plain(n2g, w_mlp[:, ffcols:])
    sg = jax.nn.sigmoid(gt)
    hid = (gt * sg * up).astype(BF)
    output = (mid_f + team_sum_scatter(dot_plain(hid, w_dn).astype(BF))).astype(BF)

    cotg = team_gather(cotangent)
    dhid = dot_right_t(cotg, w_dn)
    down_part = dot_left_t(hid, cotg).astype(BF)
    dgt = (dhid * up * sg * (1.0 + gt * (1.0 - sg))).astype(BF)
    dup = (dhid * gt * sg).astype(BF)
    dmlp = jnp.concatenate([dgt, dup], axis=-1)
    dn2 = team_sum_scatter(dot_right_t(dmlp, w_mlp).astype(BF))
    mlp_part = dot_left_t(n2g, dmlp).astype(BF)
    gain_m_part = jnp.sum(dn2 * n2, axis=0)
    dx2 = cotangent.astype(F32) + inv2 * (dn2 - n2 * jnp.mean(dn2 * n2, axis=-1, keepdims=True))
    dag = team_gather(dx2.astype(BF))
    out_part = dot_left_t(dag, ob)
    dob = dot_plain(dag, w_out_t).astype(BF)

    doh = dob.reshape(nz, nc, rows, heads, HEAD_DIM).transpose(0, 1, 3, 2, 4)
    delta = jnp.sum(doh.astype(F32) * context, axis=-1)
    dqs = []
    dk = jnp.zeros((nc, nz * ny * rows, HEAD_DIM), F32)
    dv = jnp.zeros((nc, nz * ny * rows, HEAD_DIM), F32)
    for z in range(nz):
        p, keys = block_scores(z)
        dv = dv.at[:, :keys].add(
            jnp.einsum("chrk,chrd->ckd", p.astype(BF), doh[z], preferred_element_type=F32)
        )
        dp = jnp.einsum("chrd,ckd->chrk", doh[z], v_all[:, :keys], preferred_element_type=F32)
        ds = (p * (dp - delta[z][..., None])).astype(BF)
        dqs.append(
            jnp.einsum("chrk,ckd->chrd", ds, k_all[:, :keys], preferred_element_type=F32) * scale
        )
        dk = dk.at[:, :keys].add(
            jnp.einsum("chrk,chrd->ckd", ds, qh[z], preferred_element_type=F32) * scale
        )
    dq = jnp.stack(dqs).transpose(0, 1, 3, 2, 4).reshape(total, heads, HEAD_DIM)
    dkv = jnp.concatenate([dk, dv], axis=-1).astype(BF)
    dkv = dkv.reshape(nc, nz, ny, rows, 2 * HEAD_DIM).transpose(2, 1, 0, 3, 4)
    dkv = lax.all_to_all(dkv, "y", 0, 0, tiled=False).astype(F32).sum(0)
    dkv = dkv.reshape(total, 2 * HEAD_DIM)
    dkv = lax.psum(dkv, "core")
    dka = rope_reverse(dkv[:, :HEAD_DIM], cos_t, sin_t)
    dva = dkv[:, HEAD_DIM:]
    dka = jnp.where(core_at == 0, dka, 0.0)
    dva = jnp.where(core_at == 1, dva, 0.0)
    dqa = rope_reverse(dq, cos_t[:, None], sin_t[:, None]).reshape(total, qcols)
    dqkv = jnp.concatenate([dqa, dka, dva], axis=-1).astype(BF)
    dn1 = team_sum_scatter(dot_right_t(dqkv, w_qkv).astype(BF))
    qkv_part = dot_left_t(n1g, dqkv)
    gain_a_part = jnp.sum(dn1 * n1, axis=0)
    input_grad = dx2 + inv1 * (dn1 - n1 * jnp.mean(dn1 * n1, axis=-1, keepdims=True))

    attn_part = jnp.concatenate([qkv_part, out_part], axis=-1)
    attn_g = team_exchange(grads_scatter(attn_part).astype(BF)).astype(F32)
    mlp_g = team_exchange(grads_scatter(mlp_part).astype(BF)).astype(F32)
    down_blocks = down_part.reshape(nx * ny, piece, width)
    grad_down = jnp.sum(lax.all_to_all(down_blocks, DATA, 0, 0, tiled=False).astype(F32), axis=0)
    grad_query = attn_g[:, :, :qcols].transpose(1, 0, 2).reshape(own, HEADS * HEAD_DIM) * gain_a
    kv_g = attn_g[:, :, qcols : qcols + 2 * HEAD_DIM].reshape(KV_HEADS, kv_rep, own, 2 * HEAD_DIM).sum(1)
    grad_key = kv_g[..., :HEAD_DIM].transpose(1, 0, 2).reshape(own, KV_HEADS * HEAD_DIM) * gain_a
    grad_value = kv_g[..., HEAD_DIM:].transpose(1, 0, 2).reshape(own, KV_HEADS * HEAD_DIM) * gain_a
    grad_out = attn_g[:, :, qcols + 2 * HEAD_DIM :].transpose(1, 0, 2).reshape(own, HEADS * HEAD_DIM).T

    def from_ff(g):
        g = g.reshape(nz, nc, own, nx, ny, piece).transpose(2, 3, 1, 0, 4, 5)
        return g.reshape(own, ff) * gain_m

    grad_gate = from_ff(mlp_g[:, :, :ffcols])
    grad_up = from_ff(mlp_g[:, :, ffcols:])
    gains = jnp.stack([gain_a_part, gain_m_part], 0).reshape(2, nx * team * ny, own).transpose(1, 0, 2)
    gains = lax.all_to_all(gains, ALL, 0, 0, tiled=False).sum(0)
    grad_attn_gain = gains[0] / gain_a[:, 0]
    grad_mlp_gain = gains[1] / gain_m[:, 0]
    return (
        output, input_grad, grad_query, grad_key, grad_value, grad_out,
        grad_attn_gain, grad_gate, grad_up, grad_down, grad_mlp_gain,
    )


def solution(mesh):
    fsdp, seq = mesh.shape["fsdp"], mesh.shape["seq"]
    nc, nz = 2, 4
    grid = Mesh(mesh.devices.reshape(fsdp // nc, nc, nz, seq // nz), ALL)
    row, col, vec = P(ALL, None), P(None, ALL), P(ALL)
    in_specs = (row, vec, vec, row, row, row, row, col, vec, row, row, row, vec)
    out_specs = (row, row, row, row, row, col, vec, row, row, row, vec)
    return jax.shard_map(shards, mesh=grid, in_specs=in_specs, out_specs=out_specs, check_vma=False)
```

time: 4840 us -> 990 us (0.20)
  waiting for transfers between devices: 4430 us -> 435 us
  matrix products: 214 us -> 111 us
  local copies, waits for them, and re-layouts: 19.5 us -> 95.4 us
  starting transfers between devices: 0.81 us -> 65 us
  blocking collectives: 131 us -> 186 us
  other arithmetic: 17.6 us -> 66.6 us
    reduce_scatter x7 -> x0, waiting for transfers between devices: 3760 us -> none  [the longest x1 970 us: shards(): lax.psum_scatter(gate_part, ('fsdp', 'seq'), scatter_dimension=0, tiled=T...]
    all_gather x7, waiting for transfers between devices: 548 us -> 63.1 us  [the longest x4 53.2 us: team_gather(): return lax.all_gather(rows, TEAM, axis=0, tiled=True)]
    all_to_all x0 -> x11, waiting for transfers between devices: none -> 355 us  [the longest x3 262 us: team_sum_scatter(): arrived = lax.all_to_all(blocks, TEAM, 0, 0, tiled=False)]
    unnamed x18 -> x8, waiting for transfers between devices: 123 us -> 1.88 us
    all_to_all x0 -> x2, blocking collectives: none -> 118 us  [the longest x1 96.7 us: team_sum_scatter(): arrived = lax.all_to_all(blocks, TEAM, 0, 0, tiled=False)]
    dot_general x35 -> x33, matrix products: 214 us -> 98.9 us  [the longest x5 30.5 us: dot_plain(): return jnp.dot(a, b, preferred_element_type=F32)]
    unnamed x2 -> x0, blocking collectives: 79.8 us -> none
    all_to_all x0 -> x11, starting transfers between devices: none -> 64.5 us  [the longest x3 19.9 us: team_exchange(): return lax.all_to_all(blocks, TEAM, 0, 0, tiled=False)]
  transfers between devices with their start and end apart: 16 -> 19, of which waited for: 15 -> 11; matrix products, arithmetic and copies ran while one was open for 4% -> 23% of each run, Pallas kernels for 0% -> 0%
where the time goes in v1:
time: 990 us; the launch traced here: 975 us
  waiting for transfers between devices  435 us (44%)
  blocking collectives  186 us (19%)
  matrix products  111 us (11%)
  local copies, waits for them, and re-layouts  95.4 us (10%)
  other arithmetic  66.6 us (7%)
  starting transfers between devices  65 us (7%)
  between operations  16.2 us (2%)
    all_to_all x3, waiting for transfers between devices, team_sum_scatter(): arrived = lax.all_to_all(blocks, TEAM, 0, 0, tiled=False)  262 us
    all_to_all x1, blocking collectives, team_sum_scatter(): arrived = lax.all_to_all(blocks, TEAM, 0, 0, tiled=False)  96.7 us
    all_to_all x2, waiting for transfers between devices, grads_scatter(): arrived = lax.all_to_all(parts, DATA, 0, 0, tiled=False)  77.7 us
    all_gather x1, blocking collectives, team_gather(): return lax.all_gather(rows, TEAM, axis=0, tiled=True)  54.7 us
    all_gather x4, waiting for transfers between devices, team_gather(): return lax.all_gather(rows, TEAM, axis=0, tiled=True)  53.2 us
    dot_general x5, matrix products, dot_plain(): return jnp.dot(a, b, preferred_element_type=F32)  30.5 us
    dot_general x4, matrix products, dot_right_t(): lax.dot_general(a, b, (((1,), (1,)), ((), ())), preferred_element_type=F32)  27.2 us
    dot_general x4, matrix products, dot_left_t(): lax.dot_general(a, b, (((0,), (0,)), ((), ())), preferred_element_type=F32)  23.8 us
  transfers between devices with their start and end apart: 19, of which 11 were waited for; matrix products, arithmetic and copies ran while one was open for 23% of the time, Pallas kernels for 0%

profile of v1, /device:TPU:31, one launch (start us, length us, event | category | flops | bytes accessed | tf_op | source)
XLA Modules:
  0.0 975.2 jit_solution(3480389458058632932)
XLA Ops:
  11.6 21.0 %all_to_all.65 = bf16[8,64,640]{2,1,0:T(8,128)(2,1)} all-to-all(bf16[8,64,640]{2,1,0:T(8,128)(2,1)S(1)} %copy.196), channel_id=1, replica_groups=mesh['x'=2,'core'=2,'z'=4,'y'=2] {'z','core'}, dimensions={0} | all-to-all | bytes 1310720 | tf_op jit(solution)/shard_map/all_to_all | solution.py:43
  39.5 4.7 reshape.606
  47.4 6.9 all-to-all-start.2
  55.1 54.7 %all_gather.33 = f32[1024,128]{0,1:T(8,128)S(1)} all-gather(f32[128,128]{0,1:T(8,128)S(1)} %pad_maximum_fusion.14), channel_id=1, replica_groups=mesh['x'=2,'core'=2,'z'=4,'y'=2] {'z','core'}, dimensions={0}, use_global_device_ids=true | all-gather | bytes 589824 | tf_op jit(solution)/shard_map/all_gather | solution.py:32
  115.9 10.5 %all-gather.10.cloned.1.call-done = bf16[1024,2048]{1,0:T(8,128)(2,1)} async-done(((bf16[128,2048]{1,0:T(8,128)(2,1)}), bf16[1024,2048]{1,0:T(8,128)(2,1)}) %all-gather.10.cloned.1.call-update) | async-done | bytes 4194320 | tf_op jit(solution)/shard_map/all_gather | solution.py:32
  126.5 4.0 fusion.23
  138.1 13.9 %all_gather.37 = bf16[2,4,2,128,128]{4,3,2,1,0:T(8,128)(2,1)S(1)} all-gather(bf16[1,4,2,128,128]{4,3,2,1,0:T(8,128)(2,1)S(1)} %bitcast.402), channel_id=1, replica_groups=mesh['x'=2,'core'=2,'z'=4,'y'=2] {'y'}, dimensions={0}, use_global_device_ids=true | all-gather | bytes 786432 | tf_op jit(solution)/shard_map/all_gather | solution.py:159
  159.4 4.0 fusion.111
  168.4 4.4 fusion.110
  172.8 2.8 fusion.14
  177.4 4.7 convolution_convert_fusion.4
  182.1 5.4 all-to-all-start.1
  188.1 122.8 %all-to-all-done.1 = bf16[8,128,2048]{2,1,0:T(8,128)(2,1)} async-done(((bf16[8,128,2048]{2,1,0:T(8,128)(2,1)}), bf16[8,128,2048]{2,1,0:T(8,128)(2,1)}, u32[]{:S(2)}, u32[]{:S(2)}) %all-to-all-start.1) | async-done | bytes 4194336 | tf_op jit(solution)/shard_map/all_to_all | solution.py:38
  310.9 3.0 convert_reduce_fusion.3
  316.4 7.9 fusion.113
  324.4 9.9 %all-gather.22.cloned.1.call-done = bf16[32,64,1408]{2,1,0:T(8,128)(2,1)} async-done(((bf16[8,64,1408]{2,1,0:T(8,128)(2,1)}), bf16[32,64,1408]{2,1,0:T(8,128)(2,1)}) %all-gather.22.cloned.1.call-update) | async-done | bytes 5767184 | tf_op jit(solution)/shard_map/all_gather | solution.py:49
  334.3 5.7 copy.208
  339.9 42.7 %all-gather.12.cloned.1.call-done = bf16[1024,2048]{1,0:T(8,128)(2,1)} async-done(((bf16[128,2048]{1,0:T(8,128)(2,1)}), bf16[1024,2048]{1,0:T(8,128)(2,1)}) %all-gather.12.cloned.1.call-update) | async-done | bytes 4194320 | tf_op jit(solution)/shard_map/all_gather | solution.py:32
  382.6 8.4 fusion.5
  391.1 5.7 multiply_convert_fusion.3
  396.8 8.6 convolution_convert_fusion.2
  405.5 96.7 %all_to_all.66 = bf16[8,128,2048]{2,1,0:T(8,128)(2,1)S(1)} all-to-all(bf16[8,128,2048]{2,1,0:T(8,128)(2,1)S(1)} %bitcast.394), channel_id=1, replica_groups=mesh['x'=2,'core'=2,'z'=4,'y'=2] {'z','core'}, dimensions={0} | all-to-all | bytes 8388608 | tf_op jit(solution)/shard_map/all_to_all | solution.py:38
  504.9 9.4 convolution_convert_fusion
  514.3 3.0 copy.226
  517.3 5.4 all-to-all-start.10
  522.7 7.5 convolution_convert_fusion.5
  530.2 55.8 %all-to-all-done.10 = bf16[4,512,1408]{2,1,0:T(8,128)(2,1)} async-done(((bf16[4,512,1408]{2,1,0:T(8,128)(2,1)}), bf16[4,512,1408]{2,1,0:T(8,128)(2,1)}, u32[]{:S(2)}, u32[]{:S(2)}) %all-to-all-start.10) | async-done | bytes 5767200 | tf_op jit(solution)/shard_map/all_to_all | solution.py:61
  586.0 5.2 all-to-all-start.12
  591.2 5.0 reduce_sum.230
  596.2 4.5 convolution_convert_fusion.8
  600.8 2.8 reshape.653
  603.5 2.5 copy.210
  619.7 3.0 reshape.616
  622.7 3.0 reshape.615
  636.1 6.5 copy.218
  643.7 5.0 all-to-all-start.5
  648.9 5.7 all-to-all-done.5
  654.6 6.9 all-to-all-start.11
  672.6 2.3 convolution_convert_fusion.7
  674.8 14.6 %all-reduce.4.cloned.1.call-done = f32[1024,128]{0,1:T(8,128)} async-done(((f32[1024,128]{0,1:T(8,128)}), f32[1024,128]{0,1:T(8,128)}) %all-reduce.4.cloned.1.call-update) | async-done | bytes 524304 | tf_op jit(solution)/shard_map/psum | solution.py:236
  692.4 4.7 convolution_convert_fusion.6
  699.2 4.8 all-to-all-start.7
  704.0 7.7 convolution_convert_fusion.3
  711.7 21.9 %all-to-all-done.7 = bf16[4,512,640]{2,1,0:T(8,128)(2,1)} async-done(((bf16[4,512,640]{2,1,0:T(8,128)(2,1)}), bf16[4,512,640]{2,1,0:T(8,128)(2,1)}, u32[]{:S(2)}, u32[]{:S(2)}) %all-to-all-start.7) | async-done | bytes 2621472 | tf_op jit(solution)/shard_map/all_to_all | solution.py:61
  733.6 5.5 all-to-all-start.3
  739.1 3.1 reduce_sum.225
  742.2 88.3 %all-to-all-done.3 = bf16[8,128,2048]{2,1,0:T(8,128)(2,1)} async-done(((bf16[8,128,2048]{2,1,0:T(8,128)(2,1)}), bf16[8,128,2048]{2,1,0:T(8,128)(2,1)}, u32[]{:S(2)}, u32[]{:S(2)}) %all-to-all-start.3) | async-done | bytes 4194336 | tf_op jit(solution)/shard_map/all_to_all | solution.py:38
  830.5 6.1 all-to-all-start.8
  836.7 6.0 convolution_convert_fusion.1
  842.7 9.5 all-to-all-done.8
  853.0 7.3 all-to-all-start.6
  860.3 3.6 convert_reduce_fusion.4
  866.1 4.7 reshape.629
  870.8 2.5 copy.228
  873.4 4.4 reshape.630
  877.8 4.7 reshape.627
  882.5 2.5 copy.227
  885.0 4.7 reshape.628
  889.8 3.3 broadcast_multiply_fusion
  893.2 4.0 convert_reduce_fusion.2
  900.6 51.2 %all-to-all-done.6 = bf16[8,128,2048]{2,1,0:T(8,128)(2,1)} async-done(((bf16[8,128,2048]{2,1,0:T(8,128)(2,1)}), bf16[8,128,2048]{2,1,0:T(8,128)(2,1)}, u32[]{:S(2)}, u32[]{:S(2)}) %all-to-all-start.6) | async-done | bytes 4194336 | tf_op jit(solution)/shard_map/all_to_all | solution.py:38
  951.8 3.0 convert_reduce_fusion
  956.9 6.0 all-to-all-start.9
  962.9 3.1 fusion.54
  (320 shorter events, 99.7 us)
Async XLA Ops:
  7.2 106.6 %all-gather.20.cloned.1.call-start = ((), (), s32[]{:S(2)}) async-start(), calls=%async_computation.19 | async-start | bytes 3276800 | tf_op jit(solution)/shard_map/all_gather | solution.py:49
  11.0 21.6 %copy-start.4 = (bf16[128,2048]{1,0:T(8,128)(2,1)S(1)}, bf16[128,2048]{1,0:T(8,128)(2,1)}, u32[]{:S(2)}) copy-start(bf16[128,2048]{1,0:T(8,128)(2,1)} %param.33) | copy-start | bytes 1572868
  11.4 23.1 %copy-start.68 = (bf16[64]{0:T(256)(128)(2,1)S(1)}, bf16[64]{0:T(256)(128)(2,1)}, u32[]{:S(2)}) copy-start(bf16[64]{0:T(256)(128)(2,1)} %param.45) | copy-start | bytes 388
  11.5 23.1 %copy-start.51 = (bf16[64,5632]{1,0:T(8,128)(2,1)S(1)}, bf16[64,5632]{1,0:T(8,128)(2,1)}, u32[]{:S(2)}) copy-start(bf16[64,5632]{1,0:T(8,128)(2,1)} %param.42) | copy-start | bytes 2162692
  11.5 23.1 %copy-start.52 = (bf16[64,5632]{1,0:T(8,128)(2,1)S(1)}, bf16[64,5632]{1,0:T(8,128)(2,1)}, u32[]{:S(2)}) copy-start(bf16[64,5632]{1,0:T(8,128)(2,1)} %param.43) | copy-start | bytes 2162692
  32.6 93.9 %all-gather.10.cloned.1.call-start = ((), (), s32[]{:S(2)}) async-start(), calls=%async_computation.13 | async-start | bytes 4718592 | tf_op jit(solution)/shard_map/all_gather | solution.py:32
  33.8 282.6 %all-gather.14.cloned.1.call-start = ((), (), s32[]{:S(2)}) async-start(), calls=%async_computation.15 | async-start | bytes 3604480 | tf_op jit(solution)/shard_map/all_gather | solution.py:192
  45.8 9.0 copy-start.71
  45.8 9.0 copy-start.72
  47.4 134.7 %all-to-all-start.2 = ((bf16[8,64,1408]{2,1,0:T(8,128)(2,1)}), bf16[8,64,1408]{2,1,0:T(8,128)(2,1)}, u32[]{:S(2)}, u32[]{:S(2)}) async-start(bf16[8,64,1408]{2,1,0:T(8,128)(2,1)} %pad_maximum_fusion.4), calls=%async_computation.2 | async-start | bytes 2883584 | tf_op jit(solution)/shard_map/all_to_all | solution.py:43
  54.3 262.2 %all-gather.16.cloned.1.call-start = ((), (), s32[]{:S(2)}) async-start(), calls=%async_computation.16 | async-start | bytes 4718592 | tf_op jit(solution)/shard_map/all_gather | solution.py:32
  112.8 22.7 %copy-start.45 = (f32[1024,32]{0,1:T(8,128)}, f32[1024,32]{0,1:T(8,128)S(1)}, u32[]{:S(2)}) copy-start(f32[1024,32]{0,1:T(8,128)S(1)} %get-tuple-element.145) | copy-start | bytes 393220
  112.8 22.7 %copy-start.47 = (f32[1024,32]{0,1:T(8,128)}, f32[1024,32]{0,1:T(8,128)S(1)}, u32[]{:S(2)}) copy-start(f32[1024,32]{0,1:T(8,128)S(1)} %get-tuple-element.144) | copy-start | bytes 393220
  115.9 10.5 %copy-start.16 = (bf16[2,2,4,2,64,640]{5,4,3,2,1,0:T(8,128)(2,1)}, bf16[2,2,4,2,64,640]{5,4,3,2,1,0:T(8,128)(2,1)S(1)}, u32[]{:S(2)}) copy-start(bf16[2,2,4,2,64,640]{5,4,3,2,1,0:T(8,128)(2,1)S(1)} %copy.197) | copy-start | bytes 7864324
  136.6 15.4 %copy-start.33 = (f32[1024,64]{0,1:T(8,128)}, f32[1024,64]{0,1:T(8,128)S(1)}, u32[]{:S(2)}) copy-start(f32[1024,64]{0,1:T(8,128)S(1)} %get-tuple-element.152) | copy-start | bytes 786436
  136.6 15.3 %copy-start.38 = (f32[1024,64]{0,1:T(8,128)}, f32[1024,64]{0,1:T(8,128)S(1)}, u32[]{:S(2)}) copy-start(f32[1024,64]{0,1:T(8,128)S(1)} %get-tuple-element.150) | copy-start | bytes 786436
  152.8 22.8 %copy-start.10 = (bf16[2,1024,128]{1,2,0:T(8,128)(2,1)}, bf16[2,1024,128]{1,2,0:T(8,128)(2,1)S(1)}, u32[]{:S(2)}) copy-start(bf16[2,1024,128]{1,2,0:T(8,128)(2,1)S(1)} %reshape.604) | copy-start | bytes 1572868
  152.8 4.5 copy-start.56
  157.3 6.3 copy-start.19
  159.3 4.0 copy-start.39
  159.3 4.0 copy-start.61
  165.0 11.4 %copy-start.36 = (f32[1,2,4,128,64]{3,4,2,1,0:T(8,128)}, f32[1,2,4,128,64]{3,4,2,1,0:T(8,128)S(1)}, u32[]{:S(2)}) copy-start(f32[1,2,4,128,64]{3,4,2,1,0:T(8,128)S(1)} %convolution_bitcast_fusion.8) | copy-start | bytes 786436
  177.4 4.7 copy-start.27
  182.1 128.8 %all-to-all-start.1 = ((bf16[8,128,2048]{2,1,0:T(8,128)(2,1)}), bf16[8,128,2048]{2,1,0:T(8,128)(2,1)}, u32[]{:S(2)}, u32[]{:S(2)}) async-start(bf16[8,128,2048]{2,1,0:T(8,128)(2,1)} %bitcast.364), calls=%async_computation.1 | async-start | bytes 8388608 | tf_op jit(solution)/shard_map/all_to_all | solution.py:38
  187.5 146.8 %all-gather.22.cloned.1.call-start = ((), (), s32[]{:S(2)}) async-start(), calls=%async_computation.20 | async-start | bytes 7208960 | tf_op jit(solution)/shard_map/all_gather | solution.py:49
  188.1 194.5 %all-gather.12.cloned.1.call-start = ((), (), s32[]{:S(2)}) async-start(), calls=%async_computation.14 | async-start | bytes 4718592 | tf_op jit(solution)/shard_map/all_gather | solution.py:32
  316.1 280.1 %all-gather.18.cloned.1.call-start = ((), (), s32[]{:S(2)}) async-start(), calls=%async_computation.17 | async-start | bytes 4718592 | tf_op jit(solution)/shard_map/all_gather | solution.py:32
  382.6 8.5 copy-start.14
  382.6 8.5 copy-start.70
  382.6 8.5 copy-start.73
  396.8 8.6 copy-start.74
  503.8 10.5 %copy-start.65 = (f32[128]{0:T(128)}, f32[128]{0:T(128)S(1)}, u32[]{:S(2)}) copy-start(f32[128]{0:T(128)S(1)} %broadcast_multiply_fusion.7) | copy-start | bytes 1540
  517.3 68.7 %all-to-all-start.10 = ((bf16[4,512,1408]{2,1,0:T(8,128)(2,1)}), bf16[4,512,1408]{2,1,0:T(8,128)(2,1)}, u32[]{:S(2)}, u32[]{:S(2)}) async-start(bf16[4,512,1408]{2,1,0:T(8,128)(2,1)} %bitcast.365), calls=%async_computation.10 | async-start | bytes 11534336 | tf_op jit(solution)/shard_map/all_to_all | solution.py:61
  586.0 57.7 %all-to-all-start.12 = ((bf16[4,176,2048]{2,1,0:T(8,128)(2,1)}), bf16[4,176,2048]{2,1,0:T(8,128)(2,1)}, u32[]{:S(2)}, u32[]{:S(2)}) async-start(bf16[4,176,2048]{2,1,0:T(8,128)(2,1)} %bitcast.395), calls=%async_computation.12 | async-start | bytes 5767168 | tf_op jit(solution)/shard_map/all_to_all | solution.py:252
  609.5 8.0 copy-start.41
  610.1 6.9 copy-start.25
  612.7 3.7 copy-start.12
  629.8 5.1 copy-start.13
  629.8 5.1 copy-start.43
  636.1 12.7 %copy-start.24 = (f32[1024,4,64]{0,2,1:T(8,128)S(1)}, f32[1024,4,64]{0,2,1:T(8,128)}, u32[]{:S(2)}) copy-start(f32[1024,4,64]{0,2,1:T(8,128)} %reshape.616) | copy-start | bytes 3145732
  636.1 12.7 %copy-start.34 = (f32[1024,64]{0,1:T(8,128)S(1)}, f32[1024,64]{0,1:T(8,128)}, u32[]{:S(2)}) copy-start(f32[1024,64]{0,1:T(8,128)} %copy-done.33) | copy-start | bytes 786436
  643.7 10.9 %all-to-all-start.5 = ((bf16[2,4,2,128,128]{3,1,4,2,0:T(4,128)(2,1)}), bf16[2,4,2,128,128]{3,1,4,2,0:T(4,128)(2,1)}, u32[]{:S(2)}, u32[]{:S(2)}) async-start(bf16[2,4,2,128,128]{3,1,4,2,0:T(4,128)(2,1)} %maximum_bitcast_fusion.1), calls=%async_computation.5 | async-start | bytes 1048576 | tf_op jit(solution)/shard_map/all_to_all | solution.py:234
  654.6 44.6 %all-to-all-start.11 = ((bf16[8,64,1408]{2,1,0:T(8,128)(2,1)}), bf16[8,64,1408]{2,1,0:T(8,128)(2,1)S(1)}, u32[]{:S(2)}, u32[]{:S(2)}) async-start(bf16[8,64,1408]{2,1,0:T(8,128)(2,1)} %bitcast.370), calls=%async_computation.11 | async-start | bytes 2883584 | tf_op jit(solution)/shard_map/all_to_all | solution.py:43
  661.5 27.9 %all-reduce.4.cloned.1.call-start = ((), (), s32[]{:S(2)}) async-start(), calls=%async_computation.18 | async-start | bytes 1048576 | tf_op jit(solution)/shard_map/psum | solution.py:236
  662.7 7.7 copy-start.26
  672.5 16.8 %copy-start.46 = (f32[1024,32]{0,1:T(8,128)S(1)}, f32[1024,32]{0,1:T(8,128)}, u32[]{:S(2)}) copy-start(f32[1024,32]{0,1:T(8,128)} %copy-done.45) | copy-start | bytes 393220
  672.5 18.8 %copy-start.48 = (f32[1024,32]{0,1:T(8,128)S(1)}, f32[1024,32]{0,1:T(8,128)}, u32[]{:S(2)}) copy-start(f32[1024,32]{0,1:T(8,128)} %copy-done.47) | copy-start | bytes 393220
  672.5 19.8 %copy-start.53 = (bf16[1024,256]{0,1:T(8,128)(2,1)S(1)}, bf16[1024,256]{0,1:T(8,128)(2,1)}, u32[]{:S(2)}) copy-start(bf16[1024,256]{0,1:T(8,128)(2,1)} %fusion.58) | copy-start | bytes 1572868
  692.4 4.7 copy-start.49
  699.2 34.4 %all-to-all-start.7 = ((bf16[4,512,640]{2,1,0:T(8,128)(2,1)}), bf16[4,512,640]{2,1,0:T(8,128)(2,1)}, u32[]{:S(2)}, u32[]{:S(2)}) async-start(bf16[4,512,640]{2,1,0:T(8,128)(2,1)} %bitcast.366), calls=%async_computation.7 | async-start | bytes 5242880 | tf_op jit(solution)/shard_map/all_to_all | solution.py:61
  733.6 97.0 %all-to-all-start.3 = ((bf16[8,128,2048]{2,1,0:T(8,128)(2,1)}), bf16[8,128,2048]{2,1,0:T(8,128)(2,1)}, u32[]{:S(2)}, u32[]{:S(2)}) async-start(bf16[8,128,2048]{2,1,0:T(8,128)(2,1)} %bitcast.393), calls=%async_computation.3 | async-start | bytes 8388608 | tf_op jit(solution)/shard_map/all_to_all | solution.py:38
  830.5 21.6 %all-to-all-start.8 = ((bf16[8,64,640]{2,1,0:T(8,128)(2,1)}), bf16[8,64,640]{2,1,0:T(8,128)(2,1)S(1)}, u32[]{:S(2)}, u32[]{:S(2)}) async-start(bf16[8,64,640]{2,1,0:T(8,128)(2,1)} %bitcast.397), calls=%async_computation.8 | async-start | bytes 1310720 | tf_op jit(solution)/shard_map/all_to_all | solution.py:43
  853.0 98.8 %all-to-all-start.6 = ((bf16[8,128,2048]{2,1,0:T(8,128)(2,1)}), bf16[8,128,2048]{2,1,0:T(8,128)(2,1)}, u32[]{:S(2)}, u32[]{:S(2)}) async-start(bf16[8,128,2048]{2,1,0:T(8,128)(2,1)} %bitcast.391), calls=%async_computation.6 | async-start | bytes 8388608 | tf_op jit(solution)/shard_map/all_to_all | solution.py:38
  882.5 7.3 copy-start.64
  885.0 4.8 copy-start.15
  893.1 4.1 copy-start.32
  900.5 55.2 %copy-start.5 = (bf16[128,2048]{1,0:T(8,128)(2,1)S(1)}, bf16[128,2048]{1,0:T(8,128)(2,1)}, u32[]{:S(2)}) copy-start(bf16[128,2048]{1,0:T(8,128)(2,1)} %param.33) | copy-start | bytes 1572868
  900.5 55.2 %copy-start.60 = (f32[128]{0:T(128)S(1)}, f32[128]{0:T(128)}, u32[]{:S(2)}) copy-start(f32[128]{0:T(128)} %copy-done.59) | copy-start | bytes 1540
  900.5 62.4 %copy-start.1 = (f32[128,2048]{1,0:T(8,128)S(1)}, f32[128,2048]{1,0:T(8,128)}, u32[]{:S(2)}) copy-start(f32[128,2048]{1,0:T(8,128)} %copy-done) | copy-start | bytes 3145732
  900.5 62.4 %copy-start.21 = (bf16[128,2048]{1,0:T(8,128)(2,1)S(1)}, bf16[128,2048]{1,0:T(8,128)(2,1)}, u32[]{:S(2)}) copy-start(bf16[128,2048]{1,0:T(8,128)(2,1)} %param.36) | copy-start | bytes 1572868
  900.5 62.4 %copy-start.66 = (f32[128]{0:T(128)S(1)}, f32[128]{0:T(128)}, u32[]{:S(2)}) copy-start(f32[128]{0:T(128)} %copy-done.65) | copy-start | bytes 1540
  956.9 9.1 all-to-all-start.9
  962.9 4.5 copy-start.67
  962.9 4.4 copy-start.69
  (30 other events, 71.1 us)
Sparse Core Ops, SparseCore 0:
  32.7 39.4 all-gather.19
  74.3 52.1 all-gather.9
  128.3 46.8 all-gather.13
  176.7 90.4 all-gather.15
  268.9 65.3 all-gather.21
  336.3 46.2 all-gather.11
  505.0 46.0 all-gather.17
  669.0 20.3 all-reduce.3

commit v2 on v1

--- a/solution.py
+++ b/solution.py
@@ -1,6 +1,10 @@
+import functools
+
 import jax
 import jax.numpy as jnp
 from jax import lax
+from jax.experimental import pallas as pl
+from jax.experimental.pallas import tpu as pltpu
 from jax.sharding import Mesh
 from jax.sharding import PartitionSpec as P
 
@@ -28,38 +32,515 @@
     return lax.dot_general(a, b, (((0,), (0,)), ((), ())), preferred_element_type=F32)
 
 
-def team_gather(rows):
-    return lax.all_gather(rows, TEAM, axis=0, tiled=True)
-
-
-def team_sum_scatter(partial):
-    team = lax.axis_size(TEAM)
-    blocks = partial.reshape(team, partial.shape[0] // team, partial.shape[1])
-    arrived = lax.all_to_all(blocks, TEAM, 0, 0, tiled=False)
-    return jnp.sum(arrived.astype(F32), axis=0)
+MESH = pl.DeviceIdType.MESH
+VM = pltpu.VMEM
+DMA = pltpu.SemaphoreType.DMA
+ROWS = 16
+
+
+def place():
+    return tuple(lax.axis_index(a) for a in ALL)
+
+
+def others(nx, ny):
+    return [(i, j) for i in range(nx) for j in range(ny) if (i, j) != (0, 0)]
+
+
+def data_peer(step, nx, ny):
+    x, _, _, y = place()
+    return lax.rem(x + step[0], nx), lax.rem(y + step[1], ny)
+
+
+def team_peer(step, nz, nc):
+    _, c, z, _ = place()
+    return lax.rem(z + step[0], nz), lax.rem(c + step[1], nc)
+
+
+def greet(nx, nc, nz, ny):
+    barrier = pltpu.get_barrier_semaphore()
+    for step in others(nx, ny):
+        px, py = data_peer(step, nx, ny)
+        pl.semaphore_signal(barrier, inc=1, device_id={"x": px, "y": py}, device_id_type=MESH)
+    for step in others(nz, nc):
+        pz, pc = team_peer(step, nz, nc)
+        pl.semaphore_signal(barrier, inc=1, device_id={"z": pz, "core": pc}, device_id_type=MESH)
+    pl.semaphore_wait(barrier, nx * ny - 1 + nz * nc - 1)
+
+
+def remote(source, target, send, recv, device):
+    return pltpu.make_async_remote_copy(
+        src_ref=source, dst_ref=target, send_sem=send, recv_sem=recv,
+        device_id=device, device_id_type=MESH,
+    )
+
+
+class Gather:
+    SEMS = [DMA((4, 4)), DMA((2, 4))]
+
+    def __init__(self, own, full, send, recv, local):
+        self.own, self.full, self.send, self.recv = own, full, send, recv
+        self.x, self.c, self.z, self.y = place()
+        self.nz = full.shape[0]
+        self.local = pltpu.make_async_copy(own, full.at[self.z, self.c], local)
+
+    def copy(self, at, kind):
+        slot = self.full.at[at, self.c]
+        device = ({"z": self.z + 1}, {"z": self.z - 1}, {"core": 1 - self.c})[kind]
+        return remote(
+            slot, slot, self.send.at[kind, at], self.recv.at[0 if kind < 2 else 1, at], device
+        )
+
+    def start(self):
+        self.local.start()
+        self.local.wait()
+        pl.when(self.z < self.nz - 1)(lambda: self.copy(self.z, 0).start())
+        pl.when(self.z > 0)(lambda: self.copy(self.z, 1).start())
+        self.copy(self.z, 2).start()
+
+    def hop(self, far):
+        @pl.when(self.z - far >= 0)
+        def _():
+            at = self.z - far
+            self.copy(at, 0).wait_recv()
+            pl.when(self.z < self.nz - 1)(lambda: self.copy(at, 0).start())
+            self.copy(at, 2).start()
+
+        @pl.when(self.z + far < self.nz)
+        def _():
+            at = self.z + far
+            self.copy(at, 1).wait_recv()
+            pl.when(self.z > 0)(lambda: self.copy(at, 1).start())
+            self.copy(at, 2).start()
+
+    def finish(self):
+        for at in range(self.nz):
+            pl.when((at <= self.z) & (self.z < self.nz - 1))(lambda at=at: self.copy(at, 0).wait_send())
+            pl.when((at >= self.z) & (self.z > 0))(lambda at=at: self.copy(at, 1).wait_send())
+            self.copy(at, 2).wait_send()
+            self.copy(at, 2).wait_recv()
+
+
+class Reduce:
+    SEMS = [DMA((3, 4)), DMA((3, 4))]
+
+    @staticmethod
+    def buffers(nz, rows, width):
+        return [VM((nz, rows, width), BF), VM((2, nz, rows, width), BF)]
+
+    def __init__(self, part, held, came, send, recv):
+        self.part, self.held, self.came, self.send, self.recv = part, held, came, send, recv
+        self.x, self.c, self.z, self.y = place()
+        self.nz, _, self.rows, self.width = part.shape
+
+    def across(self, to):
+        return remote(
+            self.part.at[to, 1 - self.c], self.held.at[to], self.send.at[2, to], self.recv.at[2, to],
+            {"core": 1 - self.c},
+        )
+
+    def along(self, to, way):
+        device = ({"z": self.z + 1}, {"z": self.z - 1})[way]
+        return remote(
+            self.held.at[to], self.came.at[way, to], self.send.at[way, to], self.recv.at[way, to], device
+        )
+
+    def order(self):
+        return [a for k in range(self.nz) for a in (self.nz - 1 - k, k)][: self.nz]
+
+    def start(self):
+        for to in self.order():
+            self.across(to).start()
+        zeros = jnp.zeros((ROWS, self.width), BF)
+        for way, end in ((0, 0), (1, self.nz - 1)):
+
+            @pl.when(self.z == end)
+            def _(way=way):
+                def clear(i, carry):
+                    for to in range(self.nz):
+                        self.came[way, to, pl.ds(pl.multiple_of(i * ROWS, ROWS), ROWS), :] = zeros
+                    return carry
+
+                lax.fori_loop(0, self.rows // ROWS, clear, 0)
+
+    def add(self, to, ways, out=None):
+        def body(i, carry):
+            at = pl.ds(pl.multiple_of(i * ROWS, ROWS), ROWS)
+            total = self.part[to, self.c, at, :].astype(F32) + self.held[to, at, :].astype(F32)
+            for way in ways:
+                total = total + self.came[way, to, at, :].astype(F32)
+            if out is None:
+                self.held[to, at, :] = total.astype(BF)
+            else:
+                out(at, total)
+            return carry
+
+        lax.fori_loop(0, self.rows // ROWS, body, 0)
+
+    def hop(self, k):
+        for way, to in ((0, self.nz - 1 - k), (1, k)):
+            active = (self.z < to) if way == 0 else (self.z > to)
+            first = (self.z == 0) if way == 0 else (self.z == self.nz - 1)
+
+            @pl.when(active)
+            def _(way=way, to=to, first=first):
+                self.across(to).wait_recv()
+                pl.when(jnp.logical_not(first))(lambda: self.along(to, way).wait_recv())
+                self.add(to, (way,))
+                self.along(to, way).start()
+
+    def last(self, out):
+        self.across(self.z).wait_recv()
+        pl.when(self.z > 0)(lambda: self.along(self.z, 0).wait_recv())
+        pl.when(self.z < self.nz - 1)(lambda: self.along(self.z, 1).wait_recv())
+        self.add(self.z, (0, 1), out)
+
+    def finish(self):
+        for to in range(self.nz):
+            self.across(to).wait_send()
+            pl.when(self.z < to)(lambda to=to: self.along(to, 0).wait_send())
+            pl.when(self.z > to)(lambda to=to: self.along(to, 1).wait_send())
+
+
+class Spread:
+    def __init__(self, source, target, send, recv, local, nx, ny):
+        self.source, self.target, self.send, self.recv = source, target, send, recv
+        self.nx, self.ny = nx, ny
+        self.x, _, _, self.y = place()
+        self.local = pltpu.make_async_copy(source(self.x, self.y), target(self.x, self.y), local)
+
+    def copies(self):
+        for i, step in enumerate(others(self.nx, self.ny)):
+            px, py = data_peer(step, self.nx, self.ny)
+            yield remote(
+                self.source(px, py), self.target(self.x, self.y), self.send.at[i], self.recv.at[i],
+                {"x": px, "y": py},
+            )
+
+    def start(self):
+        for copy in self.copies():
+            copy.start()
+        self.local.start()
+
+    def arrived(self):
+        self.local.wait()
+        for copy in self.copies():
+            copy.wait_recv()
+
+    def finish(self):
+        for copy in self.copies():
+            copy.wait_send()
+
+
+class Swap:
+    def __init__(self, blocks, slot, send, recv, local):
+        self.blocks, self.slot, self.send, self.recv = blocks, slot, send, recv
+        self.nz, self.nc = blocks.shape[:2]
+        _, self.c, self.z, _ = place()
+        self.local = pltpu.make_async_copy(blocks.at[self.z, self.c], slot(self.z, self.c), local)
+
+    def copies(self):
+        for i, step in enumerate(others(self.nz, self.nc)):
+            pz, pc = team_peer(step, self.nz, self.nc)
+            yield remote(
+                self.blocks.at[pz, pc], self.slot(self.z, self.c), self.send.at[i], self.recv.at[i],
+                {"z": pz, "core": pc},
+            )
+
+    def start(self):
+        for copy in self.copies():
+            copy.start()
+        self.local.start()
+
+    def arrived(self):
+        self.local.wait()
+        for copy in self.copies():
+            copy.wait_recv()
+
+    def finish(self):
+        for copy in self.copies():
+            copy.wait_send()
+
+
+def call(kernel, operands, in_spaces, outs, out_spaces, scratch, number):
+    return pl.pallas_call(
+        kernel,
+        out_shape=[jax.ShapeDtypeStruct(s, t) for s, t in outs],
+        in_specs=[pl.BlockSpec(memory_space=s) for s in in_spaces],
+        out_specs=[pl.BlockSpec(memory_space=s) for s in out_spaces],
+        scratch_shapes=scratch,
+        compiler_params=pltpu.CompilerParams(
+            collective_id=number, has_side_effects=True, vmem_limit_bytes=56 << 20
+        ),
+    )(*operands)
+
+
+def first_kernel(dims, n1, table, blocks, n1g, tabg, w_attn, gs, gr, ts, tr, ss, sr, ds, dr, local):
+    nx, nc, nz, ny = dims
+    x, c, z, y = place()
+    greet(*dims)
+    swap = Swap(blocks, lambda pz, pc: w_attn.at[x, pc, pz, y], ss, sr, local.at[0])
+    rows = Gather(n1, n1g, gs, gr, local.at[1])
+    tabs = Gather(table, tabg, ts, tr, local.at[2])
+    swap.start()
+    tabs.start()
+    rows.start()
+    swap.arrived()
+    spread = Spread(
+        lambda px, py: w_attn.at[x, :, :, y], lambda px, py: w_attn.at[px, :, :, py], ds, dr, local.at[3], nx, ny
+    )
+    for copy in spread.copies():
+        copy.start()
+    for far in range(1, nz):
+        tabs.hop(far)
+        rows.hop(far)
+    tabs.finish()
+    rows.finish()
+    swap.finish()
+    for copy in spread.copies():
+        copy.wait_recv()
+    spread.finish()
+
+
+def first_call(dims, n1, table, blocks):
+    nx, nc, nz, ny = dims
+    rows, width = n1.shape
+    own, cols = blocks.shape[2:]
+    peers = nx * ny - 1
+    return call(
+        functools.partial(first_kernel, dims),
+        (n1, table, blocks),
+        (VM, VM, pl.ANY),
+        [
+            ((nz, nc, rows, width), BF),
+            ((nz, nc) + table.shape, F32),
+            ((nx, nc, nz, ny, own, cols), BF),
+        ],
+        (pl.ANY, pl.ANY, pl.ANY),
+        Gather.SEMS * 2 + [DMA((nz * nc - 1,))] * 2 + [DMA((peers,))] * 2 + [DMA((4,))],
+        1,
+    )
+
+
+def middle_kernel(
+    dims, part, tokens, cot, mlp_t, down,
+    mid, n2g, cotg, w_mlp, w_dn,
+    held, came, n2, rs, rr, ns, nr, cs, cr, ms, mr, ws, wr, local,
+):
+    nx, nc, nz, ny = dims
+    x, c, z, y = place()
+    greet(*dims)
+    reduce = Reduce(part, held, came, rs, rr)
+    cots = Gather(cot, cotg, cs, cr, local.at[0])
+    gu = Spread(lambda px, py: mlp_t, lambda px, py: w_mlp.at[px, :, :, py], ms, mr, local.at[1], nx, ny)
+    dn = Spread(lambda px, py: down, lambda px, py: w_dn.at[px, py], ws, wr, local.at[2], nx, ny)
+    reduce.start()
+    gu.start()
+    dn.start()
+    cots.start()
+    for k in range(nz - 1):
+        reduce.hop(k)
+        cots.hop(k + 1)
+
+    def settle(at, total):
+        value = tokens[at, :].astype(F32) + total
+        mid[at, :] = value
+        inverse = lax.rsqrt(jnp.mean(value * value, axis=-1, keepdims=True) + EPSILON)
+        n2[at, :] = (value * inverse).astype(BF)
+
+    reduce.last(settle)
+    rows = Gather(n2, n2g, ns, nr, local.at[3])
+    rows.start()
+    for far in range(1, nz):
+        rows.hop(far)
+    rows.finish()
+    cots.finish()
+    reduce.finish()
+    gu.arrived()
+    dn.arrived()
+    gu.finish()
+    dn.finish()
+
+
+def middle_call(dims, part, tokens, cot, mlp_t, down):
+    nx, nc, nz, ny = dims
+    rows, width = tokens.shape
+    peers = nx * ny - 1
+    return call(
+        functools.partial(middle_kernel, dims),
+        (part, tokens, cot, mlp_t, down),
+        (VM, VM, VM, pl.ANY, pl.ANY),
+        [
+            ((rows, width), F32),
+            ((nz, nc, rows, width), BF),
+            ((nz, nc, rows, width), BF),
+            ((nx, nc, nz, ny) + mlp_t.shape[2:], BF),
+            ((nx, ny) + down.shape, BF),
+        ],
+        (VM, pl.ANY, pl.ANY, pl.ANY, pl.ANY),
+        Reduce.buffers(nz, rows, width)
+        + [VM((rows, width), BF)]
+        + Reduce.SEMS
+        + Gather.SEMS * 2
+        + [DMA((peers,))] * 4
+        + [DMA((4,))],
+        2,
+    )
+
+
+def back_kernel(
+    dims, part, mlp_part, mid, cot, grad_mlp, grad_dn,
+    dx2, dag, output, gain_part, came_mlp, came_dn,
+    held, came, held2, came2, low, rs, rr, os, orr, ds, dr, ms, mr, ws, wr, local,
+):
+    nx, nc, nz, ny = dims
+    x, c, z, y = place()
+    greet(*dims)
+    reduce = Reduce(part, held, came, rs, rr)
+    reduce2 = Reduce(mlp_part, held2, came2, os, orr)
+    reduce.start()
+    dn = Spread(lambda px, py: grad_dn.at[px, py], lambda px, py: came_dn.at[px, py], ws, wr, local.at[0], nx, ny)
+    gu = Spread(
+        lambda px, py: grad_mlp.at[px, :, :, py], lambda px, py: came_mlp.at[px, py], ms, mr, local.at[1], nx, ny
+    )
+    gu.start()
+    dn.start()
+    for k in range(nz - 1):
+        reduce.hop(k)
+    gain_part[...] = jnp.zeros_like(gain_part)
+
+    def settle(at, total):
+        value = mid[at, :]
+        inverse = lax.rsqrt(jnp.mean(value * value, axis=-1, keepdims=True) + EPSILON)
+        normed = value * inverse
+        gain_part[...] += jnp.sum((total * normed).reshape(ROWS // 8, 8, -1), axis=0)
+        gradient = cot[at, :].astype(F32) + inverse * (
+            total - normed * jnp.mean(total * normed, axis=-1, keepdims=True)
+        )
+        dx2[at, :] = gradient
+        low[at, :] = gradient.astype(BF)
+
+    reduce.last(settle)
+    rows = Gather(low, dag, ds, dr, local.at[2])
+    rows.start()
+    reduce2.start()
+    for k in range(nz - 1):
+        rows.hop(k + 1)
+        reduce2.hop(k)
+
+    def finish(at, total):
+        output[at, :] = (mid[at, :] + total).astype(BF)
+
+    reduce2.last(finish)
+    rows.finish()
+    reduce.finish()
+    reduce2.finish()
+    gu.arrived()
+    dn.arrived()
+    gu.finish()
+    dn.finish()
+
+
+def back_call(dims, part, mlp_part, mid, cot, grad_mlp, grad_dn):
+    nx, nc, nz, ny = dims
+    rows, width = mid.shape
+    peers = nx * ny - 1
+    return call(
+        functools.partial(back_kernel, dims),
+        (part, mlp_part, mid, cot, grad_mlp, grad_dn),
+        (VM, VM, VM, VM, pl.ANY, pl.ANY),
+        [
+            ((rows, width), F32),
+            ((nz, nc, rows, width), BF),
+            ((rows, width), BF),
+            ((8, width), F32),
+            ((nx, ny, nc, nz) + grad_mlp.shape[4:], BF),
+            ((nx, ny) + grad_dn.shape[2:], BF),
+        ],
+        (VM, pl.ANY, VM, VM, pl.ANY, pl.ANY),
+        Reduce.buffers(nz, rows, width) * 2
+        + [VM((rows, width), BF)]
+        + Reduce.SEMS * 2
+        + Gather.SEMS
+        + [DMA((peers,))] * 4
+        + [DMA((3,))],
+        3,
+    )
+
+
+def last_kernel(
+    dims, part, tokens, dx2, grad_attn,
+    input_grad, gain_part, attn_g,
+    held, came, came_attn, sums, rs, rr, ds, dr, ss, sr, local,
+):
+    nx, nc, nz, ny = dims
+    x, c, z, y = place()
+    greet(*dims)
+    reduce = Reduce(part, held, came, rs, rr)
+    reduce.start()
+    spread = Spread(
+        lambda px, py: grad_attn.at[px, :, :, py], lambda px, py: came_attn.at[px, py], ds, dr, local.at[0], nx, ny
+    )
+    spread.start()
+    for k in range(nz - 1):
+        reduce.hop(k)
+    spread.arrived()
+
+    own = sums.shape[2]
+
+    def add(i, carry):
+        at = pl.ds(pl.multiple_of(i * ROWS, ROWS), ROWS)
+        for pz in range(nz):
+            for pc in range(nc):
+                total = came_attn[0, 0, pc, pz, at, :].astype(F32)
+                for px, py in others(nx, ny):
+                    total = total + came_attn[px, py, pc, pz, at, :].astype(F32)
+                sums[pz, pc, at, :] = total.astype(BF)
+        return carry
+
+    lax.fori_loop(0, own // ROWS, add, 0)
+    swap = Swap(sums, lambda pz, pc: attn_g.at[pz, pc], ss, sr, local.at[1])
+    swap.start()
+    gain_part[...] = jnp.zeros_like(gain_part)
+
+    def settle(at, total):
+        value = tokens[at, :].astype(F32)
+        inverse = lax.rsqrt(jnp.mean(value * value, axis=-1, keepdims=True) + EPSILON)
+        normed = value * inverse
+        gain_part[...] += jnp.sum((total * normed).reshape(ROWS // 8, 8, -1), axis=0)
+        input_grad[at, :] = dx2[at, :] + inverse * (
+            total - normed * jnp.mean(total * normed, axis=-1, keepdims=True)
+        )
+
+    reduce.last(settle)
+    reduce.finish()
+    spread.finish()
+    swap.arrived()
+    swap.finish()
+
+
+def last_call(dims, part, tokens, dx2, grad_attn):
+    nx, nc, nz, ny = dims
+    rows, width = tokens.shape
+    own, cols = grad_attn.shape[4:]
+    peers = nx * ny - 1
+    return call(
+        functools.partial(last_kernel, dims),
+        (part, tokens, dx2, grad_attn),
+        (VM, VM, VM, pl.ANY),
+        [((rows, width), F32), ((8, width), F32), ((nz, nc, own, cols), BF)],
+        (VM, VM, VM),
+        Reduce.buffers(nz, rows, width)
+        + [VM((nx, ny, nc, nz, own, cols), BF), VM((nz, nc, own, cols), BF)]
+        + Reduce.SEMS
+        + [DMA((peers,))] * 2
+        + [DMA((nz * nc - 1,))] * 2
+        + [DMA((2,))],
+        4,
+    )
 
 
 def team_exchange(blocks):
     return lax.all_to_all(blocks, TEAM, 0, 0, tiled=False)
-
-
-def weights_gather(blocks):
-    z, c = lax.axis_size("z"), lax.axis_size("core")
-    rows, cols = blocks.shape[1:]
-    got = lax.all_gather(blocks, DATA, axis=0)
-    x, y = lax.axis_size("x"), lax.axis_size("y")
-    got = got.reshape(x, y, z, c, rows, cols).transpose(0, 3, 2, 1, 4, 5)
-    return got.reshape(x * c * z * y * rows, cols)
-
-
-def grads_scatter(partial):
-    x, y, z, c = (lax.axis_size(a) for a in ("x", "y", "z", "core"))
-    cols = partial.shape[1]
-    rows = partial.shape[0] // (x * y * z * c)
-    parts = partial.astype(BF).reshape(x, c, z, y, rows, cols).transpose(0, 3, 2, 1, 4, 5)
-    parts = parts.reshape(x * y, z * c * rows, cols)
-    arrived = lax.all_to_all(parts, DATA, 0, 0, tiled=False)
-    return jnp.sum(arrived.astype(F32), axis=0).reshape(z * c, rows, cols)
 
 
 def turn(values):
@@ -83,7 +564,8 @@
     tokens, positions, doc_start, cotangent, w_query, w_key, w_value, w_out,
     attn_gain, w_gate, w_up, w_down, mlp_gain,
 ):
-    nx, nc, nz, ny = (lax.axis_size(a) for a in ALL)
+    dims = tuple(lax.axis_size(a) for a in ALL)
+    nx, nc, nz, ny = dims
     team = nz * nc
     rows, width = tokens.shape
     own = w_query.shape[0]
@@ -123,10 +605,7 @@
         axis=-1,
     )
     mlp_blocks = jnp.concatenate([by_ff(scaled(w_gate, gain_m)), by_ff(scaled(w_up, gain_m))], axis=-1)
-    w_attn = weights_gather(team_exchange(attn_blocks))
-    w_qkv = w_attn[:, : qcols + 2 * HEAD_DIM]
-    w_out_t = w_attn[:, qcols + 2 * HEAD_DIM :]
-
+    mlp_t = team_exchange(mlp_blocks).reshape(nz, nc, own, 2 * ffcols).transpose(1, 0, 2, 3)
     xf = tokens.astype(F32)
     inv1 = lax.rsqrt(jnp.mean(xf * xf, axis=-1, keepdims=True) + EPSILON)
     n1 = xf * inv1
@@ -141,8 +620,14 @@
         ],
         axis=-1,
     )
-    n1g = team_gather(n1.astype(BF))
-    tab = team_gather(table)
+    n1g, tab, w_attn = first_call(
+        dims, n1.astype(BF), table, attn_blocks.reshape(nz, nc, own, attn_blocks.shape[-1])
+    )
+    n1g = n1g.reshape(team * rows, width)
+    tab = tab.reshape(team * rows, table.shape[1])
+    w_attn = w_attn.reshape(width, attn_blocks.shape[-1])
+    w_qkv = w_attn[:, : qcols + 2 * HEAD_DIM]
+    w_out_t = w_attn[:, qcols + 2 * HEAD_DIM :]
     cos_t = jnp.concatenate([tab[:, :half], tab[:, :half]], axis=-1)
     sin_t = jnp.concatenate([tab[:, half : 2 * half], tab[:, half : 2 * half]], axis=-1)
     starts = tab[:, 2 * half].astype(jnp.int32).reshape(nz, nc, rows)
@@ -183,30 +668,30 @@
     context = jnp.stack(contexts)
     ob = context.transpose(0, 1, 3, 2, 4).reshape(total, qcols).astype(BF)
 
-    mid_f = xf + team_sum_scatter(dot_right_t(ob, w_out_t).astype(BF))
-    inv2 = lax.rsqrt(jnp.mean(mid_f * mid_f, axis=-1, keepdims=True) + EPSILON)
-    n2 = mid_f * inv2
-    n2g = team_gather(n2.astype(BF))
-
-    w_mlp = weights_gather(team_exchange(mlp_blocks))
-    w_dn = lax.all_gather(w_down, DATA, axis=0, tiled=True)
+    part = dot_right_t(ob, w_out_t).astype(BF).reshape(nz, nc, rows, width)
+    mid_f, n2g, cotg, w_mlp, w_dn = middle_call(dims, part, tokens, cotangent, mlp_t, w_down)
+    n2g = n2g.reshape(total, width)
+    cotg = cotg.reshape(total, width)
+    w_mlp = w_mlp.reshape(width, 2 * ffcols)
+    w_dn = w_dn.reshape(ffcols, width)
     gt = dot_plain(n2g, w_mlp[:, :ffcols])
     up = dot_plain(n2g, w_mlp[:, ffcols:])
     sg = jax.nn.sigmoid(gt)
     hid = (gt * sg * up).astype(BF)
-    output = (mid_f + team_sum_scatter(dot_plain(hid, w_dn).astype(BF))).astype(BF)
-
-    cotg = team_gather(cotangent)
+    mlp_out = dot_plain(hid, w_dn).astype(BF).reshape(nz, nc, rows, width)
+
     dhid = dot_right_t(cotg, w_dn)
     down_part = dot_left_t(hid, cotg).astype(BF)
     dgt = (dhid * up * sg * (1.0 + gt * (1.0 - sg))).astype(BF)
     dup = (dhid * gt * sg).astype(BF)
     dmlp = jnp.concatenate([dgt, dup], axis=-1)
-    dn2 = team_sum_scatter(dot_right_t(dmlp, w_mlp).astype(BF))
-    mlp_part = dot_left_t(n2g, dmlp).astype(BF)
-    gain_m_part = jnp.sum(dn2 * n2, axis=0)
-    dx2 = cotangent.astype(F32) + inv2 * (dn2 - n2 * jnp.mean(dn2 * n2, axis=-1, keepdims=True))
-    dag = team_gather(dx2.astype(BF))
+    dn2 = dot_right_t(dmlp, w_mlp).astype(BF).reshape(nz, nc, rows, width)
+    mlp_part = dot_left_t(n2g, dmlp).astype(BF).reshape(nx, nc, nz, ny, own, 2 * ffcols)
+    dx2, dag, output, gain_m_part, mlp_came, down_came = back_call(
+        dims, dn2, mlp_out, mid_f, cotangent, mlp_part, down_part.reshape(nx, ny, piece, width)
+    )
+    dag = dag.reshape(total, width)
+    gain_m_part = gain_m_part.sum(0)
     out_part = dot_left_t(dag, ob)
     dob = dot_plain(dag, w_out_t).astype(BF)
 
@@ -240,16 +725,17 @@
     dva = jnp.where(core_at == 1, dva, 0.0)
     dqa = rope_reverse(dq, cos_t[:, None], sin_t[:, None]).reshape(total, qcols)
     dqkv = jnp.concatenate([dqa, dka, dva], axis=-1).astype(BF)
-    dn1 = team_sum_scatter(dot_right_t(dqkv, w_qkv).astype(BF))
+    dn1 = dot_right_t(dqkv, w_qkv).astype(BF).reshape(nz, nc, rows, width)
     qkv_part = dot_left_t(n1g, dqkv)
-    gain_a_part = jnp.sum(dn1 * n1, axis=0)
-    input_grad = dx2 + inv1 * (dn1 - n1 * jnp.mean(dn1 * n1, axis=-1, keepdims=True))
-
-    attn_part = jnp.concatenate([qkv_part, out_part], axis=-1)
-    attn_g = team_exchange(grads_scatter(attn_part).astype(BF)).astype(F32)
-    mlp_g = team_exchange(grads_scatter(mlp_part).astype(BF)).astype(F32)
-    down_blocks = down_part.reshape(nx * ny, piece, width)
-    grad_down = jnp.sum(lax.all_to_all(down_blocks, DATA, 0, 0, tiled=False).astype(F32), axis=0)
+    attn_part = jnp.concatenate([qkv_part, out_part], axis=-1).astype(BF)
+    attn_part = attn_part.reshape(nx, nc, nz, ny, own, attn_part.shape[-1])
+    input_grad, gain_a_part, attn_g = last_call(dims, dn1, tokens, dx2, attn_part)
+    gain_a_part = gain_a_part.sum(0)
+
+    attn_g = attn_g.reshape(team, own, attn_g.shape[-1]).astype(F32)
+    mlp_g = jnp.sum(mlp_came.astype(F32), axis=(0, 1)).astype(BF).transpose(1, 0, 2, 3)
+    mlp_g = team_exchange(mlp_g.reshape(team, own, 2 * ffcols)).astype(F32)
+    grad_down = jnp.sum(down_came.astype(F32), axis=(0, 1))
     grad_query = attn_g[:, :, :qcols].transpose(1, 0, 2).reshape(own, HEADS * HEAD_DIM) * gain_a
     kv_g = attn_g[:, :, qcols : qcols + 2 * HEAD_DIM].reshape(KV_HEADS, kv_rep, own, 2 * HEAD_DIM).sum(1)
     grad_key = kv_g[..., :HEAD_DIM].transpose(1, 0, 2).reshape(own, KV_HEADS * HEAD_DIM) * gain_a

time: 990 us -> 769 us (0.78)
  Pallas kernels: 0 us -> 413 us
  waiting for transfers between devices: 435 us -> 46.8 us
  blocking collectives: 186 us -> 8.62 us
  starting transfers between devices: 65 us -> 21.5 us
  other arithmetic: 66.6 us -> 48.3 us
  matrix products: 111 us -> 101 us
    pallas_call x0 -> x4, Pallas kernels: none -> 413 us  [call(): pl.pallas_call(kernel, out_shape=[jax.ShapeDtypeStruct(s, t) for s, t in...]
    all_to_all x6 -> x0, waiting for transfers between devices: 340 us -> none  [the longest x3 262 us: team_sum_scatter(): arrived = lax.all_to_all(blocks, TEAM, 0, 0, tiled=False)]
    all_to_all x2 -> x0, blocking collectives: 118 us -> none  [the longest x1 96.7 us: team_sum_scatter(): arrived = lax.all_to_all(blocks, TEAM, 0, 0, tiled=False)]
    all_gather x7 -> x0, waiting for transfers between devices: 63.1 us -> none  [the longest x4 53.2 us: team_gather(): return lax.all_gather(rows, TEAM, axis=0, tiled=True)]
    all_gather x1 -> x0, blocking collectives: 54.7 us -> none  [team_gather(): return lax.all_gather(rows, TEAM, axis=0, tiled=True)]
    all_to_all x6 -> x0, starting transfers between devices: 33.6 us -> none  [the longest x3 18.2 us: team_sum_scatter(): arrived = lax.all_to_all(blocks, TEAM, 0, 0, tiled=False)]
    reduce_sum x10 -> x4, other arithmetic: 24.3 us -> 8.26 us  [the longest x1 3.73 us: shards(): jnp.sum(mlp_came.astype(F32), axis=(0, 1)).astype(BF).transpose(1, 0, 2, 3)]
    all_to_all x3 -> x2, waiting for transfers between devices: 9.51 us -> 23.4 us  [team_exchange(): return lax.all_to_all(blocks, TEAM, 0, 0, tiled=False)]
  transfers between devices with their start and end apart: 19 -> 5, of which waited for: 11 -> 2; matrix products, arithmetic and copies ran while one was open for 23% -> 12% of each run, Pallas kernels for 0% -> 11%
where the time goes in v2:
time: 769 us; the launch traced here: 757 us
  Pallas kernels  413 us (54%)
  local copies, waits for them, and re-layouts  102 us (13%)
  matrix products  101 us (13%)
  other arithmetic  48.3 us (6%)
  waiting for transfers between devices  46.8 us (6%)
  starting transfers between devices  21.5 us (3%)
  between operations  15.9 us (2%)
  blocking collectives  8.62 us (1%)
    pallas_call x4, Pallas kernels, call(): pl.pallas_call(kernel, out_shape=[jax.ShapeDtypeStruct(s, t) for s, t in...  413 us
    dot_general x5, matrix products, dot_plain(): return jnp.dot(a, b, preferred_element_type=F32)  26.8 us
    dot_general x4, matrix products, dot_right_t(): lax.dot_general(a, b, (((1,), (1,)), ((), ())), preferred_element_type=F32)  26.7 us
    all_to_all x2, waiting for transfers between devices, team_exchange(): return lax.all_to_all(blocks, TEAM, 0, 0, tiled=False)  23.4 us
    psum x1, waiting for transfers between devices, shards(): dkv = lax.psum(dkv, 'core')  23.4 us
    dot_general x4, matrix products, dot_left_t(): lax.dot_general(a, b, (((0,), (0,)), ((), ())), preferred_element_type=F32)  20.5 us
  transfers between devices with their start and end apart: 5, of which 2 were waited for; matrix products, arithmetic and copies ran while one was open for 12% of the time, Pallas kernels for 11%

profile of v2, /device:TPU:31, one launch (start us, length us, event | category | flops | bytes accessed | tf_op | source)
XLA Modules:
  0.0 757.0 jit_solution(13482374791241359118)
XLA Ops:
  7.8 2.5 multiply_convert_fusion.7
  10.3 2.1 reshape.603
  14.0 4.7 reshape.605
  20.4 1.5 pad_maximum_fusion.4
  22.0 6.1 all-to-all-start
  32.1 83.7 %shard_map.222 = (bf16[4,2,128,2048]{3,2,1,0:T(8,128)(2,1)}, f32[4,2,128,128]{3,2,1,0:T(8,128)}, bf16[2,2,4,2,64,640]{5,4,3,2,1,0:T(8,128)(2,1)}) custom-call(bf16[128,2048]{1,0:T(8,128)(2,1)} %fusion.50.n1, f32[128,128]{1,0:T(8,128)} %pad_maximum_fusion.14.table, bf16[4,2,64,640]{3,2,1,0:T(8,128)(2,1)} %pad_maximum_fusion.8.blocks), custom_call_target="tpu_custom_call" | custom-call | tf_op jit(solution)/shard_map/pallas_call | solution.py:265
  115.9 4.5 fusion.20
  122.6 1.7 pad_maximum_fusion.9
  129.8 1.5 concatenate.86
  132.3 8.6 %all_gather.3 = bf16[2,4,2,128,128]{4,3,2,1,0:T(8,128)(2,1)S(1)} all-gather(bf16[1,4,2,128,128]{4,3,2,1,0:T(8,128)(2,1)S(1)} %bitcast.407), channel_id=1, replica_groups=mesh['x'=2,'core'=2,'z'=4,'y'=2] {'y'}, dimensions={0}, use_global_device_ids=true | all-gather | bytes 786432 | tf_op jit(solution)/shard_map/all_gather | solution.py:644
  142.2 1.5 fusion.64
  146.8 1.9 fusion.101
  150.0 3.9 fusion.100
  154.1 2.0 copy-done.22
  159.3 4.4 fusion.99
  163.8 2.7 fusion.14
  170.1 2.2 mul.300
  172.4 2.5 copy.209
  174.9 6.4 copy.219
  181.4 4.5 convolution_convert_fusion.4
  185.9 2.6 copy.275
  188.4 132.8 %shard_map.223 = (f32[128,2048]{1,0:T(8,128)}, bf16[4,2,128,2048]{3,2,1,0:T(8,128)(2,1)}, bf16[4,2,128,2048]{3,2,1,0:T(8,128)(2,1)}, bf16[2,2,4,2,64,1408]{5,4,3,2,1,0:T(8,128)(2,1)}, bf16[2,2,176,2048]{3,2,1,0:T(8,128)(2,1)}) custom-call(bf16[4,2,128,2048]{3,2,1,0:T(8,128)(2,1)} %bitcast.373, bf16[128,2048]{1,0:T(8,128)(2,1)} %tokens.3, ...), custom_call_target="tpu_custom_call" | custom-call | tf_op jit(solution)/shard_map/pallas_call | solution.py:265
  321.2 8.0 %fusion.103 = f32[1024,704]{0,1:T(8,128)} fusion(bf16[1024,2048]{1,0:T(8,128)(2,1)} %bitcast.429, bf16[704,2048]{1,0:T(8,128)(2,1)} %bitcast.431), kind=kOutput, calls=%fused_computation.238 | convolution fusion | flops 2952790016 | bytes 9961472 | tf_op jit(solution)/shard_map/dot_general | solution.py:28
  329.2 3.3 fusion.5
  332.5 9.8 %multiply_convert_fusion.2 = (bf16[1024,704]{0,1:T(8,128)(2,1)}, bf16[1024,704]{0,1:T(8,128)(2,1)}, bf16[1024,704]{0,1:T(8,128)(2,1)}) fusion(f32[1024,704]{0,1:T(8,128)S(1)} %fusion.5, f32[1024,704]{0,1:T(8,128)} %fusion.103, bf16[1024,2048]{1,0:T(8,128)(2,1)S(1)} %bitcast.427, bf16[2048,1408]{1,0:T(8,128)(2,1)S(1)} %bitcast.424), kind=kOutput, calls=%fused_computation.23 | convolution fusion | flops 2964324352 | bytes 17432576 | tf_op jit(solution)/shard_map/dot_general | solution.py:24
  342.3 6.0 convolution_convert_fusion.5
  348.4 5.5 convolution_convert_fusion.2
  353.9 8.5 %convolution_convert_fusion = bf16[2048,1408]{1,0:T(8,128)(2,1)} fusion(bf16[1024,2048]{1,0:T(8,128)(2,1)S(1)} %bitcast.428, bf16[1024,704]{0,1:T(8,128)(2,1)S(1)} %copy-done.63, bf16[1024,704]{0,1:T(8,128)(2,1)S(1)} %copy-done.62), kind=kOutput, calls=%fused_computation.4 | convolution fusion | flops 5914230784 | bytes 12845056 | tf_op jit(solution)/shard_map/dot_general | solution.py:32
  362.4 8.3 %convolution_convert_fusion.3 = bf16[1024,2048]{1,0:T(8,128)(2,1)} fusion(bf16[2048,1408]{1,0:T(8,128)(2,1)S(1)} %bitcast.425, bf16[1024,704]{0,1:T(8,128)(2,1)S(1)} %copy-done.63, bf16[1024,704]{0,1:T(8,128)(2,1)S(1)} %copy-done.62), kind=kOutput, calls=%fused_computation.11 | convolution fusion | flops 5913444352 | bytes 12845056 | tf_op jit(solution)/shard_map/dot_general | solution.py:28
  370.7 122.9 %shard_map.224 = (f32[128,2048]{1,0:T(8,128)}, bf16[4,2,128,2048]{3,2,1,0:T(8,128)(2,1)}, bf16[128,2048]{1,0:T(8,128)(2,1)}, f32[8,2048]{1,0:T(8,128)}, bf16[2,2...) custom-call(bf16[4,2,128,2048]{3,2,1,0:T(8,128)(2,1)} %bitcast.402, ...), custom_call_target="tpu_custom_call" | custom-call | tf_op jit(solution)/shard_map/pallas_call | solution.py:265
  493.6 3.7 convolution_convert_fusion.8
  498.8 1.5 copy.206
  501.8 1.8 fusion.27
  503.9 1.8 fusion.48
  514.6 1.8 copy.207
  516.4 3.0 reshape.619
  519.5 2.5 broadcast_multiply_fusion.2
  526.1 1.9 copy.212
  528.9 1.6 fusion.42
  531.7 2.1 maximum_bitcast_fusion.1
  533.9 4.4 all-to-all-start.1
  544.2 2.2 copy.214
  546.4 2.0 convert_reduce_fusion.1
  548.4 2.0 copy.258
  551.4 6.5 copy.220
  558.0 3.5 convolution_convert_fusion.7
  561.5 23.4 %all-reduce.4.cloned.1.call-done = f32[1024,128]{0,1:T(8,128)} async-done(((f32[1024,128]{0,1:T(8,128)}), f32[1024,128]{0,1:T(8,128)}) %all-reduce.4.cloned.1.call-update) | async-done | bytes 524304 | tf_op jit(solution)/shard_map/psum | solution.py:721
  588.3 6.0 convolution_convert_fusion.1
  594.2 2.5 convolution_convert_fusion.6
  596.7 1.9 pad_maximum_fusion.1.grad_attn
  598.6 73.1 %shard_map.225 = (f32[128,2048]{1,0:T(8,128)}, f32[8,2048]{1,0:T(8,128)}, bf16[4,2,64,640]{3,2,1,0:T(8,128)(2,1)}) custom-call(bf16[4,2,128,2048]{3,2,1,0:T(8,128)(2,1)} %bitcast.398, bf16[128,2048]{1,0:T(8,128)(2,1)} %tokens.3, f32[128,2048]{1,0:T(8,128)} %get-tuple-element.150.dx2, bf16[2,2,4,2,64,640]{5,4,3,2,1,0:T(8,128)(2,1)} %pad_maximum_fusion.1.grad_attn), custom_call_target="tpu_custom_call" | custom-call | tf_op jit(solution)/shard_map/pallas_call | solution.py:265
  673.4 5.6 all-to-all-start.2
  679.0 3.7 reduce_sum.147
  684.0 5.4 all-to-all-start.3
  689.4 3.7 convert_reduce_fusion
  698.3 23.4 %all-to-all-done.3 = bf16[8,64,1408]{2,1,0:T(8,128)(2,1)S(1)} async-done(((bf16[8,64,1408]{2,1,0:T(8,128)(2,1)}), bf16[8,64,1408]{2,1,0:T(8,128)(2,1)S(1)}, u32[]{:S(2)}, u32[]{:S(2)}) %all-to-all-start.3) | async-done | bytes 1441824 | tf_op jit(solution)/shard_map/all_to_all | solution.py:543
  721.7 2.1 fusion.94
  723.9 4.7 reshape.628
  728.6 2.6 copy.227
  731.2 3.6 reshape.629
  734.7 4.7 reshape.630
  739.5 2.6 copy.228
  742.1 3.9 reshape.631
  746.0 1.9 broadcast_multiply_fusion
  (264 shorter events, 67.4 us)
Async XLA Ops:
  7.8 2.5 copy-start.50
  20.4 7.8 %copy-start.52 = (bf16[64]{0:T(256)(128)(2,1)S(1)}, bf16[64]{0:T(256)(128)(2,1)}, u32[]{:S(2)}) copy-start(bf16[64]{0:T(256)(128)(2,1)} %param.41) | copy-start | bytes 388
  20.4 7.8 %copy-start.46 = (bf16[64,256]{1,0:T(8,128)(2,1)S(1)}, bf16[64,256]{1,0:T(8,128)(2,1)}, u32[]{:S(2)}) copy-start(bf16[64,256]{1,0:T(8,128)(2,1)} %param.38) | copy-start | bytes 98308
  20.4 7.8 %copy-start.47 = (bf16[64,256]{1,0:T(8,128)(2,1)S(1)}, bf16[64,256]{1,0:T(8,128)(2,1)}, u32[]{:S(2)}) copy-start(bf16[64,256]{1,0:T(8,128)(2,1)} %param.39) | copy-start | bytes 98308
  20.4 8.1 %copy-start.43 = (bf16[64,2048]{1,0:T(8,128)(2,1)S(1)}, bf16[64,2048]{1,0:T(8,128)(2,1)}, u32[]{:S(2)}) copy-start(bf16[64,2048]{1,0:T(8,128)(2,1)} %param.37) | copy-start | bytes 786436
  22.0 6.7 copy-start.44
  22.0 6.7 copy-start.59
  22.0 6.8 copy-start.60
  22.0 6.8 copy-start.3
  22.0 163.9 %all-to-all-start = ((bf16[8,64,1408]{2,1,0:T(8,128)(2,1)}), bf16[8,64,1408]{2,1,0:T(8,128)(2,1)}, u32[]{:S(2)}, u32[]{:S(2)}) async-start(bf16[8,64,1408]{2,1,0:T(8,128)(2,1)} %pad_maximum_fusion.4), calls=%async_computation | async-start | bytes 2883584 | tf_op jit(solution)/shard_map/all_to_all | solution.py:543
  28.2 3.9 copy-start.48
  120.4 1.8 copy-start.34
  120.4 1.4 copy-start.12
  122.4 4.7 copy-start.35
  124.3 1.2 copy-start.27
  127.1 5.0 copy-start.42
  143.7 6.3 copy-start.32
  144.4 1.6 copy-start.37
  145.9 21.4 %copy-start.26 = (f32[1,2,4,128,64]{3,4,2,1,0:T(8,128)}, f32[1,2,4,128,64]{3,4,2,1,0:T(8,128)S(1)}, u32[]{:S(2)}) copy-start(f32[1,2,4,128,64]{3,4,2,1,0:T(8,128)S(1)} %convolution_bitcast_fusion.5) | copy-start | bytes 786436
  148.7 5.2 copy-start.30
  153.9 2.3 copy-start.22
  154.1 2.8 copy-start.2
  157.6 9.7 %copy-start.28 = (f32[1,2,4,128,64]{3,4,2,1,0:T(8,128)}, f32[1,2,4,128,64]{3,4,2,1,0:T(8,128)S(1)}, u32[]{:S(2)}) copy-start(f32[1,2,4,128,64]{3,4,2,1,0:T(8,128)S(1)} %convolution_bitcast_fusion.8) | copy-start | bytes 786436
  163.8 3.5 copy-start.29
  170.1 11.2 %copy-start.20 = (bf16[1024,256]{0,1:T(8,128)(2,1)}, bf16[1024,256]{0,1:T(8,128)(2,1)S(1)}, u32[]{:S(2)}) copy-start(bf16[1024,256]{0,1:T(8,128)(2,1)S(1)} %convert_element_type.184) | copy-start | bytes 1572868
  321.2 8.0 %copy-start.55 = (bf16[2,2,4,2,64,1408]{5,4,3,2,1,0:T(8,128)(2,1)S(1)}, bf16[2,2,4,2,64,1408]{5,4,3,2,1,0:T(8,128)(2,1)}, u32[]{:S(2)}) copy-start(bf16[2,2,4,2,64,1408]{5,4,3,2,1,0:T(8,128)(2,1)} %get-tuple-element.146) | copy-start | bytes 17301508
  321.2 8.0 %copy-start.56 = (bf16[4,2,128,2048]{3,2,1,0:T(8,128)(2,1)S(1)}, bf16[4,2,128,2048]{3,2,1,0:T(8,128)(2,1)}, u32[]{:S(2)}) copy-start(bf16[4,2,128,2048]{3,2,1,0:T(8,128)(2,1)} %get-tuple-element.145) | copy-start | bytes 12582916
  332.5 9.8 %copy-start.57 = (bf16[4,2,128,2048]{3,2,1,0:T(8,128)(2,1)S(1)}, bf16[4,2,128,2048]{3,2,1,0:T(8,128)(2,1)}, u32[]{:S(2)}) copy-start(bf16[4,2,128,2048]{3,2,1,0:T(8,128)(2,1)} %get-tuple-element.143) | copy-start | bytes 12582916
  342.3 6.0 copy-start.58
  342.3 6.0 copy-start.61
  348.4 5.5 copy-start.62
  348.4 5.5 copy-start.63
  500.3 10.4 %copy-start.8 = (bf16[4,2,128,4,64]{2,4,3,1,0:T(8,128)(2,1)}, bf16[4,2,128,4,64]{2,4,3,1,0:T(8,128)(2,1)S(1)}, u32[]{:S(2)}) copy-start(bf16[4,2,128,4,64]{2,4,3,1,0:T(8,128)(2,1)S(1)} %copy.206) | copy-start | bytes 1572868
  501.8 3.9 copy-start.11
  501.8 4.7 copy-start.31
  506.6 2.3 copy-start.23
  508.8 2.8 copy-start.16
  512.5 1.3 copy-start.4
  514.6 4.9 copy-start.25
  519.5 3.6 copy-start.19
  519.5 4.8 copy-start.7
  519.5 4.8 copy-start.33
  522.0 2.8 copy-start.5
  526.1 4.4 copy-start.1
  526.1 4.5 copy-start.9
  531.5 6.8 copy-start.17
  533.9 10.3 %all-to-all-start.1 = ((bf16[2,4,2,128,128]{3,1,4,2,0:T(4,128)(2,1)}), bf16[2,4,2,128,128]{3,1,4,2,0:T(4,128)(2,1)}, u32[]{:S(2)}, u32[]{:S(2)}) async-start(bf16[2,4,2,128,128]{3,1,4,2,0:T(4,128)(2,1)} %maximum_bitcast_fusion.1), calls=%async_computation.1 | async-start | bytes 1048576 | tf_op jit(solution)/shard_map/all_to_all | solution.py:719
  538.3 46.6 %all-reduce.4.cloned.1.call-start = ((), (), s32[]{:S(2)}) async-start(), calls=%async_computation.4 | async-start | bytes 1048576 | tf_op jit(solution)/shard_map/psum | solution.py:721
  544.2 6.3 copy-start.13
  544.2 6.3 copy-start.14
  551.4 6.5 copy-start.45
  551.4 6.6 copy-start.21
  558.0 27.9 %copy-start.36 = (f32[1024,32]{0,1:T(8,128)S(1)}, f32[1024,32]{0,1:T(8,128)}, u32[]{:S(2)}) copy-start(f32[1024,32]{0,1:T(8,128)} %copy-done.35) | copy-start | bytes 393220
  561.5 26.7 %copy-start.40 = (bf16[1024,256]{1,0:T(8,128)(2,1)S(1)}, bf16[1024,256]{1,0:T(8,128)(2,1)}, u32[]{:S(2)}) copy-start(bf16[1024,256]{1,0:T(8,128)(2,1)} %add_convert_fusion) | copy-start | bytes 1572868
  588.3 6.0 copy-start.15
  673.4 10.6 %all-to-all-start.2 = ((f32[32,1,128]{2,1,0:T(1,128)}), f32[32,1,128]{2,1,0:T(1,128)S(1)}, u32[]{:S(2)}, u32[]{:S(2)}) async-start(f32[32,1,128]{2,1,0:T(1,128)} %reshape.653), calls=%async_computation.2 | async-start | bytes 32768 | tf_op jit(solution)/shard_map/all_to_all | solution.py:752
  684.0 37.7 %all-to-all-start.3 = ((bf16[8,64,1408]{2,1,0:T(8,128)(2,1)}), bf16[8,64,1408]{2,1,0:T(8,128)(2,1)S(1)}, u32[]{:S(2)}, u32[]{:S(2)}) async-start(bf16[8,64,1408]{2,1,0:T(8,128)(2,1)} %bitcast.117), calls=%async_computation.3 | async-start | bytes 2883584 | tf_op jit(solution)/shard_map/all_to_all | solution.py:543
  689.4 3.7 copy-start.39
  693.2 1.6 copy-start.49
  693.7 4.1 copy-start.53
  693.7 4.1 copy-start.54
  739.5 6.5 copy-start.51
  745.9 1.9 copy-start.41
  746.0 2.7 copy-start.38
  (5 other events, 5.4 us)
Sparse Core Ops, SparseCore 0:
  550.6 34.3 all-reduce.3

commit v3 on v2

--- a/solution.py
+++ b/solution.py
@@ -56,15 +56,20 @@
     return lax.rem(z + step[0], nz), lax.rem(c + step[1], nc)
 
 
-def greet(nx, nc, nz, ny):
+def greet(nx, nc, nz, ny, cross=False):
     barrier = pltpu.get_barrier_semaphore()
+    x, c, z, y = place()
+    extra = ny - 1 if cross else 0
+    for i in range(extra):
+        device = {"y": lax.rem(y + 1 + i, ny), "core": 1 - c}
+        pl.semaphore_signal(barrier, inc=1, device_id=device, device_id_type=MESH)
     for step in others(nx, ny):
         px, py = data_peer(step, nx, ny)
         pl.semaphore_signal(barrier, inc=1, device_id={"x": px, "y": py}, device_id_type=MESH)
     for step in others(nz, nc):
         pz, pc = team_peer(step, nz, nc)
         pl.semaphore_signal(barrier, inc=1, device_id={"z": pz, "core": pc}, device_id_type=MESH)
-    pl.semaphore_wait(barrier, nx * ny - 1 + nz * nc - 1)
+    pl.semaphore_wait(barrier, nx * ny - 1 + nz * nc - 1 + extra)
 
 
 def remote(source, target, send, recv, device):
@@ -539,24 +544,304 @@
     )
 
 
-def team_exchange(blocks):
-    return lax.all_to_all(blocks, TEAM, 0, 0, tiled=False)
-
-
-def turn(values):
-    half = values.shape[-1] // 2
-    return jnp.concatenate([-values[..., half:], values[..., :half]], axis=-1)
-
-
-def rope_apply(values, cos_table, sin_table):
-    return values * cos_table + turn(values) * sin_table
-
-
-def rope_reverse(gradient, cos_table, sin_table):
-    half = gradient.shape[-1] // 2
-    scaled = gradient * sin_table
-    return gradient * cos_table + jnp.concatenate(
-        [scaled[..., half:], -scaled[..., :half]], axis=-1
+def nt(a, b):
+    return lax.dot_general(a, b, (((1,), (1,)), ((), ())), preferred_element_type=F32)
+
+
+def nn(a, b):
+    return jnp.dot(a, b, preferred_element_type=F32)
+
+
+def lanes(shape):
+    return lax.broadcasted_iota(jnp.int32, shape, len(shape) - 1)
+
+
+def rope_lanes(tab):
+    at = lanes(tab.shape)
+    cos = jnp.where(at < 32, tab, 0.0)
+    sin = jnp.where((at >= 32) & (at < 64), tab, 0.0)
+    cos = cos + pltpu.roll(cos, 32, 1)
+    cos = cos + pltpu.roll(cos, 64, 1)
+    sin = sin - pltpu.roll(sin, 96, 1)
+    sin = sin + pltpu.roll(sin, 64, 1)
+    return cos, sin
+
+
+def swap_halves(u):
+    return jnp.where(lax.rem(lanes(u.shape), 64) < 32, pltpu.roll(u, 96, 1), pltpu.roll(u, 32, 1))
+
+
+def two_heads(u):
+    first = lanes(u.shape) < 64
+    zero = jnp.zeros_like(u)
+    return jnp.concatenate([jnp.where(first, u, zero), jnp.where(first, zero, u)], axis=0)
+
+
+def join_heads(t):
+    rows = t.shape[1] // 2
+    return jnp.concatenate([t[:64, :rows], t[64:, rows:]], axis=0).T
+
+
+def bias_of(tab, keys, first_row):
+    rows = tab.shape[0]
+    starts = tab.T[64:65, :].astype(jnp.int32)
+    key = lax.broadcasted_iota(jnp.int32, (keys, rows), 0)
+    row = first_row + lax.broadcasted_iota(jnp.int32, (keys, rows), 1)
+    bias = jnp.where((key >= starts) & (key <= row), 0.0, MASKED)
+    return jnp.concatenate([bias, bias], axis=1)
+
+
+def attend_kernel(
+    dims, n1g, w, tab, mlp_blocks,
+    q, kk, vv, stat, ob, part, mlp_t,
+    kv, vt, ss, sr, ys, yr, local,
+):
+    nx, nc, nz, ny = dims
+    x, c, z, y = place()
+    rows, width = n1g.shape[2:]
+    qcols = q.shape[-1]
+    pairs = qcols // 128
+    greet(*dims)
+    swap = Swap(mlp_blocks, lambda pz, pc: mlp_t.at[pc, pz], ss, sr, local.at[0])
+    swap.start()
+
+    def project(i, carry):
+        res = nn(n1g[i].reshape(nc * rows, width), w[:, : qcols + 128])
+        cos, sin = rope_lanes(tab[i].reshape(nc * rows, 128))
+        for p in range(pairs):
+            u = res[:, p * 128 : p * 128 + 128]
+            u = (u * cos + swap_halves(u) * sin) * (HEAD_DIM ** (-0.5))
+            q[i, :, :, p * 128 : p * 128 + 128] = u.astype(BF).reshape(nc, rows, 128)
+        u = res[:, qcols : qcols + 128]
+        u = jnp.where(lanes(u.shape) < 64, u * cos + swap_halves(u) * sin, u).astype(BF)
+        for pc in range(nc):
+            kv[pc, i, y] = u[pc * rows : (pc + 1) * rows]
+        return carry
+
+    lax.fori_loop(0, nz, project, 0)
+    sends = []
+    for i in range(ny - 1):
+        slot = kv.at[:, :, y]
+        sends.append(remote(slot, slot, ys.at[i], yr.at[i], {"y": lax.rem(y + 1 + i, ny)}))
+    for copy in sends:
+        copy.start()
+    for copy in sends:
+        copy.wait_recv()
+
+    span = ny * rows
+
+    def double(i, carry):
+        pc, pz = i // nz, lax.rem(i, nz)
+        u = kv[pc, pz].reshape(span, 128).astype(F32)
+        r = pltpu.roll(u, 64, 1)
+        first = lanes(u.shape) < 64
+        at = pl.ds(pl.multiple_of(pz * span, span), span)
+        kk[pc, at, :] = jnp.where(first, u, r).astype(BF)
+        values = jnp.where(first, r, u)
+        vv[pc, at, :] = values.astype(BF)
+        vt[pc, :, at] = values.T.astype(BF)
+        return carry
+
+    lax.fori_loop(0, nc * nz, double, 0)
+
+    def attend(pc, carry):
+        for pz in range(nz):
+            keys = (pz + 1) * span
+            bias = bias_of(tab[pz, pc], keys, (pz * ny + y) * rows)
+            for p in range(pairs):
+                q2 = two_heads(q[pz, pc, :, p * 128 : p * 128 + 128])
+                s = nt(kk[pc, :keys, :], q2) + bias
+                top = jnp.max(s, axis=0, keepdims=True)
+                e = jnp.exp(s - top)
+                total = jnp.sum(e, axis=0, keepdims=True)
+                stat[pz, pc, p : p + 1, :] = top + jnp.log(total)
+                weights = (e * (1.0 / total)).astype(BF)
+                o = join_heads(nn(vt[pc, :, :keys], weights))
+                ob[pz, pc, :, p * 128 : p * 128 + 128] = o.astype(BF)
+        return carry
+
+    lax.fori_loop(0, nc, attend, 0)
+
+    def output(i, carry):
+        pz, n = i // 4, lax.rem(i, 4)
+        at = pl.ds(pl.multiple_of(n * (width // 4), width // 4), width // 4)
+        res = nt(ob[pz].reshape(nc * rows, qcols), w[at, qcols + 128 : 2 * qcols + 128])
+        part[pz, :, :, at] = res.astype(BF).reshape(nc, rows, width // 4)
+        return carry
+
+    lax.fori_loop(0, nz * 4, output, 0)
+    for copy in sends:
+        copy.wait_send()
+    swap.arrived()
+    swap.finish()
+
+
+def attend_call(dims, n1g, w, tab, mlp_blocks):
+    nx, nc, nz, ny = dims
+    rows, width = n1g.shape[2:]
+    qcols = (w.shape[1] - 128) // 2
+    keys = nz * ny * rows
+    members = nz * nc - 1
+    own, cols = mlp_blocks.shape[2:]
+    return call(
+        functools.partial(attend_kernel, dims),
+        (n1g, w, tab, mlp_blocks),
+        (VM, VM, VM, pl.ANY),
+        [
+            ((nz, nc, rows, qcols), BF),
+            ((nc, keys, 128), BF),
+            ((nc, keys, 128), BF),
+            ((nz, nc, 8, 2 * rows), F32),
+            ((nz, nc, rows, qcols), BF),
+            ((nz, nc, rows, width), BF),
+            ((nc, nz, own, cols), BF),
+        ],
+        (VM, VM, VM, VM, VM, VM, pl.ANY),
+        [VM((nc, nz, ny, rows, 128), BF), VM((nc, 128, keys), BF)]
+        + [DMA((members,))] * 2
+        + [DMA((max(ny - 1, 1),))] * 2
+        + [DMA((1,))],
+        5,
+    )
+
+
+def attend_back_kernel(
+    dims, dag, w, tab, q, kk, vv, stat, mlp_sum,
+    dqkv, part, mlp_g,
+    do, kt, dk, dv, out, came, ss, sr, ys, yr, local,
+):
+    nx, nc, nz, ny = dims
+    x, c, z, y = place()
+    rows, width = dag.shape[2:]
+    qcols = q.shape[-1]
+    pairs = qcols // 128
+    span = ny * rows
+    greet(*dims, cross=True)
+    swap = Swap(mlp_sum, lambda pz, pc: mlp_g.at[pz, pc], ss, sr, local.at[0])
+    swap.start()
+
+    def project(i, carry):
+        res = nn(dag[i].reshape(nc * rows, width), w[:, qcols + 128 : 2 * qcols + 128])
+        do[i] = res.astype(BF).reshape(nc, rows, qcols)
+        return carry
+
+    lax.fori_loop(0, nz, project, 0)
+
+    def turned(i, carry):
+        pc, pz = i // nz, lax.rem(i, nz)
+        at = pl.ds(pl.multiple_of(pz * span, span), span)
+        kt[pc, :, at] = kk[pc, at, :].astype(F32).T.astype(BF)
+        return carry
+
+    lax.fori_loop(0, nc * nz, turned, 0)
+
+    def attend(pc, carry):
+        for pz in reversed(range(nz)):
+            keys = (pz + 1) * span
+            bias = bias_of(tab[pz, pc], keys, (pz * ny + y) * rows)
+            cos, sin = rope_lanes(tab[pz, pc])
+            for p in range(pairs):
+                q2 = two_heads(q[pz, pc, :, p * 128 : p * 128 + 128])
+                do2 = two_heads(do[pz, pc, :, p * 128 : p * 128 + 128])
+                s = nt(kk[pc, :keys, :], q2) + bias
+                weights = jnp.exp(s - stat[pz, pc, p : p + 1, :])
+                dw = nt(vv[pc, :keys, :], do2)
+                dw = weights * dw
+                delta = jnp.sum(dw, axis=0, keepdims=True)
+                ds = (dw - weights * delta).astype(BF)
+                dv_new = nn(weights.astype(BF), do2)
+                dk_new = nn(ds, q2)
+                if pz == nz - 1 and p == 0:
+                    dv[pc, :keys, :] = dv_new
+                    dk[pc, :keys, :] = dk_new
+                else:
+                    dv[pc, :keys, :] += dv_new
+                    dk[pc, :keys, :] += dk_new
+                u = join_heads(nn(kt[pc, :, :keys], ds)) * (HEAD_DIM ** (-0.5))
+                u = u * cos - swap_halves(u) * sin
+                dqkv[pz, pc, :, p * 128 : p * 128 + 128] = u.astype(BF)
+        return carry
+
+    lax.fori_loop(0, nc, attend, 0)
+
+    def fold(i, carry):
+        pc, pz = i // nz, lax.rem(i, nz)
+        at = pl.ds(pl.multiple_of(pz * span, span), span)
+        key, value = dk[pc, at, :], dv[pc, at, :]
+        first = lanes(key.shape) < 64
+        both = jnp.where(first, key + pltpu.roll(key, 64, 1), value + pltpu.roll(value, 64, 1))
+        both = both.astype(BF)
+        for py in range(ny):
+            out[pc, py, pz] = both[py * rows : (py + 1) * rows]
+        return carry
+
+    lax.fori_loop(0, nc * nz, fold, 0)
+    sends = []
+    for i, (sy, sc) in enumerate(others(ny, nc)):
+        py, pc = lax.rem(y + sy, ny), lax.rem(c + sc, nc)
+        sends.append(remote(out.at[pc, py], came.at[i], ys.at[i], yr.at[i], {"y": py, "core": pc}))
+    for copy in sends:
+        copy.start()
+    for copy in sends:
+        copy.wait_recv()
+
+    def settle(pz, carry):
+        total = out[c, y, pz].astype(F32)
+        for i in range(len(sends)):
+            total = total + came[i, pz].astype(F32)
+        cos, sin = rope_lanes(tab[pz, c])
+        first = lanes(total.shape) < 64
+        total = jnp.where(first, total * cos - swap_halves(total) * sin, total)
+        dqkv[pz, c, :, qcols : qcols + 128] = total.astype(BF)
+        dqkv[pz, 1 - c, :, qcols : qcols + 128] = jnp.zeros((rows, 128), BF)
+        return carry
+
+    lax.fori_loop(0, nz, settle, 0)
+
+    def output(i, carry):
+        pz, n = i // 4, lax.rem(i, 4)
+        at = pl.ds(pl.multiple_of(n * (width // 4), width // 4), width // 4)
+        res = nt(dqkv[pz].reshape(nc * rows, qcols + 128), w[at, : qcols + 128])
+        part[pz, :, :, at] = res.astype(BF).reshape(nc, rows, width // 4)
+        return carry
+
+    lax.fori_loop(0, nz * 4, output, 0)
+    for copy in sends:
+        copy.wait_send()
+    swap.arrived()
+    swap.finish()
+
+
+def attend_back_call(dims, dag, w, tab, q, kk, vv, stat, mlp_sum):
+    nx, nc, nz, ny = dims
+    rows, width = dag.shape[2:]
+    qcols = q.shape[-1]
+    keys = nz * ny * rows
+    members = nz * nc - 1
+    near = ny * nc - 1
+    own, cols = mlp_sum.shape[2:]
+    return call(
+        functools.partial(attend_back_kernel, dims),
+        (dag, w, tab, q, kk, vv, stat, mlp_sum),
+        (VM, VM, VM, VM, VM, VM, VM, pl.ANY),
+        [
+            ((nz, nc, rows, qcols + 128), BF),
+            ((nz, nc, rows, width), BF),
+            ((nz, nc, own, cols), BF),
+        ],
+        (VM, VM, pl.ANY),
+        [
+            VM((nz, nc, rows, qcols), BF),
+            VM((nc, 128, keys), BF),
+            VM((nc, keys, 128), F32),
+            VM((nc, keys, 128), F32),
+            VM((nc, ny, nz, rows, 128), BF),
+            VM((near, nz, rows, 128), BF),
+        ]
+        + [DMA((members,))] * 2
+        + [DMA((near,))] * 2
+        + [DMA((1,))],
+        6,
     )
 
 
@@ -575,9 +860,6 @@
     ff = w_gate.shape[1]
     piece = w_down.shape[0]
     ffcols = piece * nx * ny
-    y_at = lax.axis_index("y")
-    core_at = lax.axis_index("core")
-    scale = HEAD_DIM ** (-0.5)
 
     gain_a = attn_gain.astype(F32)[:, None]
     gain_m = mlp_gain.astype(F32)[:, None]
@@ -605,7 +887,6 @@
         axis=-1,
     )
     mlp_blocks = jnp.concatenate([by_ff(scaled(w_gate, gain_m)), by_ff(scaled(w_up, gain_m))], axis=-1)
-    mlp_t = team_exchange(mlp_blocks).reshape(nz, nc, own, 2 * ffcols).transpose(1, 0, 2, 3)
     xf = tokens.astype(F32)
     inv1 = lax.rsqrt(jnp.mean(xf * xf, axis=-1, keepdims=True) + EPSILON)
     n1 = xf * inv1
@@ -623,52 +904,11 @@
     n1g, tab, w_attn = first_call(
         dims, n1.astype(BF), table, attn_blocks.reshape(nz, nc, own, attn_blocks.shape[-1])
     )
-    n1g = n1g.reshape(team * rows, width)
-    tab = tab.reshape(team * rows, table.shape[1])
     w_attn = w_attn.reshape(width, attn_blocks.shape[-1])
-    w_qkv = w_attn[:, : qcols + 2 * HEAD_DIM]
-    w_out_t = w_attn[:, qcols + 2 * HEAD_DIM :]
-    cos_t = jnp.concatenate([tab[:, :half], tab[:, :half]], axis=-1)
-    sin_t = jnp.concatenate([tab[:, half : 2 * half], tab[:, half : 2 * half]], axis=-1)
-    starts = tab[:, 2 * half].astype(jnp.int32).reshape(nz, nc, rows)
-
-    qkv = dot_plain(n1g, w_qkv)
     total = team * rows
-    q = rope_apply(
-        qkv[:, :qcols].reshape(total, heads, HEAD_DIM), cos_t[:, None], sin_t[:, None]
-    ).astype(BF)
-    k = rope_apply(qkv[:, qcols : qcols + HEAD_DIM], cos_t, sin_t).astype(BF)
-    v = qkv[:, qcols + HEAD_DIM :].astype(BF)
-
-    kv_own = jnp.concatenate([k, v], axis=-1).reshape(nz, nc, rows, 2 * HEAD_DIM)
-    kv_all = lax.all_gather(kv_own, "y", axis=0).transpose(2, 1, 0, 3, 4)
-    kv_all = kv_all.reshape(nc, nz * ny * rows, 2 * HEAD_DIM)
-    k_all, v_all = kv_all[..., :HEAD_DIM], kv_all[..., HEAD_DIM:]
-    qh = q.reshape(nz, nc, rows, heads, HEAD_DIM).transpose(0, 1, 3, 2, 4)
-
-    def block_scores(z):
-        keys = (z + 1) * ny * rows
-        s = jnp.einsum("chrd,ckd->chrk", qh[z], k_all[:, :keys], preferred_element_type=F32) * scale
-        row_at = (z * ny + y_at) * rows + jnp.arange(rows, dtype=jnp.int32)
-        cols = jnp.arange(keys, dtype=jnp.int32)
-        allowed = (cols[None, None, :] >= starts[z][:, :, None]) & (
-            cols[None, None, :] <= row_at[None, :, None]
-        )
-        s = jnp.where(allowed[:, None], s, MASKED)
-        top = jnp.max(s, axis=-1, keepdims=True)
-        e = jnp.exp(s - top)
-        return e / jnp.sum(e, axis=-1, keepdims=True), keys
-
-    contexts = []
-    for z in range(nz):
-        p, keys = block_scores(z)
-        contexts.append(
-            jnp.einsum("chrk,ckd->chrd", p.astype(BF), v_all[:, :keys], preferred_element_type=F32)
-        )
-    context = jnp.stack(contexts)
-    ob = context.transpose(0, 1, 3, 2, 4).reshape(total, qcols).astype(BF)
-
-    part = dot_right_t(ob, w_out_t).astype(BF).reshape(nz, nc, rows, width)
+    q, kk, vv, stat, ob, part, mlp_t = attend_call(
+        dims, n1g, w_attn, tab, mlp_blocks.reshape(nz, nc, own, 2 * ffcols)
+    )
     mid_f, n2g, cotg, w_mlp, w_dn = middle_call(dims, part, tokens, cotangent, mlp_t, w_down)
     n2g = n2g.reshape(total, width)
     cotg = cotg.reshape(total, width)
@@ -690,51 +930,18 @@
     dx2, dag, output, gain_m_part, mlp_came, down_came = back_call(
         dims, dn2, mlp_out, mid_f, cotangent, mlp_part, down_part.reshape(nx, ny, piece, width)
     )
-    dag = dag.reshape(total, width)
     gain_m_part = gain_m_part.sum(0)
-    out_part = dot_left_t(dag, ob)
-    dob = dot_plain(dag, w_out_t).astype(BF)
-
-    doh = dob.reshape(nz, nc, rows, heads, HEAD_DIM).transpose(0, 1, 3, 2, 4)
-    delta = jnp.sum(doh.astype(F32) * context, axis=-1)
-    dqs = []
-    dk = jnp.zeros((nc, nz * ny * rows, HEAD_DIM), F32)
-    dv = jnp.zeros((nc, nz * ny * rows, HEAD_DIM), F32)
-    for z in range(nz):
-        p, keys = block_scores(z)
-        dv = dv.at[:, :keys].add(
-            jnp.einsum("chrk,chrd->ckd", p.astype(BF), doh[z], preferred_element_type=F32)
-        )
-        dp = jnp.einsum("chrd,ckd->chrk", doh[z], v_all[:, :keys], preferred_element_type=F32)
-        ds = (p * (dp - delta[z][..., None])).astype(BF)
-        dqs.append(
-            jnp.einsum("chrk,ckd->chrd", ds, k_all[:, :keys], preferred_element_type=F32) * scale
-        )
-        dk = dk.at[:, :keys].add(
-            jnp.einsum("chrk,chrd->ckd", ds, qh[z], preferred_element_type=F32) * scale
-        )
-    dq = jnp.stack(dqs).transpose(0, 1, 3, 2, 4).reshape(total, heads, HEAD_DIM)
-    dkv = jnp.concatenate([dk, dv], axis=-1).astype(BF)
-    dkv = dkv.reshape(nc, nz, ny, rows, 2 * HEAD_DIM).transpose(2, 1, 0, 3, 4)
-    dkv = lax.all_to_all(dkv, "y", 0, 0, tiled=False).astype(F32).sum(0)
-    dkv = dkv.reshape(total, 2 * HEAD_DIM)
-    dkv = lax.psum(dkv, "core")
-    dka = rope_reverse(dkv[:, :HEAD_DIM], cos_t, sin_t)
-    dva = dkv[:, HEAD_DIM:]
-    dka = jnp.where(core_at == 0, dka, 0.0)
-    dva = jnp.where(core_at == 1, dva, 0.0)
-    dqa = rope_reverse(dq, cos_t[:, None], sin_t[:, None]).reshape(total, qcols)
-    dqkv = jnp.concatenate([dqa, dka, dva], axis=-1).astype(BF)
-    dn1 = dot_right_t(dqkv, w_qkv).astype(BF).reshape(nz, nc, rows, width)
-    qkv_part = dot_left_t(n1g, dqkv)
+    mlp_sum = jnp.sum(mlp_came.astype(F32), axis=(0, 1)).astype(BF).transpose(1, 0, 2, 3)
+    dqkv, dn1, mlp_g = attend_back_call(dims, dag, w_attn, tab, q, kk, vv, stat, mlp_sum)
+    out_part = dot_left_t(dag.reshape(total, width), ob.reshape(total, qcols))
+    qkv_part = dot_left_t(n1g.reshape(total, width), dqkv.reshape(total, qcols + 128))
     attn_part = jnp.concatenate([qkv_part, out_part], axis=-1).astype(BF)
     attn_part = attn_part.reshape(nx, nc, nz, ny, own, attn_part.shape[-1])
     input_grad, gain_a_part, attn_g = last_call(dims, dn1, tokens, dx2, attn_part)
     gain_a_part = gain_a_part.sum(0)
 
     attn_g = attn_g.reshape(team, own, attn_g.shape[-1]).astype(F32)
-    mlp_g = jnp.sum(mlp_came.astype(F32), axis=(0, 1)).astype(BF).transpose(1, 0, 2, 3)
-    mlp_g = team_exchange(mlp_g.reshape(team, own, 2 * ffcols)).astype(F32)
+    mlp_g = mlp_g.reshape(team, own, 2 * ffcols).astype(F32)
     grad_down = jnp.sum(down_came.astype(F32), axis=(0, 1))
     grad_query = attn_g[:, :, :qcols].transpose(1, 0, 2).reshape(own, HEADS * HEAD_DIM) * gain_a
     kv_g = attn_g[:, :, qcols : qcols + 2 * HEAD_DIM].reshape(KV_HEADS, kv_rep, own, 2 * HEAD_DIM).sum(1)

time: 769 us -> 622 us (0.81)
  Pallas kernels: 413 us -> 483 us
  local copies, waits for them, and re-layouts: 102 us -> 44.8 us
  matrix products: 101 us -> 51.1 us
  waiting for transfers between devices: 46.8 us -> 0.01 us
  other arithmetic: 48.3 us -> 29.6 us
  starting transfers between devices: 21.5 us -> 5.64 us
  between operations: 15.9 us -> 1.41 us
  blocking collectives: 8.62 us -> 0 us
    pallas_call x4 -> x6, Pallas kernels: 413 us -> 483 us  [call(): pl.pallas_call(kernel, out_shape=[jax.ShapeDtypeStruct(s, t) for s, t in...]
    all_to_all x3 -> x0, waiting for transfers between devices: 23.4 us -> none  [the longest x2 23.4 us: team_exchange(): return lax.all_to_all(blocks, TEAM, 0, 0, tiled=False)]
    psum x1 -> x0, waiting for transfers between devices: 23.4 us -> none  [shards(): dkv = lax.psum(dkv, 'core')]
    dot_general x20 -> x0, matrix products: 16.1 us -> none  [the longest x4 3.98 us: shards(): jnp.einsum('chrd,ckd->chrk', doh[z], v_all[:, :keys], preferred_element_t...]
    all_to_all x3 -> x0, starting transfers between devices: 15.9 us -> none  [the longest x2 11.5 us: team_exchange(): return lax.all_to_all(blocks, TEAM, 0, 0, tiled=False)]
    reshape x11 -> x0, local copies, waits for them, and re-layouts: 15.8 us -> none  [the longest x3 5.26 us: shards(): dq = jnp.stack(dqs).transpose(0, 1, 3, 2, 4).reshape(total, heads, HEAD_DIM)]
    dot_general x2 -> x0, local copies, waits for them, and re-layouts: 12.9 us -> none  [dot_left_t(): lax.dot_general(a, b, (((0,), (0,)), ((), ())), preferred_element_type=F32)]
    dot_general x4 -> x2, matrix products: 26.7 us -> 14.4 us  [dot_right_t(): lax.dot_general(a, b, (((1,), (1,)), ((), ())), preferred_element_type=F32)]
  transfers between devices with their start and end apart: 5 -> 1, of which waited for: 2 -> 0; matrix products, arithmetic and copies ran while one was open for 12% -> 6% of each run, Pallas kernels for 11% -> 0%
where the time goes in v3:
time: 622 us; the launch traced here: 616 us
  Pallas kernels  483 us (78%)
  matrix products  51.1 us (8%)
  local copies, waits for them, and re-layouts  44.8 us (7%)
  other arithmetic  29.6 us (5%)
    pallas_call x6, Pallas kernels, call(): pl.pallas_call(kernel, out_shape=[jax.ShapeDtypeStruct(s, t) for s, t in...  483 us
    dot_general x4, matrix products, dot_left_t(): lax.dot_general(a, b, (((0,), (0,)), ((), ())), preferred_element_type=F32)  20.1 us
    dot_general x3, matrix products, dot_plain(): return jnp.dot(a, b, preferred_element_type=F32)  16.7 us
    reshape x4, local copies, waits for them, and re-layouts, from_ff(): g = g.reshape(nz, nc, own, nx, ny, piece).transpose(2, 3, 1, 0, 4, 5)  14.6 us
    dot_general x2, matrix products, dot_right_t(): lax.dot_general(a, b, (((1,), (1,)), ((), ())), preferred_element_type=F32)  14.4 us
  transfers between devices with their start and end apart: 1, of which 0 were waited for; matrix products, arithmetic and copies ran while one was open for 6% of the time, Pallas kernels for 0%

profile of v3, /device:TPU:31, one launch (start us, length us, event | category | flops | bytes accessed | tf_op | source)
XLA Modules:
  0.0 615.9 jit_solution(16967114836270217417)
XLA Ops:
  0.7 0.8 convert_element_type.93
  1.4 0.9 multiply_convert_fusion.7
  2.6 1.1 multiply_convert_fusion.5
  3.7 1.0 copy.102
  4.7 0.7 convert_element_type.90
  5.4 0.7 convert_element_type.91
  6.0 1.2 fusion.5
  7.3 0.9 fusion.6.n1
  8.2 1.2 multiply_convert_fusion.4
  9.4 2.1 reshape.152
  11.5 0.7 copy.101
  12.2 0.9 concatenate.36
  13.1 4.9 reshape.153
  18.0 0.7 copy.100
  18.7 0.9 concatenate.37
  19.6 0.3 multiply_cosine_fusion
  20.0 1.5 pad_maximum_fusion.4.mlp_blocks
  21.6 0.7 pad_maximum_fusion.6.table
  22.4 1.0 pad_maximum_fusion.5.blocks
  23.4 60.3 %shard_map.212 = (bf16[4,2,128,2048]{3,2,1,0:T(8,128)(2,1)}, f32[4,2,128,128]{3,2,1,0:T(8,128)}, bf16[2,2,4,2,64,640]{5,4,3,2,1,0:T(8,128)(2,1)}) custom-call(bf16[128,2048]{1,0:T(8,128)(2,1)} %fusion.6.n1, f32[128,128]{1,0:T(8,128)} %pad_maximum_fusion.6.table, bf16[4,2,64,640]{3,2,1,0:T(8,128)(2,1)} %pad_maximum_fusion.5.blocks), custom_call_target="tpu_custom_call" | custom-call | tf_op jit(solution)/shard_map/pallas_call | solution.py:270
  83.7 40.5 %shard_map.213 = (bf16[4,2,128,256]{3,2,1,0:T(8,128)(2,1)}, bf16[2,1024,128]{2,1,0:T(8,128)(2,1)}, bf16[2,1024,128]{2,1,0:T(8,128)(2,1)}, f32[4,2,8,256]{3,2,1,0...) custom-call(bf16[4,2,128,2048]{3,2,1,0:T(8,128)(2,1)} %get-tuple-ele, ...), custom_call_target="tpu_custom_call" | custom-call | tf_op jit(solution)/shard_map/pallas_call | solution.py:270
  124.3 131.6 %shard_map.214 = (f32[128,2048]{1,0:T(8,128)}, bf16[4,2,128,2048]{3,2,1,0:T(8,128)(2,1)}, bf16[4,2,128,2048]{3,2,1,0:T(8,128)(2,1)}, bf16[2,2,4,2,64,1408]{5,4,3,2,1,0:T(8,128)(2,1)}, bf16[2,2,176,2048]{3,2,1,0:T(8,128)(2,1)}) custom-call(bf16[4,2,128,2048]{3,2,1,0:T(8,128)(2,1)} %get-tuple-element.41.part, bf16[128,2048]{1,0:T(8,128)(2,1)} %tokens.3, ...), custom_call_target="tpu_custom_call" | custom-call | tf_op jit(solution)/shard_map/pallas_call | solution.py:270
  255.9 6.0 fusion.10
  261.9 3.3 fusion
  265.2 8.3 %multiply_convert_fusion = (bf16[1024,704]{0,1:T(8,128)(2,1)}, bf16[1024,704]{0,1:T(8,128)(2,1)}, bf16[1024,704]{0,1:T(8,128)(2,1)}) fusion(f32[1024,704]{0,1:T(8,128)S(1)} %fusion, f32[1024,704]{0,1:T(8,128)S(1)} %fusion.10, bf16[1024,2048]{1,0:T(8,128)(2,1)S(1)} %bitcast.124, bf16[2048,1408]{1,0:T(8,128)(2,1)S(1)} %bitcast.121), kind=kOutput, calls=%fused_computation.11 | convolution fusion | flops 2964324352 | bytes 17432576 | tf_op jit(solution)/shard_map/dot_general | solution.py:24
  273.6 6.1 convolution_convert_fusion.3
  279.6 5.1 convolution_convert_fusion.1
  284.7 9.0 %convolution_convert_fusion = bf16[2048,1408]{1,0:T(8,128)(2,1)} fusion(bf16[1024,2048]{1,0:T(8,128)(2,1)S(1)} %bitcast.125, bf16[1024,704]{0,1:T(8,128)(2,1)S(1)} %copy-done.22, bf16[1024,704]{0,1:T(8,128)(2,1)S(1)} %copy-done.21), kind=kOutput, calls=%fused_computation | convolution fusion | flops 5914230784 | bytes 12845056 | tf_op jit(solution)/shard_map/dot_general | solution.py:32
  293.7 8.4 %convolution_convert_fusion.2 = bf16[1024,2048]{1,0:T(8,128)(2,1)} fusion(bf16[2048,1408]{1,0:T(8,128)(2,1)S(1)} %bitcast.122, bf16[1024,704]{0,1:T(8,128)(2,1)S(1)} %copy-done.22, bf16[1024,704]{0,1:T(8,128)(2,1)S(1)} %copy-done.21), kind=kOutput, calls=%fused_computation.3 | convolution fusion | flops 5913444352 | bytes 12845056 | tf_op jit(solution)/shard_map/dot_general | solution.py:28
  302.0 123.1 %shard_map.215 = (f32[128,2048]{1,0:T(8,128)}, bf16[4,2,128,2048]{3,2,1,0:T(8,128)(2,1)}, bf16[128,2048]{1,0:T(8,128)(2,1)}, f32[8,2048]{1,0:T(8,128)}, bf16[2,2...) custom-call(bf16[4,2,128,2048]{3,2,1,0:T(8,128)(2,1)} %bitcast.108, ...), custom_call_target="tpu_custom_call" | custom-call | tf_op jit(solution)/shard_map/pallas_call | solution.py:270
  425.1 3.7 reduce_sum.67
  428.9 1.2 copy.99
  430.1 54.7 %shard_map.216 = (bf16[4,2,128,384]{3,2,1,0:T(8,128)(2,1)}, bf16[4,2,128,2048]{3,2,1,0:T(8,128)(2,1)}, bf16[4,2,64,1408]{3,2,1,0:T(8,128)(2,1)}) custom-call(bf16[4,2,128,2048]{3,2,1,0:T(8,128)(2,1)} %get-tuple-element.49.dag, bf16[2048,640]{1,0:T(8,128)(2,1)} %bitcast.100, f32[4,2,128,128]{3,2,1,0:T(8,128)} %get-tuple-element.40.tab, ...), custom_call_target="tpu_custom_call" | custom-call | tf_op jit(solution)/shard_map/pallas_call | solution.py:270
  484.8 3.7 bitcast_convert_fusion
  488.5 1.4 fusion.4
  489.9 1.9 pad_maximum_fusion.1.grad_attn
  491.8 73.1 %shard_map.217 = (f32[128,2048]{1,0:T(8,128)}, f32[8,2048]{1,0:T(8,128)}, bf16[4,2,64,640]{3,2,1,0:T(8,128)(2,1)}) custom-call(bf16[4,2,128,2048]{3,2,1,0:T(8,128)(2,1)} %get-tuple-element.55.part, bf16[128,2048]{1,0:T(8,128)(2,1)} %tokens.3, f32[128,2048]{1,0:T(8,128)} %get-tuple-element.56.dx2, bf16[2,2,4,2,64,640]{5,4,3,2,1,0:T(8,128)(2,1)} %pad_maximum_fusion.1.grad_attn), custom_call_target="tpu_custom_call" | custom-call | tf_op jit(solution)/shard_map/pallas_call | solution.py:270
  564.9 1.0 reduce_sum.69
  566.1 0.7 reshape.175
  566.8 5.6 all-to-all-start
  572.4 1.2 bitcast_convert_fusion.2
  573.6 0.7 bitcast_reduce_fusion
  574.3 1.1 slice_bitcast_fusion
  575.4 0.3 bitcast_convert_fusion.1
  575.7 2.2 fusion.9
  577.9 4.7 reshape.167
  582.6 2.6 copy.98
  585.2 3.6 reshape.168
  588.8 4.7 reshape.169
  593.5 2.6 copy.97
  596.1 3.8 reshape.170
  600.1 0.1 reshape.164
  600.3 0.1 reshape.165
  600.5 1.1 copy.86
  601.6 1.6 broadcast_multiply_fusion.2
  603.1 3.6 convert_reduce_fusion
  606.7 1.9 broadcast_multiply_fusion
  608.7 0.7 broadcast_multiply_fusion.3
  609.4 0.8 copy.87
  610.2 0.5 broadcast.33
  610.8 0.7 reduce.1
  611.6 1.2 bitcast_divide_fusion
  612.8 1.9 copy.108
  614.7 1.0 copy.109
  (67 shorter events, 1.1 us)
Async XLA Ops:
  0.6 6.6 %copy-start = (bf16[128,2048]{1,0:T(8,128)(2,1)S(1)}, bf16[128,2048]{1,0:T(8,128)(2,1)}, u32[]{:S(2)}) copy-start(bf16[128,2048]{1,0:T(8,128)(2,1)} %tokens.3) | copy-start | bytes 1572868
  0.7 7.6 %copy-start.14 = (bf16[64]{0:T(256)(128)(2,1)S(1)}, bf16[64]{0:T(256)(128)(2,1)}, u32[]{:S(2)}) copy-start(bf16[64]{0:T(256)(128)(2,1)} %param.25) | copy-start | bytes 388
  0.7 7.5 %copy-start.7 = (bf16[64,5632]{1,0:T(8,128)(2,1)S(1)}, bf16[64,5632]{1,0:T(8,128)(2,1)}, u32[]{:S(2)}) copy-start(bf16[64,5632]{1,0:T(8,128)(2,1)} %param.22) | copy-start | bytes 2162692
  1.4 8.0 %copy-start.10 = (f32[64]{0:T(128)}, f32[64]{0:T(128)S(1)}, u32[]{:S(2)}) copy-start(f32[64]{0:T(128)S(1)} %convert_element_type.93) | copy-start | bytes 772
  2.5 5.7 copy-start.8
  8.2 4.0 copy-start.12
  255.9 6.0 copy-start.15
  255.9 6.0 copy-start.16
  265.2 8.3 %copy-start.17 = (bf16[4,2,128,2048]{3,2,1,0:T(8,128)(2,1)S(1)}, bf16[4,2,128,2048]{3,2,1,0:T(8,128)(2,1)}, u32[]{:S(2)}) copy-start(bf16[4,2,128,2048]{3,2,1,0:T(8,128)(2,1)} %get-tuple-element.43) | copy-start | bytes 12582916
  273.5 6.1 copy-start.18
  273.5 6.1 copy-start.20
  279.6 5.1 copy-start.21
  279.6 5.1 copy-start.22
  430.1 54.7 %copy-start.1 = (bf16[4,2,128,2048]{3,2,1,0:T(8,128)(2,1)S(1)}, bf16[4,2,128,2048]{3,2,1,0:T(8,128)(2,1)}, u32[]{:S(2)}) copy-start(bf16[4,2,128,2048]{3,2,1,0:T(8,128)(2,1)} %get-tuple-element.38.n1g) | copy-start | bytes 12582916
  484.8 3.7 copy-start.2
  484.8 3.7 copy-start.19
  491.8 74.2 %copy-start.9 = (f32[8,2048]{1,0:T(8,128)S(1)}, f32[8,2048]{1,0:T(8,128)}, u32[]{:S(2)}) copy-start(f32[8,2048]{1,0:T(8,128)} %get-tuple-element.62) | copy-start | bytes 196612
  564.9 10.5 %copy-start.4 = (bf16[4,2,64,1408]{3,2,1,0:T(8,128)(2,1)S(1)}, bf16[4,2,64,1408]{3,2,1,0:T(8,128)(2,1)}, u32[]{:S(2)}) copy-start(bf16[4,2,64,1408]{3,2,1,0:T(8,128)(2,1)} %get-tuple-element.63) | copy-start | bytes 4325380
  566.8 43.4 %all-to-all-start = ((f32[32,1,128]{2,1,0:T(1,128)}), f32[32,1,128]{2,1,0:T(1,128)S(1)}, u32[]{:S(2)}, u32[]{:S(2)}) async-start(f32[32,1,128]{2,1,0:T(1,128)} %reshape.175), calls=%async_computation | async-start | bytes 32768 | tf_op jit(solution)/shard_map/all_to_all | solution.py:959
  596.1 3.8 copy-start.5
  601.6 5.2 copy-start.13
  606.7 1.9 copy-start.11
  606.7 2.7 copy-start.3
  608.7 6.0 copy-start.6

commit v4 on v3

--- a/solution.py
+++ b/solution.py
@@ -36,6 +36,8 @@
 VM = pltpu.VMEM
 DMA = pltpu.SemaphoreType.DMA
 ROWS = 16
+PARTS = 2
+WINDOW = 2
 
 
 def place():
@@ -79,97 +81,79 @@
     )
 
 
+def piece_of(part, rows):
+    return pl.ds(part * (rows // PARTS), rows // PARTS)
+
+
 class Gather:
-    SEMS = [DMA((4, 4)), DMA((2, 4))]
+    SEMS = [DMA((3, 4, PARTS)), DMA((2, 4, PARTS)), DMA((PARTS,))]
 
     def __init__(self, own, full, send, recv, local):
-        self.own, self.full, self.send, self.recv = own, full, send, recv
+        self.own, self.full, self.send, self.recv, self.local = own, full, send, recv, local
         self.x, self.c, self.z, self.y = place()
-        self.nz = full.shape[0]
-        self.local = pltpu.make_async_copy(own, full.at[self.z, self.c], local)
-
-    def copy(self, at, kind):
-        slot = self.full.at[at, self.c]
+        self.nz, _, self.rows = full.shape[:3]
+
+    def copy(self, at, kind, part, mine=False):
+        rows = piece_of(part, self.rows)
+        slot = self.full.at[at, self.c, rows]
         device = ({"z": self.z + 1}, {"z": self.z - 1}, {"core": 1 - self.c})[kind]
         return remote(
-            slot, slot, self.send.at[kind, at], self.recv.at[0 if kind < 2 else 1, at], device
+            self.own.at[rows] if mine else slot, slot, self.send.at[kind, at, part],
+            self.recv.at[0 if kind < 2 else 1, at, part], device,
         )
 
-    def start(self):
-        self.local.start()
-        self.local.wait()
-        pl.when(self.z < self.nz - 1)(lambda: self.copy(self.z, 0).start())
-        pl.when(self.z > 0)(lambda: self.copy(self.z, 1).start())
-        self.copy(self.z, 2).start()
-
-    def hop(self, far):
-        @pl.when(self.z - far >= 0)
-        def _():
-            at = self.z - far
-            self.copy(at, 0).wait_recv()
-            pl.when(self.z < self.nz - 1)(lambda: self.copy(at, 0).start())
-            self.copy(at, 2).start()
-
-        @pl.when(self.z + far < self.nz)
-        def _():
-            at = self.z + far
-            self.copy(at, 1).wait_recv()
-            pl.when(self.z > 0)(lambda: self.copy(at, 1).start())
-            self.copy(at, 2).start()
+    def keep(self, part):
+        rows = piece_of(part, self.rows)
+        return pltpu.make_async_copy(self.own.at[rows], self.full.at[self.z, self.c, rows], self.local.at[part])
+
+    def begin(self, part):
+        self.keep(part).start()
+        self.copy(self.z, 2, part, True).start()
 
     def finish(self):
-        for at in range(self.nz):
-            pl.when((at <= self.z) & (self.z < self.nz - 1))(lambda at=at: self.copy(at, 0).wait_send())
-            pl.when((at >= self.z) & (self.z > 0))(lambda at=at: self.copy(at, 1).wait_send())
-            self.copy(at, 2).wait_send()
-            self.copy(at, 2).wait_recv()
+        for part in range(PARTS):
+            self.keep(part).wait()
+            for at in range(self.nz):
+                self.copy(at, 2, part).wait_send()
+                self.copy(at, 2, part).wait_recv()
 
 
 class Reduce:
-    SEMS = [DMA((3, 4)), DMA((3, 4))]
+    SEMS = [DMA((2, 4, PARTS)), DMA((2, 4, PARTS)), DMA((4,)), DMA((4,))]
 
     @staticmethod
     def buffers(nz, rows, width):
         return [VM((nz, rows, width), BF), VM((2, nz, rows, width), BF)]
 
-    def __init__(self, part, held, came, send, recv):
+    def __init__(self, part, held, came, send, recv, across_send, across_recv):
         self.part, self.held, self.came, self.send, self.recv = part, held, came, send, recv
+        self.across_send, self.across_recv = across_send, across_recv
         self.x, self.c, self.z, self.y = place()
         self.nz, _, self.rows, self.width = part.shape
 
     def across(self, to):
         return remote(
-            self.part.at[to, 1 - self.c], self.held.at[to], self.send.at[2, to], self.recv.at[2, to],
+            self.part.at[to, 1 - self.c], self.held.at[to], self.across_send.at[to], self.across_recv.at[to],
             {"core": 1 - self.c},
         )
 
-    def along(self, to, way):
+    def along(self, to, way, part):
         device = ({"z": self.z + 1}, {"z": self.z - 1})[way]
+        rows = piece_of(part, self.rows)
         return remote(
-            self.held.at[to], self.came.at[way, to], self.send.at[way, to], self.recv.at[way, to], device
+            self.held.at[to, rows], self.came.at[way, to, rows], self.send.at[way, to, part],
+            self.recv.at[way, to, part], device,
         )
 
-    def order(self):
-        return [a for k in range(self.nz) for a in (self.nz - 1 - k, k)][: self.nz]
-
     def start(self):
-        for to in self.order():
+        for to in [a for k in range(self.nz) for a in (self.nz - 1 - k, k)][: self.nz]:
             self.across(to).start()
-        zeros = jnp.zeros((ROWS, self.width), BF)
-        for way, end in ((0, 0), (1, self.nz - 1)):
-
-            @pl.when(self.z == end)
-            def _(way=way):
-                def clear(i, carry):
-                    for to in range(self.nz):
-                        self.came[way, to, pl.ds(pl.multiple_of(i * ROWS, ROWS), ROWS), :] = zeros
-                    return carry
-
-                lax.fori_loop(0, self.rows // ROWS, clear, 0)
-
-    def add(self, to, ways, out=None):
+
+    def add(self, to, ways, part, out=None):
+        size = self.rows // PARTS
+
         def body(i, carry):
-            at = pl.ds(pl.multiple_of(i * ROWS, ROWS), ROWS)
+            at = pl.ds(pl.multiple_of(part * size + i * ROWS, ROWS), ROWS)
             total = self.part[to, self.c, at, :].astype(F32) + self.held[to, at, :].astype(F32)
             for way in ways:
                 total = total + self.came[way, to, at, :].astype(F32)
@@ -179,31 +163,108 @@
                 out(at, total)
             return carry
 
-        lax.fori_loop(0, self.rows // ROWS, body, 0)
-
-    def hop(self, k):
-        for way, to in ((0, self.nz - 1 - k), (1, k)):
-            active = (self.z < to) if way == 0 else (self.z > to)
-            first = (self.z == 0) if way == 0 else (self.z == self.nz - 1)
-
-            @pl.when(active)
-            def _(way=way, to=to, first=first):
-                self.across(to).wait_recv()
-                pl.when(jnp.logical_not(first))(lambda: self.along(to, way).wait_recv())
-                self.add(to, (way,))
-                self.along(to, way).start()
-
-    def last(self, out):
-        self.across(self.z).wait_recv()
-        pl.when(self.z > 0)(lambda: self.along(self.z, 0).wait_recv())
-        pl.when(self.z < self.nz - 1)(lambda: self.along(self.z, 1).wait_recv())
-        self.add(self.z, (0, 1), out)
+        lax.fori_loop(0, size // ROWS, body, 0)
+
+    def last(self, part, out):
+        if part == 0:
+            self.across(self.z).wait_recv()
+        for at in range(self.nz):
+
+            @pl.when(self.z == at)
+            def _(at=at):
+                ways = ([0] if at > 0 else []) + ([1] if at < self.nz - 1 else [])
+                for way in ways:
+                    self.along(at, way, part).wait_recv()
+                self.add(at, ways, part, out)
 
     def finish(self):
         for to in range(self.nz):
             self.across(to).wait_send()
-            pl.when(self.z < to)(lambda to=to: self.along(to, 0).wait_send())
-            pl.when(self.z > to)(lambda to=to: self.along(to, 1).wait_send())
+
+
+def plan(nz, reduces, gathers):
+    last = nz - 1
+    rows = []
+    for e in range(nz):
+        sums = [("R", last - k) for k in range(last) if last - k > e]
+        blocks = [("G", e - k) for k in range(e + 1)]
+        if reduces and gathers:
+            if e == last:
+                rows.append([None] + blocks[1:-1] + [None] + blocks[-1:])
+            else:
+                woven = blocks[:-1] + sums[:1] + blocks[-1:] + sums[1:]
+                rows.append(woven)
+        elif reduces:
+            rows.append([None] * e + sums)
+        else:
+            rows.append(blocks if e < last else [None] + blocks[1:])
+    return rows
+
+
+def flow(reduce, gather, before=None, work=()):
+    work = list(work)
+    any_one = reduce or gather
+    nz, z = any_one.nz, any_one.z
+    table = plan(nz, reduce is not None, gather is not None)
+    pending = {(way, e): [] for way in (0, 1) for e in range(nz)}
+
+    def pace(key, make):
+        queue = pending[key]
+        if len(queue) >= WINDOW:
+            queue.pop(0)().wait_send()
+        make().start()
+        queue.append(make)
+
+    def step(way, e, kind, place_at, part):
+        block = place_at if way == 0 else nz - 1 - place_at
+        if kind == "R":
+            if part == 0:
+                reduce.across(block).wait_recv()
+            if e > 0:
+                reduce.along(block, way, part).wait_recv()
+            reduce.add(block, (way,) if e > 0 else (), part)
+            pace((way, e), functools.partial(reduce.along, block, way, part))
+        else:
+            mine = place_at == e
+            if not mine:
+                gather.copy(block, way, part).wait_recv()
+            if e < nz - 1:
+                pace((way, e), functools.partial(gather.copy, block, way, part, mine))
+            if not mine:
+                gather.copy(block, 2, part).start()
+
+    for t in range(max(len(row) for row in table)):
+        for part in range(PARTS):
+            if t == 0 and before is not None:
+                before(part)
+            if t == 0 and gather is not None:
+                gather.begin(part)
+            for way in (0, 1):
+                for e in range(nz):
+                    op = table[e][t] if t < len(table[e]) else None
+                    if op is not None:
+                        pl.when(z == (e if way == 0 else nz - 1 - e))(
+                            functools.partial(step, way, e, op[0], op[1], part)
+                        )
+            if work:
+                work.pop(0)()
+    for item in work:
+        item()
+
+    def finish():
+        for (way, e), queue in pending.items():
+            if queue:
+
+                @pl.when(z == (e if way == 0 else nz - 1 - e))
+                def _(queue=queue):
+                    for make in queue:
+                        make().wait_send()
+
+        for one in (reduce, gather):
+            if one is not None:
+                one.finish()
+
+    return finish
 
 
 class Spread:
@@ -279,72 +340,148 @@
     )(*operands)
 
 
-def first_kernel(dims, n1, table, blocks, n1g, tabg, w_attn, gs, gr, ts, tr, ss, sr, ds, dr, local):
+def lanes(shape):
+    return lax.broadcasted_iota(jnp.int32, shape, len(shape) - 1)
+
+
+def by_rows(count, body):
+    if count % ROWS or count == ROWS:
+        body(slice(0, count))
+    else:
+
+        def step(i, carry):
+            body(pl.ds(pl.multiple_of(i * ROWS, ROWS), ROWS))
+            return carry
+
+        lax.fori_loop(0, count // ROWS, step, 0)
+
+
+def first_kernel(
+    dims, tokens, table, gains, w_query, w_key, w_value, w_out, w_gate, w_up, down,
+    n1g, tabg, w_attn, mlp_blocks, w_dn,
+    n1, blocks, gs, gr, gl, ts, tr, tl, ss, sr, ds, dr, ws, wr, local,
+):
     nx, nc, nz, ny = dims
     x, c, z, y = place()
+    own = w_query.shape[0]
+    qcols = HEADS // (nz * nc) * HEAD_DIM
+    span = w_gate.shape[1] // (nx * nc * nz)
+    dn = Spread(lambda px, py: down, lambda px, py: w_dn.at[px, py], ws, wr, local.at[1], nx, ny)
     greet(*dims)
+
+    def pack(at):
+        gain = gains[at, 0:1]
+        for t in range(nz * nc):
+            cols = slice(t * qcols, (t + 1) * qcols)
+            blocks[t // nc, t % nc, at, :qcols] = (w_query[at, cols].astype(F32) * gain).astype(BF)
+        for pair in range(KV_HEADS // 2):
+            cols = slice(pair * 128, pair * 128 + 128)
+            key, value = w_key[at, cols].astype(F32) * gain, w_value[at, cols].astype(F32) * gain
+            first = lanes(key.shape) < 64
+            both = (
+                jnp.where(first, key, pltpu.roll(value, 64, 1)),
+                jnp.where(first, pltpu.roll(key, 64, 1), value),
+            )
+            for k in range(2):
+                for rep in range(nz * nc // KV_HEADS):
+                    t = (pair * 2 + k) * (nz * nc // KV_HEADS) + rep
+                    blocks[t // nc, t % nc, at, qcols : qcols + 128] = both[k].astype(BF)
+
+    by_rows(own, pack)
+    for t in range(nz * nc):
+        turned = w_out[t * qcols : (t + 1) * qcols, :].astype(F32).T
+        blocks[t // nc, t % nc, :, qcols + 128 :] = turned.astype(BF)
     swap = Swap(blocks, lambda pz, pc: w_attn.at[x, pc, pz, y], ss, sr, local.at[0])
-    rows = Gather(n1, n1g, gs, gr, local.at[1])
-    tabs = Gather(table, tabg, ts, tr, local.at[2])
     swap.start()
-    tabs.start()
-    rows.start()
-    swap.arrived()
-    spread = Spread(
-        lambda px, py: w_attn.at[x, :, :, y], lambda px, py: w_attn.at[px, :, :, py], ds, dr, local.at[3], nx, ny
-    )
-    for copy in spread.copies():
-        copy.start()
-    for far in range(1, nz):
-        tabs.hop(far)
-        rows.hop(far)
-    tabs.finish()
-    rows.finish()
+    dn.start()
+
+    def norm(at):
+        value = tokens[at, :].astype(F32)
+        inverse = lax.rsqrt(jnp.mean(value * value, axis=-1, keepdims=True) + EPSILON)
+        n1[at, :] = (value * inverse).astype(BF)
+
+    by_rows(tokens.shape[0], norm)
+    rows = Gather(n1, n1g, gs, gr, gl)
+    tabs = Gather(table, tabg, ts, tr, tl)
+
+    def spread_copies():
+        for i, step in enumerate(others(nx, ny)):
+            px, py = data_peer(step, nx, ny)
+            slot = w_attn.at[x, :, :, y]
+            yield remote(slot, slot, ds.at[i], dr.at[i], {"x": px, "y": py})
+
+    def spread():
+        swap.arrived()
+        for copy in spread_copies():
+            copy.start()
+
+    def pack_mlp(at):
+        gain = gains[at, 1:2]
+        for k, weight in enumerate((w_gate, w_up)):
+            for t in range(nz * nc):
+                for i in range(nx):
+                    chunk = (i * nc + t % nc) * nz + t // nc
+                    to = (k * nx + i) * span
+                    piece = weight[at, chunk * span : (chunk + 1) * span].astype(F32) * gain
+                    mlp_blocks[t // nc, t % nc, at, to : to + span] = piece.astype(BF)
+
+    end = flow(None, rows, None, [spread])
+    by_rows(own, pack_mlp)
+    end2 = flow(None, tabs)
+    end()
+    end2()
     swap.finish()
-    for copy in spread.copies():
+    for copy in spread_copies():
         copy.wait_recv()
-    spread.finish()
-
-
-def first_call(dims, n1, table, blocks):
-    nx, nc, nz, ny = dims
-    rows, width = n1.shape
-    own, cols = blocks.shape[2:]
+    for copy in spread_copies():
+        copy.wait_send()
+    dn.arrived()
+    dn.finish()
+
+
+def first_call(dims, tokens, table, gains, w_query, w_key, w_value, w_out, w_gate, w_up, down):
+    nx, nc, nz, ny = dims
+    rows, width = tokens.shape
+    own = w_query.shape[0]
+    cols = 2 * HEADS // (nz * nc) * HEAD_DIM + 128
     peers = nx * ny - 1
+    mlp_cols = 2 * w_gate.shape[1] // (nz * nc)
     return call(
         functools.partial(first_kernel, dims),
-        (n1, table, blocks),
-        (VM, VM, pl.ANY),
+        (tokens, table, gains, w_query, w_key, w_value, w_out, w_gate, w_up, down),
+        (VM,) * 9 + (pl.ANY,),
         [
             ((nz, nc, rows, width), BF),
             ((nz, nc) + table.shape, F32),
             ((nx, nc, nz, ny, own, cols), BF),
+            ((nz, nc, own, mlp_cols), BF),
+            ((nx, ny) + down.shape, BF),
         ],
-        (pl.ANY, pl.ANY, pl.ANY),
-        Gather.SEMS * 2 + [DMA((nz * nc - 1,))] * 2 + [DMA((peers,))] * 2 + [DMA((4,))],
+        (pl.ANY, pl.ANY, pl.ANY, VM, pl.ANY),
+        [VM((rows, width), BF), VM((nz, nc, own, cols), BF)]
+        + Gather.SEMS * 2
+        + [DMA((nz * nc - 1,))] * 2
+        + [DMA((peers,))] * 4
+        + [DMA((2,))],
         1,
     )
 
 
 def middle_kernel(
-    dims, part, tokens, cot, mlp_t, down,
-    mid, n2g, cotg, w_mlp, w_dn,
-    held, came, n2, rs, rr, ns, nr, cs, cr, ms, mr, ws, wr, local,
+    dims, part, tokens, cot, mlp_t,
+    mid, n2g, cotg, w_mlp,
+    held, came, n2, rs, rr, rxs, rxr, ns, nr, nl, cs, cr, cl, ms, mr, local,
 ):
     nx, nc, nz, ny = dims
     x, c, z, y = place()
     greet(*dims)
-    reduce = Reduce(part, held, came, rs, rr)
-    cots = Gather(cot, cotg, cs, cr, local.at[0])
-    gu = Spread(lambda px, py: mlp_t, lambda px, py: w_mlp.at[px, :, :, py], ms, mr, local.at[1], nx, ny)
-    dn = Spread(lambda px, py: down, lambda px, py: w_dn.at[px, py], ws, wr, local.at[2], nx, ny)
+    reduce = Reduce(part, held, came, rs, rr, rxs, rxr)
+    cots = Gather(cot, cotg, cs, cr, cl)
+    rows = Gather(n2, n2g, ns, nr, nl)
+    gu = Spread(lambda px, py: mlp_t, lambda px, py: w_mlp.at[px, :, :, py], ms, mr, local.at[0], nx, ny)
     reduce.start()
     gu.start()
-    dn.start()
-    cots.start()
-    for k in range(nz - 1):
-        reduce.hop(k)
-        cots.hop(k + 1)
+    end = flow(reduce, cots)
 
     def settle(at, total):
         value = tokens[at, :].astype(F32) + total
@@ -352,65 +489,55 @@
         inverse = lax.rsqrt(jnp.mean(value * value, axis=-1, keepdims=True) + EPSILON)
         n2[at, :] = (value * inverse).astype(BF)
 
-    reduce.last(settle)
-    rows = Gather(n2, n2g, ns, nr, local.at[3])
-    rows.start()
-    for far in range(1, nz):
-        rows.hop(far)
-    rows.finish()
-    cots.finish()
-    reduce.finish()
+    end2 = flow(None, rows, lambda part: reduce.last(part, settle))
+    end2()
+    end()
     gu.arrived()
-    dn.arrived()
     gu.finish()
-    dn.finish()
-
-
-def middle_call(dims, part, tokens, cot, mlp_t, down):
+
+
+def middle_call(dims, part, tokens, cot, mlp_t):
     nx, nc, nz, ny = dims
     rows, width = tokens.shape
     peers = nx * ny - 1
     return call(
         functools.partial(middle_kernel, dims),
-        (part, tokens, cot, mlp_t, down),
-        (VM, VM, VM, pl.ANY, pl.ANY),
+        (part, tokens, cot, mlp_t),
+        (VM, VM, VM, pl.ANY),
         [
             ((rows, width), F32),
             ((nz, nc, rows, width), BF),
             ((nz, nc, rows, width), BF),
             ((nx, nc, nz, ny) + mlp_t.shape[2:], BF),
-            ((nx, ny) + down.shape, BF),
         ],
-        (VM, pl.ANY, pl.ANY, pl.ANY, pl.ANY),
+        (VM, pl.ANY, pl.ANY, pl.ANY),
         Reduce.buffers(nz, rows, width)
         + [VM((rows, width), BF)]
         + Reduce.SEMS
         + Gather.SEMS * 2
-        + [DMA((peers,))] * 4
-        + [DMA((4,))],
+        + [DMA((peers,))] * 2
+        + [DMA((1,))],
         2,
     )
 
 
 def back_kernel(
-    dims, part, mlp_part, mid, cot, grad_mlp, grad_dn,
-    dx2, dag, output, gain_part, came_mlp, came_dn,
-    held, came, held2, came2, low, rs, rr, os, orr, ds, dr, ms, mr, ws, wr, local,
+    dims, part, mlp_part, mid, cot, grad_mlp,
+    dx2, dag, output, gain_part, came_mlp,
+    held, came, held2, came2, low, rs, rr, rxs, rxr, os, orr, oxs, oxr, ds, dr, dl, ms, mr, local,
 ):
     nx, nc, nz, ny = dims
     x, c, z, y = place()
     greet(*dims)
-    reduce = Reduce(part, held, came, rs, rr)
-    reduce2 = Reduce(mlp_part, held2, came2, os, orr)
+    reduce = Reduce(part, held, came, rs, rr, rxs, rxr)
+    reduce2 = Reduce(mlp_part, held2, came2, os, orr, oxs, oxr)
+    rows = Gather(low, dag, ds, dr, dl)
     reduce.start()
-    dn = Spread(lambda px, py: grad_dn.at[px, py], lambda px, py: came_dn.at[px, py], ws, wr, local.at[0], nx, ny)
     gu = Spread(
-        lambda px, py: grad_mlp.at[px, :, :, py], lambda px, py: came_mlp.at[px, py], ms, mr, local.at[1], nx, ny
+        lambda px, py: grad_mlp.at[px, :, :, py], lambda px, py: came_mlp.at[px, py], ms, mr, local.at[0], nx, ny
     )
     gu.start()
-    dn.start()
-    for k in range(nz - 1):
-        reduce.hop(k)
+    end = flow(reduce, None)
     gain_part[...] = jnp.zeros_like(gain_part)
 
     def settle(at, total):
@@ -424,87 +551,106 @@
         dx2[at, :] = gradient
         low[at, :] = gradient.astype(BF)
 
-    reduce.last(settle)
-    rows = Gather(low, dag, ds, dr, local.at[2])
-    rows.start()
     reduce2.start()
-    for k in range(nz - 1):
-        rows.hop(k + 1)
-        reduce2.hop(k)
+    end2 = flow(reduce2, rows, lambda part: reduce.last(part, settle))
 
     def finish(at, total):
         output[at, :] = (mid[at, :] + total).astype(BF)
 
-    reduce2.last(finish)
-    rows.finish()
-    reduce.finish()
-    reduce2.finish()
+    for part in range(PARTS):
+        reduce2.last(part, finish)
+    end2()
+    end()
     gu.arrived()
-    dn.arrived()
     gu.finish()
-    dn.finish()
-
-
-def back_call(dims, part, mlp_part, mid, cot, grad_mlp, grad_dn):
+
+
+def back_call(dims, part, mlp_part, mid, cot, grad_mlp):
     nx, nc, nz, ny = dims
     rows, width = mid.shape
     peers = nx * ny - 1
     return call(
         functools.partial(back_kernel, dims),
-        (part, mlp_part, mid, cot, grad_mlp, grad_dn),
-        (VM, VM, VM, VM, pl.ANY, pl.ANY),
+        (part, mlp_part, mid, cot, grad_mlp),
+        (VM, VM, VM, VM, pl.ANY),
         [
             ((rows, width), F32),
             ((nz, nc, rows, width), BF),
             ((rows, width), BF),
             ((8, width), F32),
             ((nx, ny, nc, nz) + grad_mlp.shape[4:], BF),
-            ((nx, ny) + grad_dn.shape[2:], BF),
         ],
-        (VM, pl.ANY, VM, VM, pl.ANY, pl.ANY),
+        (VM, pl.ANY, VM, VM, pl.ANY),
         Reduce.buffers(nz, rows, width) * 2
         + [VM((rows, width), BF)]
         + Reduce.SEMS * 2
         + Gather.SEMS
-        + [DMA((peers,))] * 4
-        + [DMA((3,))],
+        + [DMA((peers,))] * 2
+        + [DMA((1,))],
         3,
     )
 
 
 def last_kernel(
-    dims, part, tokens, dx2, grad_attn,
-    input_grad, gain_part, attn_g,
-    held, came, came_attn, sums, rs, rr, ds, dr, ss, sr, local,
+    dims, part, tokens, dx2, gains, mlp_g, came_dn, grad_attn,
+    input_grad, gain_part, grad_query, grad_key, grad_value, grad_out, grad_gate, grad_up, grad_down,
+    held, came, came_attn, sums, attn_g, rs, rr, rxs, rxr, ds, dr, ss, sr, local,
 ):
     nx, nc, nz, ny = dims
     x, c, z, y = place()
-    greet(*dims)
-    reduce = Reduce(part, held, came, rs, rr)
-    reduce.start()
+    own, cols = sums.shape[2:]
+    qcols = (cols - 128) // 2
+    span = mlp_g.shape[-1] // (2 * nx)
+    reduce = Reduce(part, held, came, rs, rr, rxs, rxr)
     spread = Spread(
         lambda px, py: grad_attn.at[px, :, :, py], lambda px, py: came_attn.at[px, py], ds, dr, local.at[0], nx, ny
     )
+    swap = Swap(sums, lambda pz, pc: attn_g.at[pz, pc], ss, sr, local.at[1])
+    greet(*dims)
+    reduce.start()
     spread.start()
-    for k in range(nz - 1):
-        reduce.hop(k)
-    spread.arrived()
-
-    own = sums.shape[2]
-
-    def add(i, carry):
-        at = pl.ds(pl.multiple_of(i * ROWS, ROWS), ROWS)
+
+    def unpack_mlp(at):
+        gain = gains[at, 1:2]
+        for k, grad in enumerate((grad_gate, grad_up)):
+            for t in range(nz * nc):
+                for i in range(nx):
+                    chunk = (i * nc + t % nc) * nz + t // nc
+                    source = (k * nx + i) * span
+                    piece = mlp_g[t // nc, t % nc, at, source : source + span].astype(F32) * gain
+                    grad[at, chunk * span : (chunk + 1) * span] = piece
+
+    def down(at):
+        total = came_dn[0, 0, at, :].astype(F32)
+        for px, py in others(nx, ny):
+            total = total + came_dn[px, py, at, :].astype(F32)
+        grad_down[at, :] = total
+
+    def add(at):
         for pz in range(nz):
             for pc in range(nc):
                 total = came_attn[0, 0, pc, pz, at, :].astype(F32)
                 for px, py in others(nx, ny):
                     total = total + came_attn[px, py, pc, pz, at, :].astype(F32)
                 sums[pz, pc, at, :] = total.astype(BF)
-        return carry
-
-    lax.fori_loop(0, own // ROWS, add, 0)
-    swap = Swap(sums, lambda pz, pc: attn_g.at[pz, pc], ss, sr, local.at[1])
-    swap.start()
+
+    def exchange():
+        spread.arrived()
+        by_rows(own, add)
+        swap.start()
+
+    def nothing():
+        return None
+
+    work = [
+        lambda: by_rows(own, unpack_mlp),
+        nothing,
+        lambda: by_rows(grad_down.shape[0], down),
+        nothing,
+        nothing,
+        exchange,
+    ]
+    end = flow(reduce, None, None, work)
     gain_part[...] = jnp.zeros_like(gain_part)
 
     def settle(at, total):
@@ -516,26 +662,61 @@
             total - normed * jnp.mean(total * normed, axis=-1, keepdims=True)
         )
 
-    reduce.last(settle)
-    reduce.finish()
+    for half in range(PARTS):
+        reduce.last(half, settle)
+    end()
     spread.finish()
     swap.arrived()
     swap.finish()
 
-
-def last_call(dims, part, tokens, dx2, grad_attn):
+    def unpack(at):
+        gain = gains[at, 0:1]
+        heads = []
+        for t in range(nz * nc):
+            block = attn_g[t // nc, t % nc, at, : qcols + 128].astype(F32) * gain
+            grad_query[at, t * qcols : (t + 1) * qcols] = block[:, :qcols]
+            if t % (nz * nc // KV_HEADS):
+                heads[-1] = heads[-1] + block[:, qcols:]
+            else:
+                heads.append(block[:, qcols:])
+        for pair in range(KV_HEADS // 2):
+            one, two = heads[2 * pair], heads[2 * pair + 1]
+            first = lanes(one.shape) < 64
+            grad_key[at, pair * 128 : pair * 128 + 128] = jnp.where(first, one, pltpu.roll(two, 64, 1))
+            grad_value[at, pair * 128 : pair * 128 + 128] = jnp.where(first, pltpu.roll(one, 64, 1), two)
+
+    by_rows(own, unpack)
+    for t in range(nz * nc):
+        block = attn_g[t // nc, t % nc, :, qcols + 128 :].astype(F32)
+        grad_out[t * qcols : (t + 1) * qcols, :] = block.T
+
+
+def last_call(dims, part, tokens, dx2, gains, mlp_g, came_dn, grad_attn):
     nx, nc, nz, ny = dims
     rows, width = tokens.shape
     own, cols = grad_attn.shape[4:]
+    qcols = (cols - 128) // 2
+    heads = nz * nc * qcols
+    ff = mlp_g.shape[-1] // 2 * nz * nc
     peers = nx * ny - 1
     return call(
         functools.partial(last_kernel, dims),
-        (part, tokens, dx2, grad_attn),
-        (VM, VM, VM, pl.ANY),
-        [((rows, width), F32), ((8, width), F32), ((nz, nc, own, cols), BF)],
-        (VM, VM, VM),
+        (part, tokens, dx2, gains, mlp_g, came_dn, grad_attn),
+        (VM,) * 6 + (pl.ANY,),
+        [
+            ((rows, width), F32),
+            ((8, width), F32),
+            ((own, heads), F32),
+            ((own, KV_HEADS * HEAD_DIM), F32),
+            ((own, KV_HEADS * HEAD_DIM), F32),
+            ((heads, own), F32),
+            ((own, ff), F32),
+            ((own, ff), F32),
+            (came_dn.shape[2:], F32),
+        ],
+        (VM,) * 9,
         Reduce.buffers(nz, rows, width)
-        + [VM((nx, ny, nc, nz, own, cols), BF), VM((nz, nc, own, cols), BF)]
+        + [VM((nx, ny, nc, nz, own, cols), BF), VM((nz, nc, own, cols), BF), VM((nz, nc, own, cols), BF)]
         + Reduce.SEMS
         + [DMA((peers,))] * 2
         + [DMA((nz * nc - 1,))] * 2
@@ -550,10 +731,6 @@
 
 def nn(a, b):
     return jnp.dot(a, b, preferred_element_type=F32)
-
-
-def lanes(shape):
-    return lax.broadcasted_iota(jnp.int32, shape, len(shape) - 1)
 
 
 def rope_lanes(tab):
@@ -706,9 +883,9 @@
 
 
 def attend_back_kernel(
-    dims, dag, w, tab, q, kk, vv, stat, mlp_sum,
-    dqkv, part, mlp_g,
-    do, kt, dk, dv, out, came, ss, sr, ys, yr, local,
+    dims, dag, w, tab, q, kk, vv, stat, mlp_sum, grad_dn,
+    dqkv, part, mlp_g, came_dn,
+    do, kt, dk, dv, out, came, ss, sr, ys, yr, ws, wr, local,
 ):
     nx, nc, nz, ny = dims
     x, c, z, y = place()
@@ -719,6 +896,8 @@
     greet(*dims, cross=True)
     swap = Swap(mlp_sum, lambda pz, pc: mlp_g.at[pz, pc], ss, sr, local.at[0])
     swap.start()
+    dn = Spread(lambda px, py: grad_dn.at[px, py], lambda px, py: came_dn.at[px, py], ws, wr, local.at[1], nx, ny)
+    dn.start()
 
     def project(i, carry):
         res = nn(dag[i].reshape(nc * rows, width), w[:, qcols + 128 : 2 * qcols + 128])
@@ -810,9 +989,11 @@
         copy.wait_send()
     swap.arrived()
     swap.finish()
-
-
-def attend_back_call(dims, dag, w, tab, q, kk, vv, stat, mlp_sum):
+    dn.arrived()
+    dn.finish()
+
+
+def attend_back_call(dims, dag, w, tab, q, kk, vv, stat, mlp_sum, grad_dn):
     nx, nc, nz, ny = dims
     rows, width = dag.shape[2:]
     qcols = q.shape[-1]
@@ -822,14 +1003,15 @@
     own, cols = mlp_sum.shape[2:]
     return call(
         functools.partial(attend_back_kernel, dims),
-        (dag, w, tab, q, kk, vv, stat, mlp_sum),
-        (VM, VM, VM, VM, VM, VM, VM, pl.ANY),
+        (dag, w, tab, q, kk, vv, stat, mlp_sum, grad_dn),
+        (VM, VM, VM, VM, VM, VM, VM, pl.ANY, pl.ANY),
         [
             ((nz, nc, rows, qcols + 128), BF),
             ((nz, nc, rows, width), BF),
             ((nz, nc, own, cols), BF),
+            (grad_dn.shape, BF),
         ],
-        (VM, VM, pl.ANY),
+        (VM, VM, pl.ANY, pl.ANY),
         [
             VM((nz, nc, rows, qcols), BF),
             VM((nc, 128, keys), BF),
@@ -840,7 +1022,8 @@
         ]
         + [DMA((members,))] * 2
         + [DMA((near,))] * 2
-        + [DMA((1,))],
+        + [DMA((nx * ny - 1,))] * 2
+        + [DMA((2,))],
         6,
     )
 
@@ -856,40 +1039,10 @@
     own = w_query.shape[0]
     heads = HEADS // team
     qcols = heads * HEAD_DIM
-    kv_rep = team // KV_HEADS
-    ff = w_gate.shape[1]
     piece = w_down.shape[0]
     ffcols = piece * nx * ny
 
-    gain_a = attn_gain.astype(F32)[:, None]
-    gain_m = mlp_gain.astype(F32)[:, None]
-
-    def by_heads(w):
-        return w.reshape(own, team, -1).transpose(1, 0, 2)
-
-    def by_kv(w):
-        return jnp.repeat(w.reshape(own, KV_HEADS, HEAD_DIM).transpose(1, 0, 2), kv_rep, axis=0)
-
-    def scaled(w, gain):
-        return (w.astype(F32) * gain).astype(BF)
-
-    def by_ff(w):
-        w = w.reshape(own, nx, nc, nz, ny, piece).transpose(3, 2, 0, 1, 4, 5)
-        return w.reshape(team, own, ffcols)
-
-    attn_blocks = jnp.concatenate(
-        [
-            by_heads(scaled(w_query, gain_a)),
-            by_kv(scaled(w_key, gain_a)),
-            by_kv(scaled(w_value, gain_a)),
-            by_heads(w_out.T),
-        ],
-        axis=-1,
-    )
-    mlp_blocks = jnp.concatenate([by_ff(scaled(w_gate, gain_m)), by_ff(scaled(w_up, gain_m))], axis=-1)
-    xf = tokens.astype(F32)
-    inv1 = lax.rsqrt(jnp.mean(xf * xf, axis=-1, keepdims=True) + EPSILON)
-    n1 = xf * inv1
+    gains = jnp.stack([attn_gain, mlp_gain], axis=1).astype(F32)
     half = HEAD_DIM // 2
     frequency = 10000.0 ** (-2.0 * jnp.arange(half, dtype=F32) / HEAD_DIM)
     angles = positions.astype(F32)[:, None] * frequency[None, :]
@@ -901,15 +1054,13 @@
         ],
         axis=-1,
     )
-    n1g, tab, w_attn = first_call(
-        dims, n1.astype(BF), table, attn_blocks.reshape(nz, nc, own, attn_blocks.shape[-1])
-    )
-    w_attn = w_attn.reshape(width, attn_blocks.shape[-1])
+    n1g, tab, w_attn, mlp_blocks, w_dn = first_call(
+        dims, tokens, table, gains, w_query, w_key, w_value, w_out, w_gate, w_up, w_down
+    )
+    w_attn = w_attn.reshape(width, w_attn.shape[-1])
     total = team * rows
-    q, kk, vv, stat, ob, part, mlp_t = attend_call(
-        dims, n1g, w_attn, tab, mlp_blocks.reshape(nz, nc, own, 2 * ffcols)
-    )
-    mid_f, n2g, cotg, w_mlp, w_dn = middle_call(dims, part, tokens, cotangent, mlp_t, w_down)
+    q, kk, vv, stat, ob, part, mlp_t = attend_call(dims, n1g, w_attn, tab, mlp_blocks)
+    mid_f, n2g, cotg, w_mlp = middle_call(dims, part, tokens, cotangent, mlp_t)
     n2g = n2g.reshape(total, width)
     cotg = cotg.reshape(total, width)
     w_mlp = w_mlp.reshape(width, 2 * ffcols)
@@ -927,38 +1078,23 @@
     dmlp = jnp.concatenate([dgt, dup], axis=-1)
     dn2 = dot_right_t(dmlp, w_mlp).astype(BF).reshape(nz, nc, rows, width)
     mlp_part = dot_left_t(n2g, dmlp).astype(BF).reshape(nx, nc, nz, ny, own, 2 * ffcols)
-    dx2, dag, output, gain_m_part, mlp_came, down_came = back_call(
-        dims, dn2, mlp_out, mid_f, cotangent, mlp_part, down_part.reshape(nx, ny, piece, width)
-    )
+    dx2, dag, output, gain_m_part, mlp_came = back_call(dims, dn2, mlp_out, mid_f, cotangent, mlp_part)
     gain_m_part = gain_m_part.sum(0)
     mlp_sum = jnp.sum(mlp_came.astype(F32), axis=(0, 1)).astype(BF).transpose(1, 0, 2, 3)
-    dqkv, dn1, mlp_g = attend_back_call(dims, dag, w_attn, tab, q, kk, vv, stat, mlp_sum)
+    dqkv, dn1, mlp_g, down_came = attend_back_call(
+        dims, dag, w_attn, tab, q, kk, vv, stat, mlp_sum, down_part.reshape(nx, ny, piece, width)
+    )
     out_part = dot_left_t(dag.reshape(total, width), ob.reshape(total, qcols))
     qkv_part = dot_left_t(n1g.reshape(total, width), dqkv.reshape(total, qcols + 128))
     attn_part = jnp.concatenate([qkv_part, out_part], axis=-1).astype(BF)
     attn_part = attn_part.reshape(nx, nc, nz, ny, own, attn_part.shape[-1])
-    input_grad, gain_a_part, attn_g = last_call(dims, dn1, tokens, dx2, attn_part)
-    gain_a_part = gain_a_part.sum(0)
-
-    attn_g = attn_g.reshape(team, own, attn_g.shape[-1]).astype(F32)
-    mlp_g = mlp_g.reshape(team, own, 2 * ffcols).astype(F32)
-    grad_down = jnp.sum(down_came.astype(F32), axis=(0, 1))
-    grad_query = attn_g[:, :, :qcols].transpose(1, 0, 2).reshape(own, HEADS * HEAD_DIM) * gain_a
-    kv_g = attn_g[:, :, qcols : qcols + 2 * HEAD_DIM].reshape(KV_HEADS, kv_rep, own, 2 * HEAD_DIM).sum(1)
-    grad_key = kv_g[..., :HEAD_DIM].transpose(1, 0, 2).reshape(own, KV_HEADS * HEAD_DIM) * gain_a
-    grad_value = kv_g[..., HEAD_DIM:].transpose(1, 0, 2).reshape(own, KV_HEADS * HEAD_DIM) * gain_a
-    grad_out = attn_g[:, :, qcols + 2 * HEAD_DIM :].transpose(1, 0, 2).reshape(own, HEADS * HEAD_DIM).T
-
-    def from_ff(g):
-        g = g.reshape(nz, nc, own, nx, ny, piece).transpose(2, 3, 1, 0, 4, 5)
-        return g.reshape(own, ff) * gain_m
-
-    grad_gate = from_ff(mlp_g[:, :, :ffcols])
-    grad_up = from_ff(mlp_g[:, :, ffcols:])
-    gains = jnp.stack([gain_a_part, gain_m_part], 0).reshape(2, nx * team * ny, own).transpose(1, 0, 2)
-    gains = lax.all_to_all(gains, ALL, 0, 0, tiled=False).sum(0)
-    grad_attn_gain = gains[0] / gain_a[:, 0]
-    grad_mlp_gain = gains[1] / gain_m[:, 0]
+    (
+        input_grad, gain_a_part, grad_query, grad_key, grad_value, grad_out, grad_gate, grad_up, grad_down
+    ) = last_call(dims, dn1, tokens, dx2, gains, mlp_g, down_came, attn_part)
+    parts = jnp.stack([gain_a_part.sum(0), gain_m_part], 0).reshape(2, nx * team * ny, own)
+    parts = lax.all_to_all(parts.transpose(1, 0, 2), ALL, 0, 0, tiled=False).sum(0)
+    grad_attn_gain = parts[0] / gains[:, 0]
+    grad_mlp_gain = parts[1] / gains[:, 1]
     return (
         output, input_grad, grad_query, grad_key, grad_value, grad_out,
         grad_attn_gain, grad_gate, grad_up, grad_down, grad_mlp_gain,

time: 622 us -> 503 us (0.81)
  the two profiles are of different devices: /device:TPU:31 before, /device:TPU:0 now
where the time goes in v4:
time: 503 us; the launch traced here: 496 us
  Pallas kernels  400 us (80%)
  matrix products  54.7 us (11%)
  local copies, waits for them, and re-layouts  16.4 us (3%)
  other arithmetic  13.8 us (3%)
  starting transfers between devices  5.33 us (1%)
    pallas_call x6, Pallas kernels, call(): pl.pallas_call(kernel, out_shape=[jax.ShapeDtypeStruct(s, t) for s, t in...  400 us
    dot_general x3, matrix products, dot_plain(): return jnp.dot(a, b, preferred_element_type=F32)  23 us
    dot_general x4, matrix products, dot_left_t(): lax.dot_general(a, b, (((0,), (0,)), ((), ())), preferred_element_type=F32)  18.1 us
    unnamed x52, local copies, waits for them, and re-layouts  13.6 us
    dot_general x2, matrix products, dot_right_t(): lax.dot_general(a, b, (((1,), (1,)), ((), ())), preferred_element_type=F32)  13.6 us
  transfers between devices with their start and end apart: 1, of which 1 were waited for; matrix products, arithmetic and copies ran while one was open for 1% of the time, Pallas kernels for 0%

profile of v4, /device:TPU:0, one launch (start us, length us, event | category | flops | bytes accessed | tf_op | source)
XLA Modules:
  0.0 495.6 jit_solution(9711394251344311816)
XLA Ops:
  0.7 0.7 convert_element_type.34
  1.3 0.7 convert_element_type.35
  2.0 0.7 pad_maximum_fusion.5
  2.7 0.1 copy.43
  2.8 0.6 convert_element_type.36.gains
  3.4 2.0 copy.44.w_out
  5.3 0.3 multiply_cosine_fusion
  5.7 0.1 broadcast_in_dim.2
  5.7 0.7 pad_maximum_fusion.4.table
  6.5 72.7 %shard_map.212 = (bf16[4,2,128,2048]{3,2,1,0:T(8,128)(2,1)}, f32[4,2,128,128]{3,2,1,0:T(8,128)}, bf16[2,2,4,2,64,640]{5,4,3,2,1,0:T(8,128)(2,1)}, bf16[4,2,64,14...) custom-call(bf16[128,2048]{1,0:T(8,128)(2,1)} %tokens.5, f32[128,128]{1,0:T(8,128)} %pad_maximum_fusion.4.table, ...), custom_call_target="tpu_custom_call" | custom-call | tf_op jit(solution)/shard_map/pallas_call | solution.py:331
  79.1 32.9 %shard_map.213 = (bf16[4,2,128,256]{3,2,1,0:T(8,128)(2,1)}, bf16[2,1024,128]{2,1,0:T(8,128)(2,1)}, bf16[2,1024,128]{2,1,0:T(8,128)(2,1)}, f32[4,2,8,256]{3,2,1,0...) custom-call(bf16[4,2,128,2048]{3,2,1,0:T(8,128)(2,1)} %get-tuple-ele, ...), custom_call_target="tpu_custom_call" | custom-call | tf_op jit(solution)/shard_map/pallas_call | solution.py:331
  112.1 95.6 %shard_map.214 = (f32[128,2048]{1,0:T(8,128)}, bf16[4,2,128,2048]{3,2,1,0:T(8,128)(2,1)}, bf16[4,2,128,2048]{3,2,1,0:T(8,128)(2,1)}, bf16[2,2,4,2,64,1408]{5,4,3,2,1,0:T(8,128)(2,1)}) custom-call(bf16[4,2,128,2048]{3,2,1,0:T(8,128)(2,1)} %get-tuple-element.49.part, bf16[128,2048]{1,0:T(8,128)(2,1)} %tokens.5, bf16[128,2048]{1,0:T(8,128)(2,1)} %cot.3, ...), custom_call_target="tpu_custom_call" | custom-call | tf_op jit(solution)/shard_map/pallas_call | solution.py:331
  207.7 0.0 copy-start.14
  207.7 0.0 copy-start.15
  207.7 0.0 slice-start
  207.8 8.1 %fusion = f32[1024,704]{0,1:T(8,128)} fusion(bf16[1024,2048]{1,0:T(8,128)(2,1)} %bitcast.60, bf16[2048,1408]{1,0:T(8,128)(2,1)} %bitcast.55), kind=kOutput, calls=%fused_computation.4 | convolution fusion | flops 2952790016 | bytes 10223616 | tf_op jit(solution)/shard_map/dot_general | solution.py:24
  215.9 0.0 copy-done.14
  215.9 0.0 copy-done.15
  215.9 0.0 copy-start.13
  215.9 4.8 fusion.7
  220.7 0.0 slice-done
  220.7 0.0 slice-done.1
  220.7 0.0 copy-done.13
  220.7 9.8 %multiply_convert_fusion = (bf16[1024,704]{0,1:T(8,128)(2,1)S(1)}, bf16[1024,704]{0,1:T(8,128)(2,1)S(1)}, bf16[1024,704]{0,1:T(8,128)(2,1)}) fusion(f32[1024,704]{0,1:T(8,128)} %fusion, f32[1024,704]{0,1:T(8,128)} %fusion.7, bf16[1024,2048]{1,0:T(8,128)(2,1)S(1)} %bitcast.61, bf16[2048,1408]{1,0:T(8,128)(2,1)S(1)} %bitcast.58), kind=kOutput, calls=%fused_computation.10 | convolution fusion | flops 2964324352 | bytes 17432576 | tf_op jit(solution)/shard_map/dot_general | solution.py:24
  230.5 4.5 convolution_convert_fusion.3
  235.0 5.1 %convolution_convert_fusion.1 = bf16[1024,2048]{1,0:T(8,128)(2,1)} fusion(bf16[1024,704]{0,1:T(8,128)(2,1)S(1)} %get-tuple-element.125, bf16[704,2048]{1,0:T(8,128)(2,1)S(1)} %bitcast.66), kind=kOutput, calls=%fused_computation.1 | convolution fusion | flops 2954887168 | bytes 8519680 | tf_op jit(solution)/shard_map/dot_general | solution.py:24
  240.1 0.0 copy-done.17
  240.1 8.5 %convolution_convert_fusion = bf16[2048,1408]{1,0:T(8,128)(2,1)} fusion(bf16[1024,2048]{1,0:T(8,128)(2,1)S(1)} %bitcast.62, bf16[1024,704]{0,1:T(8,128)(2,1)S(1)} %copy-done.17, bf16[1024,704]{0,1:T(8,128)(2,1)S(1)} %get-tuple-element.126), kind=kOutput, calls=%fused_computation | convolution fusion | flops 5914230784 | bytes 12845056 | tf_op jit(solution)/shard_map/dot_general | solution.py:32
  248.7 8.8 %convolution_convert_fusion.2 = bf16[1024,2048]{1,0:T(8,128)(2,1)} fusion(bf16[2048,1408]{1,0:T(8,128)(2,1)S(1)} %bitcast.59, bf16[1024,704]{0,1:T(8,128)(2,1)S(1)} %copy-done.17, bf16[1024,704]{0,1:T(8,128)(2,1)S(1)} %get-tuple-element.126), kind=kOutput, calls=%fused_computation.2 | convolution fusion | flops 5913444352 | bytes 12845056 | tf_op jit(solution)/shard_map/dot_general | solution.py:28
  257.5 89.3 %shard_map.215 = (f32[128,2048]{1,0:T(8,128)}, bf16[4,2,128,2048]{3,2,1,0:T(8,128)(2,1)}, bf16[128,2048]{1,0:T(8,128)(2,1)}, f32[8,2048]{1,0:T(8,128)}, bf16[2,2,2,4,64,1408]{5,4,3,2,1,0:T(8,128)(2,1)}) custom-call(bf16[4,2,128,2048]{3,2,1,0:T(8,128)(2,1)} %bitcast.51, bf16[4,2,128,2048]{3,2,1,0:T(8,128)(2,1)} %bitcast.50, ...), custom_call_target="tpu_custom_call" | custom-call | tf_op jit(solution)/shard_map/pallas_call | solution.py:331
  346.7 3.7 reduce_sum.39
  350.5 1.2 copy.54
  351.7 53.8 %shard_map.216 = (bf16[4,2,128,384]{3,2,1,0:T(8,128)(2,1)}, bf16[4,2,128,2048]{3,2,1,0:T(8,128)(2,1)}, bf16[4,2,64,1408]{3,2,1,0:T(8,128)(2,1)}, bf16[2,2,176,2048]{3,2,1,0:T(8,128)(2,1)}) custom-call(bf16[4,2,128,2048]{3,2,1,0:T(8,128)(2,1)} %get-tuple-element.57.dag, bf16[2048,640]{1,0:T(8,128)(2,1)} %bitcast.47, ...), custom_call_target="tpu_custom_call" | custom-call | tf_op jit(solution)/shard_map/pallas_call | solution.py:331
  405.4 0.0 copy-done.1
  405.5 0.0 copy-start
  405.5 0.0 copy-start.16
  405.5 3.7 bitcast_convert_fusion
  409.2 1.4 fusion.4
  410.6 1.9 pad_maximum_fusion.1.grad_attn
  412.5 56.2 %shard_map.217 = (f32[128,2048]{1,0:T(8,128)}, f32[8,2048]{1,0:T(8,128)}, f32[64,2048]{1,0:T(8,128)}, f32[64,256]{1,0:T(8,128)}, f32[64,256]{1,0:T(8,128)}, /*in...) custom-call(bf16[4,2,128,2048]{3,2,1,0:T(8,128)(2,1)} %get-tuple-element.63.part, ...), custom_call_target="tpu_custom_call" | custom-call | tf_op jit(solution)/shard_map/pallas_call | solution.py:331
  468.7 1.0 reduce_sum.40
  469.7 0.1 stack.21
  469.8 0.1 stack.22
  469.9 0.7 reshape.83
  470.6 5.3 %all-to-all-start = ((f32[32,1,128]{2,1,0:T(1,128)}), f32[32,1,128]{2,1,0:T(1,128)S(1)}, u32[]{:S(2)}, u32[]{:S(2)}) async-start(f32[32,1,128]{2,1,0:T(1,128)} %reshape.83), calls=%async_computation | async-start | bytes 32768 | tf_op jit(solution)/shard_map/all_to_all | solution.py:1095
  476.0 0.7 slice_reduce_fusion
  476.7 2.4 copy.48
  479.1 3.9 all-to-all-done
  483.0 0.6 copy-done.12
  483.6 0.5 broadcast.22
  484.1 1.4 reduce.5
  485.5 0.7 reshape.84
  486.2 0.8 reduce_sum.42
  487.0 1.2 bitcast_divide_fusion
  488.3 0.8 copy.63
  489.1 1.0 copy.64
  490.0 0.8 copy.65
  490.8 0.6 copy.66
  491.5 0.0 copy-done.10
  491.5 0.6 copy.67
  492.1 1.1 copy.68
  493.2 1.1 copy.69
  494.3 0.0 copy-done.2
  494.3 1.1 copy.70
  (28 shorter events, 0.1 us)
Async XLA Ops:
  207.7 8.2 %copy-start.14 = (bf16[4,2,128,2048]{3,2,1,0:T(8,128)(2,1)S(1)}, bf16[4,2,128,2048]{3,2,1,0:T(8,128)(2,1)}, u32[]{:S(2)}) copy-start(bf16[4,2,128,2048]{3,2,1,0:T(8,128)(2,1)} %get-tuple-element.51) | copy-start | bytes 12582916
  207.7 8.2 %copy-start.15 = (bf16[2,2,176,2048]{3,2,1,0:T(8,128)(2,1)S(1)}, bf16[2,2,176,2048]{3,2,1,0:T(8,128)(2,1)}, u32[]{:S(2)}) copy-start(bf16[2,2,176,2048]{3,2,1,0:T(8,128)(2,1)} %get-tuple-element.52) | copy-start | bytes 8650756
  207.7 13.0 %slice-start = ((s8[5767168]{0:T(1024)(128)(4,1)}), s8[4194304]{0:T(1024)(128)(4,1)S(1)}, s32[]{:S(2)}) async-start(s8[5767168]{0:T(1024)(128)(4,1)} %bitcast.56), calls=%async_computation.1 | async-start | bytes 8388608
  215.9 4.8 slice-start.1
  215.9 4.8 copy-start.13
  235.0 5.1 %copy-start.17 = (bf16[1024,704]{0,1:T(8,128)(2,1)S(1)}, bf16[1024,704]{0,1:T(8,128)(2,1)}, u32[]{:S(2)}) copy-start(bf16[1024,704]{0,1:T(8,128)(2,1)} %get-tuple-element.127) | copy-start | bytes 4325380
  351.7 53.8 %copy-start.1 = (bf16[4,2,128,2048]{3,2,1,0:T(8,128)(2,1)S(1)}, bf16[4,2,128,2048]{3,2,1,0:T(8,128)(2,1)}, u32[]{:S(2)}) copy-start(bf16[4,2,128,2048]{3,2,1,0:T(8,128)(2,1)} %get-tuple-element.45.n1g) | copy-start | bytes 12582916
  405.5 3.7 copy-start
  405.5 3.7 copy-start.16
  412.5 57.3 %copy-start.9 = (f32[8,2048]{1,0:T(8,128)S(1)}, f32[8,2048]{1,0:T(8,128)}, u32[]{:S(2)}) copy-start(f32[8,2048]{1,0:T(8,128)} %get-tuple-element.75) | copy-start | bytes 196612
  412.5 63.5 %copy-start.6 = (f32[64,2]{1,0:T(8,128)S(1)}, f32[64,2]{1,0:T(8,128)}, u32[]{:S(2)}) copy-start(f32[64,2]{1,0:T(8,128)} %convert_element_type.36.gains) | copy-start | bytes 1540
  412.5 75.8 %copy-start.7 = (bf16[128,2048]{1,0:T(8,128)(2,1)S(1)}, bf16[128,2048]{1,0:T(8,128)(2,1)}, u32[]{:S(2)}) copy-start(bf16[128,2048]{1,0:T(8,128)(2,1)} %get-tuple-element.143) | copy-start | bytes 1572868
  468.7 20.4 %copy-start.5 = (f32[128,2048]{1,0:T(8,128)S(1)}, f32[128,2048]{1,0:T(8,128)}, u32[]{:S(2)}) copy-start(f32[128,2048]{1,0:T(8,128)} %get-tuple-element.144) | copy-start | bytes 3145732
  468.7 21.3 %copy-start.8 = (f32[64,2048]{1,0:T(8,128)S(1)}, f32[64,2048]{1,0:T(8,128)}, u32[]{:S(2)}) copy-start(f32[64,2048]{1,0:T(8,128)} %get-tuple-element.145) | copy-start | bytes 1572868
  470.6 12.4 %all-to-all-start = ((f32[32,1,128]{2,1,0:T(1,128)}), f32[32,1,128]{2,1,0:T(1,128)S(1)}, u32[]{:S(2)}, u32[]{:S(2)}) async-start(f32[32,1,128]{2,1,0:T(1,128)} %reshape.83), calls=%async_computation | async-start | bytes 32768 | tf_op jit(solution)/shard_map/all_to_all | solution.py:1095
  476.7 15.4 %copy-start.4 = (f32[64,5632]{1,0:T(8,128)S(1)}, f32[64,5632]{1,0:T(8,128)}, u32[]{:S(2)}) copy-start(f32[64,5632]{1,0:T(8,128)} %get-tuple-element.150) | copy-start | bytes 4325380
  483.0 0.6 copy-start.12
  487.0 3.8 copy-start.11
  487.0 4.4 copy-start.10
  489.1 4.1 copy-start.3
  492.1 2.2 copy-start.2

commit v5 on v4

v5 whole, which is shorter than its diff:
```python
import functools

import jax
import jax.numpy as jnp
from jax import lax
from jax.experimental import pallas as pl
from jax.experimental.pallas import tpu as pltpu
from jax.sharding import Mesh
from jax.sharding import PartitionSpec as P

HEADS = 32
KV_HEADS = 4
HEAD_DIM = 64
EPSILON = 1e-05
MASKED = -1e30
ALL = ("x", "core", "z", "y")
TEAM = ("z", "core")
DATA = ("x", "y")
BF = jnp.bfloat16
F32 = jnp.float32


MESH = pl.DeviceIdType.MESH
VM = pltpu.VMEM
DMA = pltpu.SemaphoreType.DMA
ROWS = 16
PARTS = 2
WINDOW = 2
KEYS = 1024


def place():
    return tuple(lax.axis_index(a) for a in ALL)


def others(nx, ny):
    return [(i, j) for i in range(nx) for j in range(ny) if (i, j) != (0, 0)]


def data_peer(step, nx, ny):
    x, _, _, y = place()
    return lax.rem(x + step[0], nx), lax.rem(y + step[1], ny)


def team_peer(step, nz, nc):
    _, c, z, _ = place()
    return lax.rem(z + step[0], nz), lax.rem(c + step[1], nc)


def greet(nx, nc, nz, ny, cross=False):
    barrier = pltpu.get_barrier_semaphore()
    x, c, z, y = place()
    extra = ny - 1 if cross else 0
    for i in range(extra):
        device = {"y": lax.rem(y + 1 + i, ny), "core": 1 - c}
        pl.semaphore_signal(barrier, inc=1, device_id=device, device_id_type=MESH)
    for step in others(nx, ny):
        px, py = data_peer(step, nx, ny)
        pl.semaphore_signal(barrier, inc=1, device_id={"x": px, "y": py}, device_id_type=MESH)
    for step in others(nz, nc):
        pz, pc = team_peer(step, nz, nc)
        pl.semaphore_signal(barrier, inc=1, device_id={"z": pz, "core": pc}, device_id_type=MESH)
    pl.semaphore_wait(barrier, nx * ny - 1 + nz * nc - 1 + extra)


def remote(source, target, send, recv, device):
    return pltpu.make_async_remote_copy(
        src_ref=source, dst_ref=target, send_sem=send, recv_sem=recv,
        device_id=device, device_id_type=MESH,
    )


def piece_of(part, rows):
    return pl.ds(part * (rows // PARTS), rows // PARTS)


class Gather:
    SEMS = [DMA((3, 4, PARTS)), DMA((2, 4, PARTS)), DMA((PARTS,))]

    def __init__(self, own, full, send, recv, local):
        self.own, self.full, self.send, self.recv, self.local = own, full, send, recv, local
        self.x, self.c, self.z, self.y = place()
        self.nz, _, self.rows = full.shape[:3]

    def copy(self, at, kind, part, mine=False):
        rows = piece_of(part, self.rows)
        slot = self.full.at[at, self.c, rows]
        device = ({"z": self.z + 1}, {"z": self.z - 1}, {"core": 1 - self.c})[kind]
        return remote(
            self.own.at[rows] if mine else slot, slot, self.send.at[kind, at, part],
            self.recv.at[0 if kind < 2 else 1, at, part], device,
        )

    def keep(self, part):
        rows = piece_of(part, self.rows)
        return pltpu.make_async_copy(self.own.at[rows], self.full.at[self.z, self.c, rows], self.local.at[part])

    def begin(self, part):
        self.keep(part).start()
        self.copy(self.z, 2, part, True).start()

    def finish(self):
        for part in range(PARTS):
            self.keep(part).wait()
            for at in range(self.nz):
                self.copy(at, 2, part).wait_send()
                self.copy(at, 2, part).wait_recv()


class Reduce:
    SEMS = [DMA((2, 4, PARTS)), DMA((2, 4, PARTS)), DMA((4,)), DMA((4,))]

    @staticmethod
    def buffers(nz, rows, width):
        return [VM((nz, rows, width), BF), VM((2, nz - 1, rows, width), BF)]

    def __init__(self, part, held, came, send, recv, across_send, across_recv):
        self.part, self.held, self.came, self.send, self.recv = part, held, came, send, recv
        self.across_send, self.across_recv = across_send, across_recv
        self.x, self.c, self.z, self.y = place()
        self.nz, _, self.rows, self.width = part.shape

    def across(self, to):
        return remote(
            self.part.at[to, 1 - self.c], self.held.at[to], self.across_send.at[to], self.across_recv.at[to],
            {"core": 1 - self.c},
        )

    def along(self, to, way, part):
        device = ({"z": self.z + 1}, {"z": self.z - 1})[way]
        rows = piece_of(part, self.rows)
        return remote(
            self.held.at[to, rows], self.came.at[way, to - 1 + way, rows], self.send.at[way, to, part],
            self.recv.at[way, to, part], device,
        )

    def start(self):
        for to in [a for k in range(self.nz) for a in (self.nz - 1 - k, k)][: self.nz]:
            self.across(to).start()

    def add(self, to, ways, part, out=None):
        size = self.rows // PARTS

        def body(i, carry):
            at = pl.ds(pl.multiple_of(part * size + i * ROWS, ROWS), ROWS)
            total = self.part[to, self.c, at, :].astype(F32) + self.held[to, at, :].astype(F32)
            for way in ways:
                total = total + self.came[way, to - 1 + way, at, :].astype(F32)
            if out is None:
                self.held[to, at, :] = total.astype(BF)
            else:
                out(at, total)
            return carry

        lax.fori_loop(0, size // ROWS, body, 0)

    def last(self, part, out):
        if part == 0:
            self.across(self.z).wait_recv()
        for at in range(self.nz):

            @pl.when(self.z == at)
            def _(at=at):
                ways = ([0] if at > 0 else []) + ([1] if at < self.nz - 1 else [])
                for way in ways:
                    self.along(at, way, part).wait_recv()
                self.add(at, ways, part, out)

    def finish(self):
        for to in range(self.nz):
            self.across(to).wait_send()


def plan(nz, reduces, gathers):
    last = nz - 1
    rows = []
    for e in range(nz):
        sums = [("R", last - k) for k in range(last) if last - k > e]
        blocks = [("G", e - k) for k in range(e + 1)]
        if reduces and gathers:
            if e == last:
                rows.append([None] + blocks[1:-1] + [None] + blocks[-1:])
            else:
                woven = blocks[:-1] + sums[:1] + blocks[-1:] + sums[1:]
                rows.append(woven)
        elif reduces:
            rows.append([None] * e + sums)
        else:
            rows.append(blocks if e < last else [None] + blocks[1:])
    return rows


def flow(reduce, gather, before=None, work=()):
    work = list(work)
    any_one = reduce or gather
    nz, z = any_one.nz, any_one.z
    table = plan(nz, reduce is not None, gather is not None)
    pending = {(way, e): [] for way in (0, 1) for e in range(nz)}

    def pace(key, make):
        queue = pending[key]
        if len(queue) >= WINDOW:
            queue.pop(0)().wait_send()
        make().start()
        queue.append(make)

    def step(way, e, kind, place_at, part):
        block = place_at if way == 0 else nz - 1 - place_at
        if kind == "R":
            if part == 0:
                reduce.across(block).wait_recv()
            if e > 0:
                reduce.along(block, way, part).wait_recv()
            reduce.add(block, (way,) if e > 0 else (), part)
            pace((way, e), functools.partial(reduce.along, block, way, part))
        else:
            mine = place_at == e
            if not mine:
                gather.copy(block, way, part).wait_recv()
            if e < nz - 1:
                pace((way, e), functools.partial(gather.copy, block, way, part, mine))
            if not mine:
                gather.copy(block, 2, part).start()

    for t in range(max(len(row) for row in table)):
        for part in range(PARTS):
            if t == 0 and before is not None:
                before(part)
            if t == 0 and gather is not None:
                gather.begin(part)
            for way in (0, 1):
                for e in range(nz):
                    op = table[e][t] if t < len(table[e]) else None
                    if op is not None:
                        pl.when(z == (e if way == 0 else nz - 1 - e))(
                            functools.partial(step, way, e, op[0], op[1], part)
                        )
            if work:
                work.pop(0)()
    for item in work:
        item()

    def finish():
        for (way, e), queue in pending.items():
            if queue:

                @pl.when(z == (e if way == 0 else nz - 1 - e))
                def _(queue=queue):
                    for make in queue:
                        make().wait_send()

        for one in (reduce, gather):
            if one is not None:
                one.finish()

    return finish


class Spread:
    def __init__(self, source, target, send, recv, local, nx, ny):
        self.source, self.target, self.send, self.recv = source, target, send, recv
        self.nx, self.ny = nx, ny
        self.x, _, _, self.y = place()
        self.own = lambda: pltpu.make_async_copy(source(self.x, self.y), target(self.x, self.y), local)

    def copies(self):
        for i, step in enumerate(others(self.nx, self.ny)):
            px, py = data_peer(step, self.nx, self.ny)
            yield remote(
                self.source(px, py), self.target(self.x, self.y), self.send.at[i], self.recv.at[i],
                {"x": px, "y": py},
            )

    def start(self):
        for copy in self.copies():
            copy.start()
        self.own().start()

    def start_along(self, far):
        for step, copy in zip(others(self.nx, self.ny), self.copies()):
            if step[0] == far:
                copy.start()
        if far == 0:
            self.own().start()

    def arrived(self):
        self.own().wait()
        for copy in self.copies():
            copy.wait_recv()

    def finish(self):
        for copy in self.copies():
            copy.wait_send()


class Swap:
    def __init__(self, source, slot, send, recv, local, nz, nc):
        self.source, self.slot, self.send, self.recv, self.nz, self.nc = source, slot, send, recv, nz, nc
        _, self.c, self.z, _ = place()
        self.own = lambda: pltpu.make_async_copy(source(self.z, self.c), slot(self.z, self.c), local)

    def copies(self):
        for i, step in enumerate(others(self.nz, self.nc)):
            pz, pc = team_peer(step, self.nz, self.nc)
            yield remote(
                self.source(pz, pc), self.slot(self.z, self.c), self.send.at[i], self.recv.at[i],
                {"z": pz, "core": pc},
            )

    def start(self):
        for copy in self.copies():
            copy.start()
        self.own().start()

    def arrived(self):
        self.own().wait()
        for copy in self.copies():
            copy.wait_recv()

    def finish(self):
        for copy in self.copies():
            copy.wait_send()


def call(kernel, operands, in_spaces, outs, out_spaces, scratch, number):
    return pl.pallas_call(
        kernel,
        out_shape=[jax.ShapeDtypeStruct(s, t) for s, t in outs],
        in_specs=[pl.BlockSpec(memory_space=s) for s in in_spaces],
        out_specs=[pl.BlockSpec(memory_space=s) for s in out_spaces],
        scratch_shapes=scratch,
        compiler_params=pltpu.CompilerParams(
            collective_id=number, has_side_effects=True, vmem_limit_bytes=60 << 20
        ),
    )(*operands)


def lanes(shape):
    return lax.broadcasted_iota(jnp.int32, shape, len(shape) - 1)


def by_rows(count, body):
    if count % ROWS or count == ROWS:
        body(slice(0, count))
    else:

        def step(i, carry):
            body(pl.ds(pl.multiple_of(i * ROWS, ROWS), ROWS))
            return carry

        lax.fori_loop(0, count // ROWS, step, 0)


def nt(a, b):
    return lax.dot_general(a, b, (((1,), (1,)), ((), ())), preferred_element_type=F32)


def nn(a, b):
    return jnp.dot(a, b, preferred_element_type=F32)


def tn(a, b):
    return lax.dot_general(a, b, (((0,), (0,)), ((), ())), preferred_element_type=F32)


def rope_lanes(tab):
    at = lanes(tab.shape)
    cos = jnp.where(at < 32, tab, 0.0)
    sin = jnp.where((at >= 32) & (at < 64), tab, 0.0)
    cos = cos + pltpu.roll(cos, 32, 1)
    cos = cos + pltpu.roll(cos, 64, 1)
    sin = sin - pltpu.roll(sin, 96, 1)
    sin = sin + pltpu.roll(sin, 64, 1)
    return cos, sin


def swap_halves(u):
    return jnp.where(lax.rem(lanes(u.shape), 64) < 32, pltpu.roll(u, 96, 1), pltpu.roll(u, 32, 1))


def two_heads(u):
    first = lanes(u.shape) < 64
    zero = jnp.zeros_like(u)
    return jnp.concatenate([jnp.where(first, u, zero), jnp.where(first, zero, u)], axis=0)


def join_heads(t):
    rows = t.shape[1] // 2
    return jnp.concatenate([t[:64, :rows], t[64:, rows:]], axis=0).T


def bias_of(tab, keys, first_row, first_key=0):
    rows = tab.shape[0]
    starts = tab.T[64:65, :].astype(jnp.int32)
    key = first_key + lax.broadcasted_iota(jnp.int32, (keys, rows), 0)
    row = first_row + lax.broadcasted_iota(jnp.int32, (keys, rows), 1)
    bias = jnp.where((key >= starts) & (key <= row), 0.0, MASKED)
    return jnp.concatenate([bias, bias], axis=1)


def forward_kernel(
    dims, tokens, table, gains, w_query, w_key, w_value, w_out_t, w_gate, w_up, down, cot,
    n1g, w_attn, tab, q, kk, vv, stat, ob, mid, n2g, cotg, w_mlp, w_dn,
    n1, blocks, mlp_blocks, mlp_t, kv, vt, part, held, came, n2,
    gs, gr, gl, ts, tr, ss, sr, ds, dr, ws, wr, us, ur, ys, yr, rs, rr, rxs, rxr, cs, cr, cl, ns, nr, nl, ms, mr, local,
):
    nx, nc, nz, ny = dims
    x, c, z, y = place()
    rows, width = tokens.shape
    own = w_query.shape[0]
    qcols = q.shape[-1]
    pairs = qcols // 128
    span = w_gate.shape[1] // (nx * nc * nz)
    keys_span = ny * rows
    dn = Spread(lambda px, py: down, lambda px, py: w_dn.at[px, py], ws, wr, local.at[0], nx, ny)
    swap = Swap(
        lambda pz, pc: blocks.at[pz, pc], lambda pz, pc: w_attn.at[x, pc, pz, y], ss, sr, local.at[1], nz, nc
    )
    tabs = Swap(lambda pz, pc: table, lambda pz, pc: tab.at[pz, pc], ts, tr, local.at[2], nz, nc)
    mlp_swap = Swap(
        lambda pz, pc: mlp_blocks.at[pz, pc], lambda pz, pc: mlp_t.at[pc, pz], us, ur, local.at[3], nz, nc
    )
    gu = Spread(lambda px, py: mlp_t, lambda px, py: w_mlp.at[px, :, :, py], ms, mr, local.at[4], nx, ny)
    first_rows = Gather(n1, n1g, gs, gr, gl)
    reduce = Reduce(part, held, came, rs, rr, rxs, rxr)
    cots = Gather(cot, cotg, cs, cr, cl)
    next_rows = Gather(n2, n2g, ns, nr, nl)
    greet(*dims)

    def pack(at):
        gain = gains[at, 0:1]
        for t in range(nz * nc):
            cols = slice(t * qcols, (t + 1) * qcols)
            blocks[t // nc, t % nc, at, :qcols] = (w_query[at, cols].astype(F32) * gain).astype(BF)
            blocks[t // nc, t % nc, at, qcols + 128 :] = w_out_t[at, cols]
        for pair in range(KV_HEADS // 2):
            cols = slice(pair * 128, pair * 128 + 128)
            key, value = w_key[at, cols].astype(F32) * gain, w_value[at, cols].astype(F32) * gain
            first = lanes(key.shape) < 64
            both = (
                jnp.where(first, key, pltpu.roll(value, 64, 1)),
                jnp.where(first, pltpu.roll(key, 64, 1), value),
            )
            for k in range(2):
                for rep in range(nz * nc // KV_HEADS):
                    t = (pair * 2 + k) * (nz * nc // KV_HEADS) + rep
                    blocks[t // nc, t % nc, at, qcols : qcols + 128] = both[k].astype(BF)

    by_rows(own, pack)
    swap.start()
    tabs.start()
    dn.start()

    def norm(at):
        value = tokens[at, :].astype(F32)
        inverse = lax.rsqrt(jnp.mean(value * value, axis=-1, keepdims=True) + EPSILON)
        n1[at, :] = (value * inverse).astype(BF)

    by_rows(rows, norm)

    def spread_copies():
        for i, step in enumerate(others(nx, ny)):
            px, py = data_peer(step, nx, ny)
            slot = w_attn.at[x, :, :, y]
            yield remote(slot, slot, ds.at[i], dr.at[i], {"x": px, "y": py})

    def spread():
        swap.arrived()
        for copy in spread_copies():
            copy.start()

    def pack_mlp(at):
        gain = gains[at, 1:2]
        for k, weight in enumerate((w_gate, w_up)):
            for t in range(nz * nc):
                for i in range(nx):
                    chunk = (i * nc + t % nc) * nz + t // nc
                    to = (k * nx + i) * span
                    piece = weight[at, chunk * span : (chunk + 1) * span].astype(F32) * gain
                    mlp_blocks[t // nc, t % nc, at, to : to + span] = piece.astype(BF)

    end = flow(None, first_rows, None, [spread, lambda: by_rows(own, pack_mlp)])
    end()
    mlp_swap.start()
    tabs.arrived()
    for copy in spread_copies():
        copy.wait_recv()

    def project(i, carry):
        res = nn(n1g[i].reshape(nc * rows, width), w_attn[..., : qcols + 128].reshape(width, qcols + 128))
        cos, sin = rope_lanes(tab[i].reshape(nc * rows, 128))
        for p in range(pairs):
            u = res[:, p * 128 : p * 128 + 128]
            u = (u * cos + swap_halves(u) * sin) * (HEAD_DIM ** (-0.5))
            q[i, :, :, p * 128 : p * 128 + 128] = u.astype(BF).reshape(nc, rows, 128)
        u = res[:, qcols : qcols + 128]
        u = jnp.where(lanes(u.shape) < 64, u * cos + swap_halves(u) * sin, u).astype(BF)
        for pc in range(nc):
            kv[pc, i, y] = u[pc * rows : (pc + 1) * rows]
        return carry

    lax.fori_loop(0, nz, project, 0)
    sends = []
    for i in range(ny - 1):
        slot = kv.at[:, :, y]
        sends.append(remote(slot, slot, ys.at[i], yr.at[i], {"y": lax.rem(y + 1 + i, ny)}))
    for copy in sends:
        copy.start()
    for copy in sends:
        copy.wait_recv()

    def double(i, carry):
        pc, pz = i // nz, lax.rem(i, nz)
        u = kv[pc, pz].reshape(keys_span, 128).astype(F32)
        r = pltpu.roll(u, 64, 1)
        first = lanes(u.shape) < 64
        at = pl.ds(pl.multiple_of(pz * keys_span, keys_span), keys_span)
        kk[pc, at, :] = jnp.where(first, u, r).astype(BF)
        values = jnp.where(first, r, u)
        vv[pc, at, :] = values.astype(BF)
        vt[pc, :, at] = values.T.astype(BF)
        return carry

    lax.fori_loop(0, nc * nz, double, 0)

    def attend(pc, carry):
        for pz in range(nz):
            keys = (pz + 1) * keys_span
            bias = bias_of(tab[pz, pc], keys, (pz * ny + y) * rows)
            for p in range(pairs):
                q2 = two_heads(q[pz, pc, :, p * 128 : p * 128 + 128])
                s = nt(kk[pc, :keys, :], q2) + bias
                top = jnp.max(s, axis=0, keepdims=True)
                e = jnp.exp(s - top)
                total = jnp.sum(e, axis=0, keepdims=True)
                stat[pz, pc, p : p + 1, :] = top + jnp.log(total)
                weights = (e * (1.0 / total)).astype(BF)
                o = join_heads(nn(vt[pc, :, :keys], weights))
                ob[pz, pc, :, p * 128 : p * 128 + 128] = o.astype(BF)
        return carry

    lax.fori_loop(0, nc, attend, 0)

    def output(i, carry):
        half, odd = i // 2, lax.rem(i, 2)
        pz = odd * half + (1 - odd) * (nz - 1 - half)
        for px in range(nx):
            cols = slice(px * (width // nx), (px + 1) * (width // nx))
            weights = w_attn[px, :, :, :, :, qcols + 128 :].reshape(width // nx, qcols)
            res = nt(ob[pz].reshape(nc * rows, qcols), weights)
            part[pz, :, :, cols] = res.astype(BF).reshape(nc, rows, width // nx)
        reduce.across(pz).start()
        return carry

    lax.fori_loop(0, nz, output, 0)

    def spread_mlp():
        mlp_swap.arrived()
        gu.start()

    end2 = flow(reduce, cots, None, [spread_mlp])

    def settle(at, total):
        value = tokens[at, :].astype(F32) + total
        mid[at, :] = value
        inverse = lax.rsqrt(jnp.mean(value * value, axis=-1, keepdims=True) + EPSILON)
        n2[at, :] = (value * inverse).astype(BF)

    end3 = flow(None, next_rows, lambda half: reduce.last(half, settle))
    end3()
    end2()
    gu.arrived()
    dn.arrived()
    for one in (swap, tabs, mlp_swap, gu, dn):
        one.finish()
    for copy in list(spread_copies()) + sends:
        copy.wait_send()


def forward_call(dims, tokens, table, gains, w_query, w_key, w_value, w_out_t, w_gate, w_up, down, cot):
    nx, nc, nz, ny = dims
    rows, width = tokens.shape
    own = w_query.shape[0]
    qcols = HEADS // (nz * nc) * HEAD_DIM
    cols = 2 * qcols + 128
    peers, members = nx * ny - 1, nz * nc - 1
    mlp_cols = 2 * w_gate.shape[1] // (nz * nc)
    keys = nz * ny * rows
    team_rows = (nz, nc, rows, width)
    return call(
        functools.partial(forward_kernel, dims),
        (tokens, table, gains, w_query, w_key, w_value, w_out_t, w_gate, w_up, down, cot),
        (VM,) * 9 + (pl.ANY, VM),
        [
            (team_rows, BF),
            ((nx, nc, nz, ny, own, cols), BF),
            ((nz, nc) + table.shape, F32),
            ((nz, nc, rows, qcols), BF),
            ((nc, keys, 128), BF),
            ((nc, keys, 128), BF),
            ((nz, nc, 8, 2 * rows), F32),
            ((nz, nc, rows, qcols), BF),
            ((rows, width), F32),
            (team_rows, BF),
            (team_rows, BF),
            ((nx, nc, nz, ny, own, mlp_cols), BF),
            ((nx, ny) + down.shape, BF),
        ],
        (VM,) * 9 + (pl.ANY,) * 4,
        [
            VM((rows, width), BF),
            VM((nz, nc, own, cols), BF),
            VM((nz, nc, own, mlp_cols), BF),
            VM((nc, nz, own, mlp_cols), BF),
            VM((nc, nz, ny, rows, 128), BF),
            VM((nc, 128, keys), BF),
            VM(team_rows, BF),
        ]
        + Reduce.buffers(nz, rows, width)
        + [VM((rows, width), BF)]
        + Gather.SEMS
        + [DMA((members,))] * 4
        + [DMA((peers,))] * 4
        + [DMA((members,))] * 2
        + [DMA((max(ny - 1, 1),))] * 2
        + Reduce.SEMS
        + Gather.SEMS * 2
        + [DMA((peers,))] * 2
        + [DMA((5,))],
        1,
    )


def mlp_kernel(
    dims, n2g, cotg, w_mlp, w_dn, mid, cot,
    dx2, dag, output, came_mlp, came_dn, rest_dn,
    n2v, cotv, wv, wd, hid, hid_t, dmlp, part, mlp_out, grad_mlp, grad_dn,
    held, came, held2, came2, low,
    loads, rs, rr, rxs, rxr, os, orr, oxs, oxr, ds, dr, dl, ms, mr, ws, wr, local,
):
    nx, nc, nz, ny = dims
    x, c, z, y = place()
    rows, width = mid.shape
    ff2 = wv.shape[-1]
    ff = ff2 // 2
    piece = wd.shape[2]
    block = nc * rows
    fetch_w = pltpu.make_async_copy(w_mlp, wv, loads.at[0])
    fetch_d = pltpu.make_async_copy(w_dn, wd, loads.at[1])
    fetch_w.start()

    def fetch(at, k):
        source, target = ((n2g, n2v), (cotg, cotv))[k]
        return pltpu.make_async_copy(source.at[at], target.at[at], loads.at[2 + k * nz + at])

    order = [a for k in range(nz) for a in (nz - 1 - k, k)][:nz]
    for k in range(nz):
        fetch(order[k], 0).start()
        if k == 0:
            fetch_d.start()
        fetch(order[k], 1).start()
    greet(*dims)
    reduce = Reduce(part, held, came, rs, rr, rxs, rxr)
    reduce2 = Reduce(mlp_out, held2, came2, os, orr, oxs, oxr)
    into = Gather(low, dag, ds, dr, dl)
    gu = Spread(
        lambda px, py: grad_mlp.at[px, :, :, py], lambda px, py: came_mlp.at[px, py], ms, mr, local.at[0], nx, ny
    )
    dn = Spread(lambda px, py: grad_dn.at[px, py], lambda px, py: came_dn.at[px, py], ws, wr, local.at[1], nx, ny)
    half_width = width // 2

    def down_rows(cols):
        if piece % ROWS:
            return jnp.concatenate([wd[px, py, :, cols] for px in range(nx) for py in range(ny)], axis=0)
        return wd[:, :, :, cols].reshape(ff, -1)

    def weights(px):
        return wv[px].reshape(width // nx, ff2)

    fetch_w.wait()

    def forward_back(k, carry):
        half = k // 2
        odd = lax.rem(k, 2)
        at = odd * half + (1 - odd) * (nz - 1 - half)
        fetch(at, 0).wait()
        u = nn(n2v[at].reshape(block, width), wv[...].reshape(width, ff2))
        gt, up = u[:, :ff], u[:, ff:]
        sg = jax.nn.sigmoid(gt)
        silu = gt * sg
        value = (silu * up).astype(BF)
        hid[at] = value
        hid_t[:, pl.ds(pl.multiple_of(at * block, block), block)] = value.astype(F32).T.astype(BF)
        pl.when(k == 0)(fetch_d.wait)
        fetch(at, 1).wait()
        dh = nt(cotv[at].reshape(block, width), down_rows(slice(None)))
        dgt = dh * up * sg * (1.0 + gt * (1.0 - sg))
        dmlp[at] = jnp.concatenate([dgt, dh * silu], axis=1).astype(BF)

        for px in range(nx):
            cols = slice(px * (width // nx), (px + 1) * (width // nx))
            res = nt(dmlp[at], weights(px))
            part[at, :, :, cols] = res.astype(BF).reshape(nc, rows, width // nx)
        reduce.across(at).start()
        return carry

    lax.fori_loop(0, 2, forward_back, 0)
    chunk = width // 4

    def down_grad(part_of, target):
        def body(n, carry):
            at = pl.ds(pl.multiple_of(n * chunk, chunk), chunk)
            cols = pl.ds(pl.multiple_of(part_of * half_width + n * chunk, chunk), chunk)
            res = nn(hid_t[...], cotv[:, :, :, cols].reshape(nz * block, chunk)).astype(BF)
            for px in range(nx):
                for py in range(ny):
                    k = (px * ny + py) * piece
                    target[px, py, :, at] = res[k : k + piece]
            return carry

        lax.fori_loop(0, 2, body, 0)

    def mlp_grad(far):
        px = lax.rem(x + far, nx)
        size = width // (nx * 4)

        def body(j, carry):
            cols = pl.ds(pl.multiple_of(px * (width // nx) + j * size, size), size)
            res = tn(n2v[:, :, :, cols].reshape(nz * block, size), dmlp[...].reshape(nz * block, ff2))
            own = grad_mlp.shape[4]
            grad_mlp[px, j // 2, pl.ds(lax.rem(j, 2) * (nz // 2), nz // 2)] = res.astype(BF).reshape(
                nz // 2, ny, own, ff2
            )
            return carry

        lax.fori_loop(0, 4, body, 0)
        gu.start_along(far)

    def mlp_sum(n, carry):
        cols = pl.ds(pl.multiple_of(n * chunk, chunk), chunk)
        res = nn(hid[...].reshape(nz * block, ff), down_rows(cols))
        mlp_out[:, :, :, cols] = res.astype(BF).reshape(nz, nc, rows, chunk)
        return carry

    def down_first():
        down_grad(0, grad_dn)
        dn.start()

    def down_second():
        down_grad(1, rest_dn)

    def sum_all():
        lax.fori_loop(0, 4, mlp_sum, 0)
        reduce2.start()

    def more():
        lax.fori_loop(2, 3, forward_back, 0)

    def most():
        lax.fori_loop(3, nz, forward_back, 0)

    work = [more, most] + [functools.partial(mlp_grad, far) for far in reversed(range(nx))]
    end = flow(reduce, None, None, work + [down_first, down_second, sum_all])

    def settle(at, total):
        value = mid[at, :]
        inverse = lax.rsqrt(jnp.mean(value * value, axis=-1, keepdims=True) + EPSILON)
        normed = value * inverse
        gradient = cot[at, :].astype(F32) + inverse * (
            total - normed * jnp.mean(total * normed, axis=-1, keepdims=True)
        )
        dx2[at, :] = gradient
        low[at, :] = gradient.astype(BF)

    end2 = flow(reduce2, into, lambda part: reduce.last(part, settle))

    def finish(at, total):
        output[at, :] = (mid[at, :] + total).astype(BF)

    for half in range(PARTS):
        reduce2.last(half, finish)
    end2()
    end()
    gu.arrived()
    dn.arrived()
    gu.finish()
    dn.finish()


def mlp_call(dims, n2g, cotg, w_mlp, w_dn, mid, cot):
    nx, nc, nz, ny = dims
    rows, width = mid.shape
    own, ff2 = w_mlp.shape[4:]
    block = nc * rows
    peers = nx * ny - 1
    half_dn = w_dn.shape[:3] + (width // 2,)
    return call(
        functools.partial(mlp_kernel, dims),
        (n2g, cotg, w_mlp, w_dn, mid, cot),
        (pl.ANY, pl.ANY, pl.ANY, pl.ANY, VM, VM),
        [
            ((rows, width), F32),
            ((nz, nc, rows, width), BF),
            ((rows, width), BF),
            ((nx, ny, nc, nz, own, ff2), BF),
            (half_dn, BF),
            (half_dn, BF),
        ],
        (VM, pl.ANY, VM, pl.ANY, pl.ANY, VM),
        [
            VM(n2g.shape, BF),
            VM(cotg.shape, BF),
            VM(w_mlp.shape, BF),
            VM(w_dn.shape, BF),
            VM((nz, block, ff2 // 2), BF),
            VM((ff2 // 2, nz * block), BF),
            VM((nz, block, ff2), BF),
            VM(n2g.shape, BF),
            VM(n2g.shape, BF),
            VM(w_mlp.shape, BF),
            VM(half_dn, BF),
        ]
        + Reduce.buffers(nz, rows, width) * 2
        + [VM((rows, width), BF), DMA((2 + 2 * nz,))]
        + Reduce.SEMS * 2
        + Gather.SEMS
        + [DMA((peers,))] * 4
        + [DMA((2,))],
        3,
    )


def backward_kernel(
    dims, dag, w, tab, q, kk, vv, stat, ob, came_mlp, came_dn, rest_dn, n1g, tokens, dx2, gains,
    w_query, w_key, w_value, w_gate, w_up,
    input_grad, grad_query, grad_key, grad_value, grad_out_t, grad_gate, grad_up, grad_down, grad_gain,
    do, kt, dk, dv, out, near, dqkv, part, team, stage, mlp_sum, mlp_g, rest_came, grad_attn, came_attn, sums, attn_g,
    held, came,
    loads, us, ur, ys, yr, ws, wr, rs, rr, rxs, rxr, ds, dr, ss, sr, local,
):
    nx, nc, nz, ny = dims
    x, c, z, y = place()
    rows, width = tokens.shape
    own = w_query.shape[0]
    qcols = q.shape[-1]
    pairs = qcols // 128
    keys_span = ny * rows
    ff_span = mlp_g.shape[-1] // (2 * nx)
    fetch_dag = pltpu.make_async_copy(dag, team, loads.at[2])
    fetch = pltpu.make_async_copy(n1g, team, loads.at[2])
    fetch_dag.start()
    mlp_swap = Swap(
        lambda pz, pc: mlp_sum.at[pz, pc], lambda pz, pc: mlp_g.at[pz, pc], us, ur, local.at[0], nz, nc
    )
    dn = Spread(lambda px, py: rest_dn.at[px, py], lambda px, py: rest_came.at[px, py], ws, wr, local.at[1], nx, ny)
    reduce = Reduce(part, held, came, rs, rr, rxs, rxr)
    spread = Spread(
        lambda px, py: grad_attn.at[px, :, :, py], lambda px, py: came_attn.at[px, py], ds, dr, local.at[2], nx, ny
    )
    swap = Swap(lambda pz, pc: sums.at[pz, pc], lambda pz, pc: attn_g.at[pz, pc], ss, sr, local.at[3], nz, nc)

    steps = others(nz, nc) + [(0, 0)]

    def load(i):
        pz, pc = team_peer(steps[i], nz, nc)
        return pltpu.make_async_copy(came_mlp.at[:, :, pc, pz], stage.at[i % 2], loads.at[i % 2])

    load(0).start()
    greet(*dims, cross=True)
    dn.start()
    for i, copy in enumerate(list(mlp_swap.copies()) + [mlp_swap.own()]):
        if i + 1 < len(steps):
            load(i + 1).start()
        load(i).wait()
        pz, pc = team_peer(steps[i], nz, nc)

        def add(at, i=i, pz=pz, pc=pc):
            total = stage[i % 2, 0, 0, at, :].astype(F32)
            for px, py in others(nx, ny):
                total = total + stage[i % 2, px, py, at, :].astype(F32)
            mlp_sum[pz, pc, at, :] = total.astype(BF)

        by_rows(own, add)
        copy.start()
    fetch_dag.wait()

    def project(i, carry):
        weights = w[..., qcols + 128 :].reshape(width, qcols)
        do[i] = nn(team[i].reshape(nc * rows, width), weights).astype(BF).reshape(nc, rows, qcols)
        return carry

    lax.fori_loop(0, nz, project, 0)

    def turned(i, carry):
        pc, pz = i // nz, lax.rem(i, nz)
        at = pl.ds(pl.multiple_of(pz * keys_span, keys_span), keys_span)
        kt[pc, :, at] = kk[pc, at, :].astype(F32).T.astype(BF)
        return carry

    lax.fori_loop(0, nc * nz, turned, 0)

    def attend(pc, carry):
        for pz in reversed(range(nz)):
            keys = (pz + 1) * keys_span
            most = KEYS if nz * keys_span <= KEYS else KEYS // 4
            cuts = [slice(a, min(a + most, keys)) for a in range(0, keys, most)]

            def bias_at(i, cuts=cuts, pz=pz):
                cut = cuts[i]
                return bias_of(tab[pz, pc], cut.stop - cut.start, (pz * ny + y) * rows, cut.start)

            only = bias_at(0) if len(cuts) == 1 else None
            cos, sin = rope_lanes(tab[pz, pc])
            for p in range(pairs):
                q2 = two_heads(q[pz, pc, :, p * 128 : p * 128 + 128])
                do2 = two_heads(do[pz, pc, :, p * 128 : p * 128 + 128])

                def scores(i, cuts=cuts, only=only, bias_at=bias_at, q2=q2, do2=do2, p=p, pz=pz):
                    s = nt(kk[pc, cuts[i], :], q2) + (bias_at(i) if only is None else only)
                    weights = jnp.exp(s - stat[pz, pc, p : p + 1, :])
                    return weights, weights * nt(vv[pc, cuts[i], :], do2)

                delta = sum(jnp.sum(scores(i)[1], axis=0, keepdims=True) for i in range(1, len(cuts)))
                u = 0.0
                for i, cut in enumerate(cuts):
                    weights, dw = scores(i)
                    if i == 0:
                        delta = delta + jnp.sum(dw, axis=0, keepdims=True)
                    score_grad = (dw - weights * delta).astype(BF)
                    dv_new = nn(weights.astype(BF), do2)
                    dk_new = nn(score_grad, q2)
                    if pz == nz - 1 and p == 0:
                        dv[pc, cut, :] = dv_new
                        dk[pc, cut, :] = dk_new
                    else:
                        dv[pc, cut, :] += dv_new
                        dk[pc, cut, :] += dk_new
                    u = u + nn(kt[pc, :, cut], score_grad)
                u = join_heads(u) * (HEAD_DIM ** (-0.5))
                u = u * cos - swap_halves(u) * sin
                dqkv[pz, pc, :, p * 128 : p * 128 + 128] = u.astype(BF)
        return carry

    lax.fori_loop(0, nc, attend, 0)

    def fold(i, carry):
        pc, pz = i // nz, lax.rem(i, nz)
        at = pl.ds(pl.multiple_of(pz * keys_span, keys_span), keys_span)
        key, value = dk[pc, at, :], dv[pc, at, :]
        first = lanes(key.shape) < 64
        both = jnp.where(first, key + pltpu.roll(key, 64, 1), value + pltpu.roll(value, 64, 1))
        both = both.astype(BF)
        for py in range(ny):
            out[pc, py, pz] = both[py * rows : (py + 1) * rows]
        return carry

    lax.fori_loop(0, nc * nz, fold, 0)
    sends = []
    for i, (sy, sc) in enumerate(others(ny, nc)):
        py, pc = lax.rem(y + sy, ny), lax.rem(c + sc, nc)
        sends.append(remote(out.at[pc, py], near.at[i], ys.at[i], yr.at[i], {"y": py, "core": pc}))
    for copy in sends:
        copy.start()

    def weight_grad(left, right, first, last):
        def body(j, carry):
            px, k = j // 4, lax.rem(j, 4)
            size = width // (nx * 4)
            cols = pl.ds(pl.multiple_of(j * size, size), size)
            res = tn(left[:, :, :, cols].reshape(nz * nc * rows, size), right.reshape(nz * nc * rows, last - first))
            grad_attn[px, k // 2, pl.ds(lax.rem(k, 2) * (nz // 2), nz // 2), :, :, first:last] = res.astype(
                BF
            ).reshape(nz // 2, ny, own, last - first)
            return carry

        lax.fori_loop(0, nx * 4, body, 0)

    weight_grad(team, ob[...], qcols + 128, 2 * qcols + 128)
    fetch.start()
    for copy in sends:
        copy.wait_recv()

    def settle_kv(pz, carry):
        total = out[c, y, pz].astype(F32)
        for i in range(len(sends)):
            total = total + near[i, pz].astype(F32)
        cos, sin = rope_lanes(tab[pz, c])
        first = lanes(total.shape) < 64
        total = jnp.where(first, total * cos - swap_halves(total) * sin, total)
        dqkv[pz, c, :, qcols : qcols + 128] = total.astype(BF)
        dqkv[pz, 1 - c, :, qcols : qcols + 128] = jnp.zeros((rows, 128), BF)
        return carry

    lax.fori_loop(0, nz, settle_kv, 0)

    def output(i, carry):
        half, odd = i // 2, lax.rem(i, 2)
        pz = odd * half + (1 - odd) * (nz - 1 - half)
        for px in range(nx):
            cols = slice(px * (width // nx), (px + 1) * (width // nx))
            weights = w[px, :, :, :, :, : qcols + 128].reshape(width // nx, qcols + 128)
            res = nt(dqkv[pz].reshape(nc * rows, qcols + 128), weights)
            part[pz, :, :, cols] = res.astype(BF).reshape(nc, rows, width // nx)
        reduce.across(pz).start()
        return carry

    lax.fori_loop(0, nz, output, 0)

    def own_weights():
        fetch.wait()
        weight_grad(team, dqkv[...], 0, qcols + 128)
        spread.start()

    def unpack_mlp(at):
        gain = gains[at, 1:2]
        dots = jnp.zeros(gain.shape, F32)
        for k, (grad, weight) in enumerate(((grad_gate, w_gate), (grad_up, w_up))):
            for t in range(nz * nc):
                for i in range(nx):
                    chunk = (i * nc + t % nc) * nz + t // nc
                    source = (k * nx + i) * ff_span
                    cols = slice(chunk * ff_span, (chunk + 1) * ff_span)
                    value = mlp_g[t // nc, t % nc, at, source : source + ff_span].astype(F32)
                    grad[at, cols] = value * gain
                    dots = dots + jnp.sum(value * weight[at, cols].astype(F32), axis=-1, keepdims=True)
        grad_gain[at, :] = jnp.broadcast_to(dots, (dots.shape[0], 128))

    def unpack_all():
        mlp_swap.arrived()
        by_rows(own, unpack_mlp)

    def down_all():
        dn.arrived()
        half = width // 2

        def down(at):
            for source, cols in ((came_dn, slice(0, half)), (rest_came, slice(half, width))):
                total = source[0, 0, at, :].astype(F32)
                for px, py in others(nx, ny):
                    total = total + source[px, py, at, :].astype(F32)
                grad_down[at, cols] = total

        by_rows(grad_down.shape[0], down)

    def add_attn(at):
        for pz in range(nz):
            for pc in range(nc):
                total = came_attn[0, 0, pc, pz, at, :].astype(F32)
                for px, py in others(nx, ny):
                    total = total + came_attn[px, py, pc, pz, at, :].astype(F32)
                sums[pz, pc, at, :] = total.astype(BF)

    def exchange():
        spread.arrived()
        by_rows(own, add_attn)
        swap.start()

    def nothing():
        return None

    end = flow(reduce, None, None, [own_weights, unpack_all, nothing, down_all, nothing, exchange])

    def settle(at, total):
        value = tokens[at, :].astype(F32)
        inverse = lax.rsqrt(jnp.mean(value * value, axis=-1, keepdims=True) + EPSILON)
        normed = value * inverse
        input_grad[at, :] = dx2[at, :] + inverse * (
            total - normed * jnp.mean(total * normed, axis=-1, keepdims=True)
        )

    for half in range(PARTS):
        reduce.last(half, settle)
    end()
    swap.arrived()

    def unpack(at):
        gain = gains[at, 0:1]
        dots = jnp.zeros(gain.shape, F32)
        heads = []
        for t in range(nz * nc):
            block = attn_g[t // nc, t % nc, at, :].astype(F32)
            cols = slice(t * qcols, (t + 1) * qcols)
            grad_query[at, cols] = block[:, :qcols] * gain
            dots = dots + jnp.sum(block[:, :qcols] * w_query[at, cols].astype(F32), axis=-1, keepdims=True)
            grad_out_t[at, cols] = block[:, qcols + 128 :]
            if t % (nz * nc // KV_HEADS):
                heads[-1] = heads[-1] + block[:, qcols : qcols + 128]
            else:
                heads.append(block[:, qcols : qcols + 128])
        for pair in range(KV_HEADS // 2):
            one, two = heads[2 * pair], heads[2 * pair + 1]
            first = lanes(one.shape) < 64
            cols = slice(pair * 128, pair * 128 + 128)
            key = jnp.where(first, one, pltpu.roll(two, 64, 1))
            value = jnp.where(first, pltpu.roll(one, 64, 1), two)
            grad_key[at, cols] = key * gain
            grad_value[at, cols] = value * gain
            both = key * w_key[at, cols].astype(F32) + value * w_value[at, cols].astype(F32)
            dots = dots + jnp.sum(both, axis=-1, keepdims=True)
        old = grad_gain[at, :]
        grad_gain[at, :] = jnp.where(lanes(old.shape) < 64, dots, old)

    by_rows(own, unpack)
    for one in (mlp_swap, dn, spread, swap):
        one.finish()
    for copy in sends:
        copy.wait_send()


def backward_call(
    dims, dag, w, tab, q, kk, vv, stat, ob, came_mlp, came_dn, rest_dn, n1g, tokens, dx2, gains,
    w_query, w_key, w_value, w_gate, w_up,
):
    nx, nc, nz, ny = dims
    rows, width = tokens.shape
    own = w_query.shape[0]
    qcols = q.shape[-1]
    keys = nz * ny * rows
    peers, members, near = nx * ny - 1, nz * nc - 1, ny * nc - 1
    cols, mlp_cols = w.shape[-1], came_mlp.shape[-1]
    team_rows = (nz, nc, rows, width)
    return call(
        functools.partial(backward_kernel, dims),
        (
            dag, w, tab, q, kk, vv, stat, ob, came_mlp, came_dn, rest_dn, n1g, tokens, dx2, gains,
            w_query, w_key, w_value, w_gate, w_up,
        ),
        (pl.ANY,) + (VM,) * 7 + (pl.ANY, VM, pl.ANY, pl.ANY) + (VM,) * 8,
        [
            ((rows, width), F32),
            (w_query.shape, F32),
            (w_key.shape, F32),
            (w_value.shape, F32),
            (w_query.shape, F32),
            (w_gate.shape, F32),
            (w_up.shape, F32),
            ((came_dn.shape[2], width), F32),
            ((own, 128), F32),
        ],
        (VM,) * 9,
        [
            VM((nz, nc, rows, qcols), BF),
            VM((nc, 128, keys), BF),
            VM((nc, keys, 128), F32),
            VM((nc, keys, 128), F32),
            VM((nc, ny, nz, rows, 128), BF),
            VM((near, nz, rows, 128), BF),
            VM((nz, nc, rows, qcols + 128), BF),
            VM(team_rows, BF),
            VM(team_rows, BF),
            VM((2, nx, ny, own, mlp_cols), BF),
            VM((nz, nc, own, mlp_cols), BF),
            VM((nz, nc, own, mlp_cols), BF),
            VM(rest_dn.shape, BF),
            VM((nx, nc, nz, ny, own, cols), BF),
            VM((nx, ny, nc, nz, own, cols), BF),
            VM((nz, nc, own, cols), BF),
            VM((nz, nc, own, cols), BF),
        ]
        + Reduce.buffers(nz, rows, width)
        + [DMA((3,))]
        + [DMA((members,))] * 2
        + [DMA((near,))] * 2
        + [DMA((peers,))] * 2
        + Reduce.SEMS
        + [DMA((peers,))] * 2
        + [DMA((members,))] * 2
        + [DMA((4,))],
        6,
    )


def shards(
    tokens, positions, doc_start, cotangent, w_query, w_key, w_value, w_out,
    attn_gain, w_gate, w_up, w_down, mlp_gain,
):
    dims = tuple(lax.axis_size(a) for a in ALL)
    rows = tokens.shape[0]

    gains = jnp.stack([attn_gain, mlp_gain], axis=1).astype(F32)
    half = HEAD_DIM // 2
    frequency = 10000.0 ** (-2.0 * jnp.arange(half, dtype=F32) / HEAD_DIM)
    angles = positions.astype(F32)[:, None] * frequency[None, :]
    table = jnp.concatenate(
        [
            jnp.cos(angles),
            jnp.sin(angles),
            jnp.broadcast_to(doc_start.astype(F32)[:, None], (rows, HEAD_DIM)),
        ],
        axis=-1,
    )
    n1g, w_attn, tab, q, kk, vv, stat, ob, mid, n2g, cotg, w_mlp, w_dn = forward_call(
        dims, tokens, table, gains, w_query, w_key, w_value, w_out.T, w_gate, w_up, w_down, cotangent
    )
    dx2, dag, output, came_mlp, came_dn, rest_dn = mlp_call(dims, n2g, cotg, w_mlp, w_dn, mid, cotangent)
    (
        input_grad, grad_query, grad_key, grad_value, grad_out_t, grad_gate, grad_up, grad_down, grad_gain
    ) = backward_call(
        dims, dag, w_attn, tab, q, kk, vv, stat, ob, came_mlp, came_dn, rest_dn, n1g, tokens, dx2, gains,
        w_query, w_key, w_value, w_gate, w_up,
    )
    return (
        output, input_grad, grad_query, grad_key, grad_value, grad_out_t.T, grad_gain[:, 0],
        grad_gate, grad_up, grad_down, grad_gain[:, 64],
    )


def solution(mesh):
    fsdp, seq = mesh.shape["fsdp"], mesh.shape["seq"]
    nc, nz = 2, 4
    grid = Mesh(mesh.devices.reshape(fsdp // nc, nc, nz, seq // nz), ALL)
    row, col, vec = P(ALL, None), P(None, ALL), P(ALL)
    in_specs = (row, vec, vec, row, row, row, row, col, vec, row, row, row, vec)
    out_specs = (row, row, row, row, row, col, vec, row, row, row, vec)
    return jax.shard_map(shards, mesh=grid, in_specs=in_specs, out_specs=out_specs, check_vma=False)
```

time: 503 us -> 420 us (0.83)
  the two profiles are of different devices: /device:TPU:0 before, /device:TPU:31 now
where the time goes in v5:
time: 420 us; the launch traced here: 413 us
  Pallas kernels  397 us (95%)
  local copies, waits for them, and re-layouts  11 us (3%)
    pallas_call x3, Pallas kernels, call(): pl.pallas_call(kernel, out_shape=[jax.ShapeDtypeStruct(s, t) for s, t in...  397 us
    unnamed x25, local copies, waits for them, and re-layouts  9.26 us

profile of v5, /device:TPU:31, one launch (start us, length us, event | category | flops | bytes accessed | tf_op | source)
XLA Modules:
  0.0 412.7 jit_solution(10887606342968043651)
XLA Ops:
  0.6 0.7 convert_element_type.9
  1.3 0.7 convert_element_type.10
  2.0 0.7 pad_maximum_fusion.1
  2.6 0.1 copy.30
  2.8 0.6 convert_element_type.11.gains
  3.4 0.1 broadcast_in_dim.2
  3.5 0.3 multiply_cosine_fusion
  3.8 0.7 pad_maximum_fusion.table
  4.5 179.4 %shard_map.212 = (bf16[4,2,128,2048]{3,2,1,0:T(8,128)(2,1)}, bf16[2,2,4,2,64,640]{5,4,3,2,1,0:T(8,128)(2,1)}, f32[4,2,128,128]{3,2,1,0:T(8,128)}, bf16[4,2,128,2...) custom-call(bf16[128,2048]{1,0:T(8,128)(2,1)} %tokens.3, ...), custom_call_target="tpu_custom_call" | custom-call | tf_op jit(solution)/shard_map/pallas_call | solution.py:326
  183.9 119.0 %shard_map.213 = (f32[128,2048]{1,0:T(8,128)}, bf16[4,2,128,2048]{3,2,1,0:T(8,128)(2,1)}, bf16[128,2048]{1,0:T(8,128)(2,1)}, bf16[2,2,2,4,64,1408]{5,4,3,2,1,0:T...) custom-call(bf16[4,2,128,2048]{3,2,1,0:T(8,128)(2,1)} %get-tuple-element.39.n2g, ...), custom_call_target="tpu_custom_call" | custom-call | tf_op jit(solution)/shard_map/pallas_call | solution.py:326
  302.9 0.0 copy-start.3
  302.9 98.5 %shard_map.214 = (f32[128,2048]{1,0:T(8,128)}, f32[64,2048]{1,0:T(8,128)}, f32[64,256]{1,0:T(8,128)}, f32[64,256]{1,0:T(8,128)}, f32[64,2048]{1,0:T(8,128)}, /*i...) custom-call(bf16[4,2,128,2048]{3,2,1,0:T(8,128)(2,1)} %get-tuple-element.45.dag, ...), custom_call_target="tpu_custom_call" | custom-call | tf_op jit(solution)/shard_map/pallas_call | solution.py:326
  401.4 0.0 copy-start.5
  401.4 0.0 copy-start.7
  401.4 0.0 copy-start.6
  401.4 0.0 copy-start.4
  401.4 1.6 slice_reduce_fusion
  403.0 0.0 copy-done.3
  403.0 0.0 copy-start.2
  403.0 0.8 copy.40
  403.8 2.3 copy.41
  406.1 0.0 copy-done.5
  406.1 0.0 copy-start.1
  406.1 0.8 copy.42
  406.9 0.0 copy-done.7
  406.9 0.6 copy.43
  407.5 0.0 copy-done.6
  407.5 0.6 copy.44
  408.2 0.0 copy-done.4
  408.2 0.8 copy.45
  409.0 0.0 copy-done.2
  409.0 0.0 copy-start
  409.0 1.1 copy.46
  410.1 0.0 copy-done.1
  410.1 1.1 copy.47
  411.2 0.0 copy-done
  411.2 1.1 copy.48
  (1 shorter events, 0.0 us)
Async XLA Ops:
  302.9 100.1 %copy-start.3 = (bf16[128,2048]{1,0:T(8,128)(2,1)S(1)}, bf16[128,2048]{1,0:T(8,128)(2,1)}, u32[]{:S(2)}) copy-start(bf16[128,2048]{1,0:T(8,128)(2,1)} %get-tuple-element.82) | copy-start | bytes 1572868
  401.4 4.7 %copy-start.5 = (f32[64,2048]{1,0:T(8,128)S(1)}, f32[64,2048]{1,0:T(8,128)}, u32[]{:S(2)}) copy-start(f32[64,2048]{1,0:T(8,128)} %get-tuple-element.84) | copy-start | bytes 1572868
  401.4 5.5 %copy-start.7 = (f32[64,256]{1,0:T(8,128)S(1)}, f32[64,256]{1,0:T(8,128)}, u32[]{:S(2)}) copy-start(f32[64,256]{1,0:T(8,128)} %get-tuple-element.85) | copy-start | bytes 196612
  401.4 6.1 %copy-start.6 = (f32[64,256]{1,0:T(8,128)S(1)}, f32[64,256]{1,0:T(8,128)}, u32[]{:S(2)}) copy-start(f32[64,256]{1,0:T(8,128)} %get-tuple-element.86) | copy-start | bytes 196612
  401.4 6.7 %copy-start.4 = (f32[64,2048]{1,0:T(8,128)S(1)}, f32[64,2048]{1,0:T(8,128)}, u32[]{:S(2)}) copy-start(f32[64,2048]{1,0:T(8,128)} %get-tuple-element.62) | copy-start | bytes 1572868
  403.0 6.0 %copy-start.2 = (f32[64,5632]{1,0:T(8,128)S(1)}, f32[64,5632]{1,0:T(8,128)}, u32[]{:S(2)}) copy-start(f32[64,5632]{1,0:T(8,128)} %get-tuple-element.89) | copy-start | bytes 4325380
  406.1 4.0 copy-start.1
  409.0 2.2 copy-start

commit v6 on v5

--- a/solution.py
+++ b/solution.py
@@ -60,7 +60,11 @@
     for step in others(nz, nc):
         pz, pc = team_peer(step, nz, nc)
         pl.semaphore_signal(barrier, inc=1, device_id={"z": pz, "core": pc}, device_id_type=MESH)
-    pl.semaphore_wait(barrier, nx * ny - 1 + nz * nc - 1 + extra)
+
+    def met():
+        pl.semaphore_wait(barrier, nx * ny - 1 + nz * nc - 1 + extra)
+
+    return met
 
 
 def remote(source, target, send, recv, device):
@@ -190,6 +194,16 @@
     return rows
 
 
+def by_need(nz, z, k):
+    last = nz - 1
+    value = 0
+    for at in range(nz):
+        when = {to: at + last - to if to > at else last - at + to for to in range(nz) if to != at}
+        blocks = sorted(when, key=lambda to: (when[to], to)) + [at]
+        value = jnp.where(z == at, blocks[k], value)
+    return value
+
+
 def flow(reduce, gather, before=None, work=()):
     work = list(work)
     any_one = reduce or gather
@@ -235,7 +249,7 @@
                         pl.when(z == (e if way == 0 else nz - 1 - e))(
                             functools.partial(step, way, e, op[0], op[1], part)
                         )
-            if work:
+            if work and (t > 0 or part == PARTS - 1):
                 work.pop(0)()
     for item in work:
         item()
@@ -275,6 +289,11 @@
         for copy in self.copies():
             copy.start()
         self.own().start()
+
+    def start_some(self, first, last):
+        for i, copy in enumerate(self.copies()):
+            if first <= i < last:
+                copy.start()
 
     def start_along(self, far):
         for step, copy in zip(others(self.nx, self.ny), self.copies()):
@@ -400,8 +419,8 @@
 
 def forward_kernel(
     dims, tokens, table, gains, w_query, w_key, w_value, w_out_t, w_gate, w_up, down, cot,
-    n1g, w_attn, tab, q, kk, vv, stat, ob, mid, n2g, cotg, w_mlp, w_dn,
-    n1, blocks, mlp_blocks, mlp_t, kv, vt, part, held, came, n2,
+    n1_out, w_out, tab, q, kk, vv, stat, ob, mid, n2g, cotg, w_mlp, w_dn,
+    n1g, w_attn, n1, blocks, mlp_blocks, mlp_t, kv, vt, part, held, came, n2,
     gs, gr, gl, ts, tr, ss, sr, ds, dr, ws, wr, us, ur, ys, yr, rs, rr, rxs, rxr, cs, cr, cl, ns, nr, nl, ms, mr, local,
 ):
     nx, nc, nz, ny = dims
@@ -425,7 +444,7 @@
     reduce = Reduce(part, held, came, rs, rr, rxs, rxr)
     cots = Gather(cot, cotg, cs, cr, cl)
     next_rows = Gather(n2, n2g, ns, nr, nl)
-    greet(*dims)
+    met = greet(*dims)
 
     def pack(at):
         gain = gains[at, 0:1]
@@ -446,17 +465,17 @@
                     t = (pair * 2 + k) * (nz * nc // KV_HEADS) + rep
                     blocks[t // nc, t % nc, at, qcols : qcols + 128] = both[k].astype(BF)
 
-    by_rows(own, pack)
-    swap.start()
-    tabs.start()
-    dn.start()
-
     def norm(at):
         value = tokens[at, :].astype(F32)
         inverse = lax.rsqrt(jnp.mean(value * value, axis=-1, keepdims=True) + EPSILON)
         n1[at, :] = (value * inverse).astype(BF)
 
     by_rows(rows, norm)
+    by_rows(own, pack)
+    met()
+    swap.start()
+    tabs.start()
+    dn.start()
 
     def spread_copies():
         for i, step in enumerate(others(nx, ny)):
@@ -482,30 +501,39 @@
     end = flow(None, first_rows, None, [spread, lambda: by_rows(own, pack_mlp)])
     end()
     mlp_swap.start()
+    keep_rows = pltpu.make_async_copy(n1g, n1_out, local.at[5])
+    keep_rows.start()
     tabs.arrived()
     for copy in spread_copies():
         copy.wait_recv()
-
-    def project(i, carry):
-        res = nn(n1g[i].reshape(nc * rows, width), w_attn[..., : qcols + 128].reshape(width, qcols + 128))
+    keep_weights = pltpu.make_async_copy(w_attn, w_out, local.at[6])
+    keep_weights.start()
+
+    def project_kv(i, carry):
+        u = nn(n1g[i].reshape(nc * rows, width), w_attn[..., qcols : qcols + 128].reshape(width, 128))
+        cos, sin = rope_lanes(tab[i].reshape(nc * rows, 128))
+        u = jnp.where(lanes(u.shape) < 64, u * cos + swap_halves(u) * sin, u).astype(BF)
+        for pc in range(nc):
+            kv[pc, i, y] = u[pc * rows : (pc + 1) * rows]
+        return carry
+
+    def project_q(i, carry):
+        res = nn(n1g[i].reshape(nc * rows, width), w_attn[..., :qcols].reshape(width, qcols))
         cos, sin = rope_lanes(tab[i].reshape(nc * rows, 128))
         for p in range(pairs):
             u = res[:, p * 128 : p * 128 + 128]
             u = (u * cos + swap_halves(u) * sin) * (HEAD_DIM ** (-0.5))
             q[i, :, :, p * 128 : p * 128 + 128] = u.astype(BF).reshape(nc, rows, 128)
-        u = res[:, qcols : qcols + 128]
-        u = jnp.where(lanes(u.shape) < 64, u * cos + swap_halves(u) * sin, u).astype(BF)
-        for pc in range(nc):
-            kv[pc, i, y] = u[pc * rows : (pc + 1) * rows]
         return carry
 
-    lax.fori_loop(0, nz, project, 0)
+    lax.fori_loop(0, nz, project_kv, 0)
     sends = []
     for i in range(ny - 1):
         slot = kv.at[:, :, y]
         sends.append(remote(slot, slot, ys.at[i], yr.at[i], {"y": lax.rem(y + 1 + i, ny)}))
     for copy in sends:
         copy.start()
+    lax.fori_loop(0, nz, project_q, 0)
     for copy in sends:
         copy.wait_recv()
 
@@ -569,6 +597,8 @@
     end3 = flow(None, next_rows, lambda half: reduce.last(half, settle))
     end3()
     end2()
+    keep_rows.wait()
+    keep_weights.wait()
     gu.arrived()
     dn.arrived()
     for one in (swap, tabs, mlp_swap, gu, dn):
@@ -606,8 +636,10 @@
             ((nx, nc, nz, ny, own, mlp_cols), BF),
             ((nx, ny) + down.shape, BF),
         ],
-        (VM,) * 9 + (pl.ANY,) * 4,
+        (pl.ANY,) * 2 + (VM,) * 7 + (pl.ANY,) * 4,
         [
+            VM(team_rows, BF),
+            VM((nx, nc, nz, ny, own, cols), BF),
             VM((rows, width), BF),
             VM((nz, nc, own, cols), BF),
             VM((nz, nc, own, mlp_cols), BF),
@@ -626,17 +658,17 @@
         + Reduce.SEMS
         + Gather.SEMS * 2
         + [DMA((peers,))] * 2
-        + [DMA((5,))],
+        + [DMA((7,))],
         1,
     )
 
 
 def mlp_kernel(
     dims, n2g, cotg, w_mlp, w_dn, mid, cot,
-    dx2, dag, output, came_mlp, came_dn, rest_dn,
-    n2v, cotv, wv, wd, hid, hid_t, dmlp, part, mlp_out, grad_mlp, grad_dn,
+    dx2, dag, output, came_mlp, grad_dn,
+    n2v, cotv, wv, wd, hid, hid_t, dmlp, part, mlp_out, grad_mlp,
     held, came, held2, came2, low,
-    loads, rs, rr, rxs, rxr, os, orr, oxs, oxr, ds, dr, dl, ms, mr, ws, wr, local,
+    loads, rs, rr, rxs, rxr, os, orr, oxs, oxr, ds, dr, dl, ms, mr, local,
 ):
     nx, nc, nz, ny = dims
     x, c, z, y = place()
@@ -653,21 +685,18 @@
         source, target = ((n2g, n2v), (cotg, cotv))[k]
         return pltpu.make_async_copy(source.at[at], target.at[at], loads.at[2 + k * nz + at])
 
-    order = [a for k in range(nz) for a in (nz - 1 - k, k)][:nz]
     for k in range(nz):
-        fetch(order[k], 0).start()
+        fetch(by_need(nz, z, k), 0).start()
         if k == 0:
             fetch_d.start()
-        fetch(order[k], 1).start()
-    greet(*dims)
+        fetch(by_need(nz, z, k), 1).start()
+    met = greet(*dims)
     reduce = Reduce(part, held, came, rs, rr, rxs, rxr)
     reduce2 = Reduce(mlp_out, held2, came2, os, orr, oxs, oxr)
     into = Gather(low, dag, ds, dr, dl)
     gu = Spread(
         lambda px, py: grad_mlp.at[px, :, :, py], lambda px, py: came_mlp.at[px, py], ms, mr, local.at[0], nx, ny
     )
-    dn = Spread(lambda px, py: grad_dn.at[px, py], lambda px, py: came_dn.at[px, py], ws, wr, local.at[1], nx, ny)
-    half_width = width // 2
 
     def down_rows(cols):
         if piece % ROWS:
@@ -679,10 +708,8 @@
 
     fetch_w.wait()
 
-    def forward_back(k, carry):
-        half = k // 2
-        odd = lax.rem(k, 2)
-        at = odd * half + (1 - odd) * (nz - 1 - half)
+    def forward_back(k):
+        at = by_need(nz, z, k)
         fetch(at, 0).wait()
         u = nn(n2v[at].reshape(block, width), wv[...].reshape(width, ff2))
         gt, up = u[:, :ff], u[:, ff:]
@@ -691,7 +718,8 @@
         value = (silu * up).astype(BF)
         hid[at] = value
         hid_t[:, pl.ds(pl.multiple_of(at * block, block), block)] = value.astype(F32).T.astype(BF)
-        pl.when(k == 0)(fetch_d.wait)
+        if k == 0:
+            fetch_d.wait()
         fetch(at, 1).wait()
         dh = nt(cotv[at].reshape(block, width), down_rows(slice(None)))
         dgt = dh * up * sg * (1.0 + gt * (1.0 - sg))
@@ -701,24 +729,21 @@
             cols = slice(px * (width // nx), (px + 1) * (width // nx))
             res = nt(dmlp[at], weights(px))
             part[at, :, :, cols] = res.astype(BF).reshape(nc, rows, width // nx)
+        if k == 0:
+            met()
         reduce.across(at).start()
+
+    forward_back(0)
+    chunk = width // 4
+
+    def down_grad(n, carry):
+        cols = pl.ds(pl.multiple_of(n * chunk, chunk), chunk)
+        res = nn(hid_t[...], cotv[:, :, :, cols].reshape(nz * block, chunk)).astype(BF)
+        for px in range(nx):
+            for py in range(ny):
+                k = (px * ny + py) * piece
+                grad_dn[px, py, :, cols] = res[k : k + piece]
         return carry
-
-    lax.fori_loop(0, 2, forward_back, 0)
-    chunk = width // 4
-
-    def down_grad(part_of, target):
-        def body(n, carry):
-            at = pl.ds(pl.multiple_of(n * chunk, chunk), chunk)
-            cols = pl.ds(pl.multiple_of(part_of * half_width + n * chunk, chunk), chunk)
-            res = nn(hid_t[...], cotv[:, :, :, cols].reshape(nz * block, chunk)).astype(BF)
-            for px in range(nx):
-                for py in range(ny):
-                    k = (px * ny + py) * piece
-                    target[px, py, :, at] = res[k : k + piece]
-            return carry
-
-        lax.fori_loop(0, 2, body, 0)
 
     def mlp_grad(far):
         px = lax.rem(x + far, nx)
@@ -743,24 +768,18 @@
         return carry
 
     def down_first():
-        down_grad(0, grad_dn)
-        dn.start()
+        lax.fori_loop(0, 2, down_grad, 0)
 
     def down_second():
-        down_grad(1, rest_dn)
+        lax.fori_loop(2, 4, down_grad, 0)
 
     def sum_all():
         lax.fori_loop(0, 4, mlp_sum, 0)
         reduce2.start()
 
-    def more():
-        lax.fori_loop(2, 3, forward_back, 0)
-
-    def most():
-        lax.fori_loop(3, nz, forward_back, 0)
-
-    work = [more, most] + [functools.partial(mlp_grad, far) for far in reversed(range(nx))]
-    end = flow(reduce, None, None, work + [down_first, down_second, sum_all])
+    work = [functools.partial(forward_back, k) for k in range(1, nz)]
+    work += [functools.partial(mlp_grad, far) for far in reversed(range(nx))]
+    end = flow(reduce, None, None, work + [sum_all])
 
     def settle(at, total):
         value = mid[at, :]
@@ -772,7 +791,7 @@
         dx2[at, :] = gradient
         low[at, :] = gradient.astype(BF)
 
-    end2 = flow(reduce2, into, lambda part: reduce.last(part, settle))
+    end2 = flow(reduce2, into, lambda part: reduce.last(part, settle), [down_first, down_second])
 
     def finish(at, total):
         output[at, :] = (mid[at, :] + total).astype(BF)
@@ -782,9 +801,7 @@
     end2()
     end()
     gu.arrived()
-    dn.arrived()
     gu.finish()
-    dn.finish()
 
 
 def mlp_call(dims, n2g, cotg, w_mlp, w_dn, mid, cot):
@@ -793,7 +810,6 @@
     own, ff2 = w_mlp.shape[4:]
     block = nc * rows
     peers = nx * ny - 1
-    half_dn = w_dn.shape[:3] + (width // 2,)
     return call(
         functools.partial(mlp_kernel, dims),
         (n2g, cotg, w_mlp, w_dn, mid, cot),
@@ -803,10 +819,9 @@
             ((nz, nc, rows, width), BF),
             ((rows, width), BF),
             ((nx, ny, nc, nz, own, ff2), BF),
-            (half_dn, BF),
-            (half_dn, BF),
+            (w_dn.shape, BF),
         ],
-        (VM, pl.ANY, VM, pl.ANY, pl.ANY, VM),
+        (VM, pl.ANY, VM, pl.ANY, VM),
         [
             VM(n2g.shape, BF),
             VM(cotg.shape, BF),
@@ -818,46 +833,48 @@
             VM(n2g.shape, BF),
             VM(n2g.shape, BF),
             VM(w_mlp.shape, BF),
-            VM(half_dn, BF),
         ]
         + Reduce.buffers(nz, rows, width) * 2
         + [VM((rows, width), BF), DMA((2 + 2 * nz,))]
         + Reduce.SEMS * 2
         + Gather.SEMS
-        + [DMA((peers,))] * 4
-        + [DMA((2,))],
+        + [DMA((peers,))] * 2
+        + [DMA((1,))],
         3,
     )
 
 
 def backward_kernel(
-    dims, dag, w, tab, q, kk, vv, stat, ob, came_mlp, came_dn, rest_dn, n1g, tokens, dx2, gains,
-    w_query, w_key, w_value, w_gate, w_up,
-    input_grad, grad_query, grad_key, grad_value, grad_out_t, grad_gate, grad_up, grad_down, grad_gain,
-    do, kt, dk, dv, out, near, dqkv, part, team, stage, mlp_sum, mlp_g, rest_came, grad_attn, came_attn, sums, attn_g,
+    dims, dag, w, tab, q, kk, vv, stat, ob, came_mlp, grad_dn, n1g,
+    dn1, raw_gate, raw_up, came_dn, own_o, own_p,
+    do, kt, dk, dv, out, near, dqkv, part, team, stage, mlp_sum, mlp_g,
+    grad_o, came_o, sums_o, grad_p, came_p, sums_p,
     held, came,
-    loads, us, ur, ys, yr, ws, wr, rs, rr, rxs, rxr, ds, dr, ss, sr, local,
+    loads, us, ur, ys, yr, ws, wr, rs, rr, rxs, rxr, ds, dr, ss, sr, es, er, fs, fr, local,
 ):
     nx, nc, nz, ny = dims
     x, c, z, y = place()
-    rows, width = tokens.shape
-    own = w_query.shape[0]
+    rows, width = dn1.shape
+    own = grad_o.shape[4]
     qcols = q.shape[-1]
     pairs = qcols // 128
     keys_span = ny * rows
-    ff_span = mlp_g.shape[-1] // (2 * nx)
     fetch_dag = pltpu.make_async_copy(dag, team, loads.at[2])
     fetch = pltpu.make_async_copy(n1g, team, loads.at[2])
     fetch_dag.start()
     mlp_swap = Swap(
         lambda pz, pc: mlp_sum.at[pz, pc], lambda pz, pc: mlp_g.at[pz, pc], us, ur, local.at[0], nz, nc
     )
-    dn = Spread(lambda px, py: rest_dn.at[px, py], lambda px, py: rest_came.at[px, py], ws, wr, local.at[1], nx, ny)
+    dn = Spread(lambda px, py: grad_dn.at[px, py], lambda px, py: came_dn.at[px, py], ws, wr, local.at[1], nx, ny)
     reduce = Reduce(part, held, came, rs, rr, rxs, rxr)
-    spread = Spread(
-        lambda px, py: grad_attn.at[px, :, :, py], lambda px, py: came_attn.at[px, py], ds, dr, local.at[2], nx, ny
-    )
-    swap = Swap(lambda pz, pc: sums.at[pz, pc], lambda pz, pc: attn_g.at[pz, pc], ss, sr, local.at[3], nz, nc)
+    spread_o = Spread(
+        lambda px, py: grad_o.at[px, :, :, py], lambda px, py: came_o.at[px, py], ds, dr, local.at[2], nx, ny
+    )
+    swap_o = Swap(lambda pz, pc: sums_o.at[pz, pc], lambda pz, pc: own_o.at[pz, pc], ss, sr, local.at[3], nz, nc)
+    spread_p = Spread(
+        lambda px, py: grad_p.at[px, :, :, py], lambda px, py: came_p.at[px, py], es, er, local.at[4], nx, ny
+    )
+    swap_p = Swap(lambda pz, pc: sums_p.at[pz, pc], lambda pz, pc: own_p.at[pz, pc], fs, fr, local.at[5], nz, nc)
 
     steps = others(nz, nc) + [(0, 0)]
 
@@ -866,8 +883,16 @@
         return pltpu.make_async_copy(came_mlp.at[:, :, pc, pz], stage.at[i % 2], loads.at[i % 2])
 
     load(0).start()
-    greet(*dims, cross=True)
-    dn.start()
+    met = greet(*dims, cross=True)
+
+    def turned(i, carry):
+        pc, pz = i // nz, lax.rem(i, nz)
+        at = pl.ds(pl.multiple_of(pz * keys_span, keys_span), keys_span)
+        kt[pc, :, at] = kk[pc, at, :].astype(F32).T.astype(BF)
+        return carry
+
+    lax.fori_loop(0, nc * nz, turned, 0)
+    early = 2 * (nx * ny - 1) // 3
     for i, copy in enumerate(list(mlp_swap.copies()) + [mlp_swap.own()]):
         if i + 1 < len(steps):
             load(i + 1).start()
@@ -881,6 +906,10 @@
             mlp_sum[pz, pc, at, :] = total.astype(BF)
 
         by_rows(own, add)
+        if i == 0:
+            met()
+            dn.start_some(0, early)
+            dn.own().start()
         copy.start()
     fetch_dag.wait()
 
@@ -890,14 +919,6 @@
         return carry
 
     lax.fori_loop(0, nz, project, 0)
-
-    def turned(i, carry):
-        pc, pz = i // nz, lax.rem(i, nz)
-        at = pl.ds(pl.multiple_of(pz * keys_span, keys_span), keys_span)
-        kt[pc, :, at] = kk[pc, at, :].astype(F32).T.astype(BF)
-        return carry
-
-    lax.fori_loop(0, nc * nz, turned, 0)
 
     def attend(pc, carry):
         for pz in reversed(range(nz)):
@@ -962,23 +983,24 @@
     for copy in sends:
         copy.start()
 
-    def weight_grad(left, right, first, last):
+    def weight_grad(right, target):
         def body(j, carry):
             px, k = j // 4, lax.rem(j, 4)
             size = width // (nx * 4)
             cols = pl.ds(pl.multiple_of(j * size, size), size)
-            res = tn(left[:, :, :, cols].reshape(nz * nc * rows, size), right.reshape(nz * nc * rows, last - first))
-            grad_attn[px, k // 2, pl.ds(lax.rem(k, 2) * (nz // 2), nz // 2), :, :, first:last] = res.astype(
-                BF
-            ).reshape(nz // 2, ny, own, last - first)
+            res = tn(team[:, :, :, cols].reshape(nz * nc * rows, size), right.reshape(nz * nc * rows, -1))
+            target[px, k // 2, pl.ds(lax.rem(k, 2) * (nz // 2), nz // 2)] = res.astype(BF).reshape(
+                nz // 2, ny, own, -1
+            )
             return carry
 
         lax.fori_loop(0, nx * 4, body, 0)
 
-    weight_grad(team, ob[...], qcols + 128, 2 * qcols + 128)
+    weight_grad(ob[...], grad_o)
     fetch.start()
     for copy in sends:
         copy.wait_recv()
+    spread_o.start()
 
     def settle_kv(pz, carry):
         total = out[c, y, pz].astype(F32)
@@ -1008,136 +1030,83 @@
 
     def own_weights():
         fetch.wait()
-        weight_grad(team, dqkv[...], 0, qcols + 128)
-        spread.start()
+        weight_grad(dqkv[...], grad_p)
+        spread_p.start()
 
     def unpack_mlp(at):
-        gain = gains[at, 1:2]
-        dots = jnp.zeros(gain.shape, F32)
-        for k, (grad, weight) in enumerate(((grad_gate, w_gate), (grad_up, w_up))):
+        span = mlp_g.shape[-1] // (2 * nx)
+        for k, raw in enumerate((raw_gate, raw_up)):
             for t in range(nz * nc):
                 for i in range(nx):
                     chunk = (i * nc + t % nc) * nz + t // nc
-                    source = (k * nx + i) * ff_span
-                    cols = slice(chunk * ff_span, (chunk + 1) * ff_span)
-                    value = mlp_g[t // nc, t % nc, at, source : source + ff_span].astype(F32)
-                    grad[at, cols] = value * gain
-                    dots = dots + jnp.sum(value * weight[at, cols].astype(F32), axis=-1, keepdims=True)
-        grad_gain[at, :] = jnp.broadcast_to(dots, (dots.shape[0], 128))
+                    piece = mlp_g[t // nc, t % nc, at, (k * nx + i) * span : (k * nx + i + 1) * span]
+                    raw[at, chunk * span : (chunk + 1) * span] = piece
 
     def unpack_all():
         mlp_swap.arrived()
         by_rows(own, unpack_mlp)
 
-    def down_all():
-        dn.arrived()
-        half = width // 2
-
-        def down(at):
-            for source, cols in ((came_dn, slice(0, half)), (rest_came, slice(half, width))):
-                total = source[0, 0, at, :].astype(F32)
-                for px, py in others(nx, ny):
-                    total = total + source[px, py, at, :].astype(F32)
-                grad_down[at, cols] = total
-
-        by_rows(grad_down.shape[0], down)
-
-    def add_attn(at):
-        for pz in range(nz):
-            for pc in range(nc):
-                total = came_attn[0, 0, pc, pz, at, :].astype(F32)
-                for px, py in others(nx, ny):
-                    total = total + came_attn[px, py, pc, pz, at, :].astype(F32)
-                sums[pz, pc, at, :] = total.astype(BF)
-
-    def exchange():
+    def down_rest():
+        dn.start_some(early, nx * ny - 1)
+
+    def exchange(spread, arrived, sums, swap):
         spread.arrived()
-        by_rows(own, add_attn)
+
+        def add(at):
+            for pz in range(nz):
+                for pc in range(nc):
+                    total = arrived[0, 0, pc, pz, at, :].astype(F32)
+                    for px, py in others(nx, ny):
+                        total = total + arrived[px, py, pc, pz, at, :].astype(F32)
+                    sums[pz, pc, at, :] = total.astype(BF)
+
+        by_rows(own, add)
         swap.start()
 
-    def nothing():
-        return None
-
-    end = flow(reduce, None, None, [own_weights, unpack_all, nothing, down_all, nothing, exchange])
+    work = [
+        own_weights,
+        unpack_all,
+        down_rest,
+        functools.partial(exchange, spread_o, came_o, sums_o, swap_o),
+        functools.partial(exchange, spread_p, came_p, sums_p, swap_p),
+    ]
+    end = flow(reduce, None, None, work)
 
     def settle(at, total):
-        value = tokens[at, :].astype(F32)
-        inverse = lax.rsqrt(jnp.mean(value * value, axis=-1, keepdims=True) + EPSILON)
-        normed = value * inverse
-        input_grad[at, :] = dx2[at, :] + inverse * (
-            total - normed * jnp.mean(total * normed, axis=-1, keepdims=True)
-        )
+        dn1[at, :] = total
 
     for half in range(PARTS):
         reduce.last(half, settle)
     end()
-    swap.arrived()
-
-    def unpack(at):
-        gain = gains[at, 0:1]
-        dots = jnp.zeros(gain.shape, F32)
-        heads = []
-        for t in range(nz * nc):
-            block = attn_g[t // nc, t % nc, at, :].astype(F32)
-            cols = slice(t * qcols, (t + 1) * qcols)
-            grad_query[at, cols] = block[:, :qcols] * gain
-            dots = dots + jnp.sum(block[:, :qcols] * w_query[at, cols].astype(F32), axis=-1, keepdims=True)
-            grad_out_t[at, cols] = block[:, qcols + 128 :]
-            if t % (nz * nc // KV_HEADS):
-                heads[-1] = heads[-1] + block[:, qcols : qcols + 128]
-            else:
-                heads.append(block[:, qcols : qcols + 128])
-        for pair in range(KV_HEADS // 2):
-            one, two = heads[2 * pair], heads[2 * pair + 1]
-            first = lanes(one.shape) < 64
-            cols = slice(pair * 128, pair * 128 + 128)
-            key = jnp.where(first, one, pltpu.roll(two, 64, 1))
-            value = jnp.where(first, pltpu.roll(one, 64, 1), two)
-            grad_key[at, cols] = key * gain
-            grad_value[at, cols] = value * gain
-            both = key * w_key[at, cols].astype(F32) + value * w_value[at, cols].astype(F32)
-            dots = dots + jnp.sum(both, axis=-1, keepdims=True)
-        old = grad_gain[at, :]
-        grad_gain[at, :] = jnp.where(lanes(old.shape) < 64, dots, old)
-
-    by_rows(own, unpack)
-    for one in (mlp_swap, dn, spread, swap):
+    for one in (dn, swap_o, swap_p):
+        one.arrived()
+    for one in (mlp_swap, dn, spread_o, swap_o, spread_p, swap_p):
         one.finish()
     for copy in sends:
         copy.wait_send()
 
 
-def backward_call(
-    dims, dag, w, tab, q, kk, vv, stat, ob, came_mlp, came_dn, rest_dn, n1g, tokens, dx2, gains,
-    w_query, w_key, w_value, w_gate, w_up,
-):
+def backward_call(dims, dag, w, tab, q, kk, vv, stat, ob, came_mlp, grad_dn, n1g):
     nx, nc, nz, ny = dims
-    rows, width = tokens.shape
-    own = w_query.shape[0]
+    rows, width = dag.shape[2:]
+    own, mlp_cols = came_mlp.shape[4:]
     qcols = q.shape[-1]
     keys = nz * ny * rows
     peers, members, near = nx * ny - 1, nz * nc - 1, ny * nc - 1
-    cols, mlp_cols = w.shape[-1], came_mlp.shape[-1]
     team_rows = (nz, nc, rows, width)
     return call(
         functools.partial(backward_kernel, dims),
-        (
-            dag, w, tab, q, kk, vv, stat, ob, came_mlp, came_dn, rest_dn, n1g, tokens, dx2, gains,
-            w_query, w_key, w_value, w_gate, w_up,
-        ),
-        (pl.ANY,) + (VM,) * 7 + (pl.ANY, VM, pl.ANY, pl.ANY) + (VM,) * 8,
+        (dag, w, tab, q, kk, vv, stat, ob, came_mlp, grad_dn, n1g),
+        (pl.ANY,) + (VM,) * 7 + (pl.ANY,) * 3,
         [
             ((rows, width), F32),
-            (w_query.shape, F32),
-            (w_key.shape, F32),
-            (w_value.shape, F32),
-            (w_query.shape, F32),
-            (w_gate.shape, F32),
-            (w_up.shape, F32),
-            ((came_dn.shape[2], width), F32),
-            ((own, 128), F32),
+            ((own, mlp_cols // 2 * nz * nc), BF),
+            ((own, mlp_cols // 2 * nz * nc), BF),
+            (grad_dn.shape, BF),
+            ((nz, nc, own, qcols), BF),
+            ((nz, nc, own, qcols + 128), BF),
         ],
-        (VM,) * 9,
+        (VM,) * 3 + (pl.ANY,) * 3,
         [
             VM((nz, nc, rows, qcols), BF),
             VM((nc, 128, keys), BF),
@@ -1151,11 +1120,11 @@
             VM((2, nx, ny, own, mlp_cols), BF),
             VM((nz, nc, own, mlp_cols), BF),
             VM((nz, nc, own, mlp_cols), BF),
-            VM(rest_dn.shape, BF),
-            VM((nx, nc, nz, ny, own, cols), BF),
-            VM((nx, ny, nc, nz, own, cols), BF),
-            VM((nz, nc, own, cols), BF),
-            VM((nz, nc, own, cols), BF),
+        ]
+        + [
+            VM(shape + (own, n), BF)
+            for n in (qcols, qcols + 128)
+            for shape in ((nx, nc, nz, ny), (nx, ny, nc, nz), (nz, nc))
         ]
         + Reduce.buffers(nz, rows, width)
         + [DMA((3,))]
@@ -1163,11 +1132,93 @@
         + [DMA((near,))] * 2
         + [DMA((peers,))] * 2
         + Reduce.SEMS
-        + [DMA((peers,))] * 2
-        + [DMA((members,))] * 2
-        + [DMA((4,))],
+        + ([DMA((peers,))] * 2 + [DMA((members,))] * 2) * 2
+        + [DMA((6,))],
         6,
     )
+
+
+def final_kernel(
+    dims, dn1, tokens, dx2, raw_gate, raw_up, came_dn, own_o, own_p, gains, w_query, w_key, w_value, w_gate, w_up,
+    input_grad, grad_query, grad_key, grad_value, grad_out_t, grad_gate, grad_up, grad_down, grad_gain,
+):
+    nx, nc, nz, ny = dims
+    team = nz * nc
+    value = tokens[...].astype(F32)
+    total = dn1[...]
+    inverse = lax.rsqrt(jnp.mean(value * value, axis=-1, keepdims=True) + EPSILON)
+    normed = value * inverse
+    input_grad[...] = dx2[...] + inverse * (total - normed * jnp.mean(total * normed, axis=-1, keepdims=True))
+
+    down = came_dn[0, 0].astype(F32)
+    for px, py in others(nx, ny):
+        down = down + came_dn[px, py].astype(F32)
+    grad_down[...] = down
+
+    gain = gains[:, 1:2]
+    both = 0.0
+    for raw, weight, grad in ((raw_gate, w_gate, grad_gate), (raw_up, w_up, grad_up)):
+        got = raw[...].astype(F32)
+        grad[...] = got * gain
+        both = both + got * weight[...].astype(F32)
+    dots_mlp = jnp.sum(both, axis=-1, keepdims=True)
+
+    gain = gains[:, 0:1]
+    qcols = own_o.shape[-1]
+    both = 0.0
+    heads = []
+    for t in range(team):
+        block = own_p[t // nc, t % nc].astype(F32)
+        cols = slice(t * qcols, (t + 1) * qcols)
+        grad_out_t[:, cols] = own_o[t // nc, t % nc].astype(F32)
+        grad_query[:, cols] = block[:, :qcols] * gain
+        both = both + block[:, :qcols] * w_query[:, cols].astype(F32)
+        if t % (team // KV_HEADS):
+            heads[-1] = heads[-1] + block[:, qcols:]
+        else:
+            heads.append(block[:, qcols:])
+    dots = jnp.sum(both, axis=-1, keepdims=True)
+    for pair in range(KV_HEADS // 2):
+        one, two = heads[2 * pair], heads[2 * pair + 1]
+        first = lanes(one.shape) < 64
+        cols = slice(pair * 128, pair * 128 + 128)
+        key = jnp.where(first, one, pltpu.roll(two, 64, 1))
+        val = jnp.where(first, pltpu.roll(one, 64, 1), two)
+        grad_key[:, cols] = key * gain
+        grad_value[:, cols] = val * gain
+        both = key * w_key[:, cols].astype(F32) + val * w_value[:, cols].astype(F32)
+        dots = dots + jnp.sum(both, axis=-1, keepdims=True)
+    shape = grad_gain.shape
+    grad_gain[...] = jnp.where(lanes(shape) < 64, dots, dots_mlp)
+
+
+def final_call(
+    dims, dn1, tokens, dx2, raw_gate, raw_up, came_dn, own_o, own_p, gains, w_query, w_key, w_value, w_gate, w_up
+):
+    own = w_query.shape[0]
+    steps = max(own // ROWS, 1)
+
+    def rows_of(shape, axis):
+        count = shape[axis]
+        each = count if steps == 1 else -(-count // (steps * ROWS)) * ROWS
+        block = shape[:axis] + (each,) + shape[axis + 1 :]
+        return pl.BlockSpec(block, lambda i: tuple(i if k == axis else 0 for k in range(len(shape))))
+
+    operands = (
+        dn1, tokens, dx2, raw_gate, raw_up, came_dn, own_o, own_p, gains, w_query, w_key, w_value, w_gate, w_up
+    )
+    outs = [
+        dn1.shape, w_query.shape, w_key.shape, w_value.shape, w_query.shape, w_gate.shape, w_up.shape,
+        came_dn.shape[2:], (own, 128),
+    ]
+    return pl.pallas_call(
+        functools.partial(final_kernel, dims),
+        grid=(steps,),
+        out_shape=[jax.ShapeDtypeStruct(s, F32) for s in outs],
+        in_specs=[rows_of(a.shape, len(a.shape) - 2) for a in operands],
+        out_specs=[rows_of(s, 0) for s in outs],
+        compiler_params=pltpu.CompilerParams(vmem_limit_bytes=60 << 20),
+    )(*operands)
 
 
 def shards(
@@ -1192,11 +1243,14 @@
     n1g, w_attn, tab, q, kk, vv, stat, ob, mid, n2g, cotg, w_mlp, w_dn = forward_call(
         dims, tokens, table, gains, w_query, w_key, w_value, w_out.T, w_gate, w_up, w_down, cotangent
     )
-    dx2, dag, output, came_mlp, came_dn, rest_dn = mlp_call(dims, n2g, cotg, w_mlp, w_dn, mid, cotangent)
+    dx2, dag, output, came_mlp, grad_dn = mlp_call(dims, n2g, cotg, w_mlp, w_dn, mid, cotangent)
+    dn1, raw_gate, raw_up, came_dn, own_o, own_p = backward_call(
+        dims, dag, w_attn, tab, q, kk, vv, stat, ob, came_mlp, grad_dn, n1g
+    )
     (
         input_grad, grad_query, grad_key, grad_value, grad_out_t, grad_gate, grad_up, grad_down, grad_gain
-    ) = backward_call(
-        dims, dag, w_attn, tab, q, kk, vv, stat, ob, came_mlp, came_dn, rest_dn, n1g, tokens, dx2, gains,
+    ) = final_call(
+        dims, dn1, tokens, dx2, raw_gate, raw_up, came_dn, own_o, own_p, gains,
         w_query, w_key, w_value, w_gate, w_up,
     )
     return (

time: 420 us -> 390 us (0.929)
  Pallas kernels: 397 us -> 376 us
  local copies, waits for them, and re-layouts: 11 us -> 2.52 us
    pallas_call x3, Pallas kernels: 397 us -> 369 us  [call(): pl.pallas_call(kernel, out_shape=[jax.ShapeDtypeStruct(s, t) for s, t in...]
    unnamed x25 -> x3, local copies, waits for them, and re-layouts: 9.26 us -> 0.8 us
    pallas_call x0 -> x1, Pallas kernels: none -> 7.16 us  [final_call(): pl.pallas_call(functools.partial(final_kernel, dims), grid=(steps,), out_...]
where the time goes in v6:
time: 390 us; the launch traced here: 383 us
  Pallas kernels  376 us (96%)
    pallas_call x3, Pallas kernels, call(): pl.pallas_call(kernel, out_shape=[jax.ShapeDtypeStruct(s, t) for s, t in...  369 us

profile of v6, /device:TPU:31, one launch (start us, length us, event | category | flops | bytes accessed | tf_op | source)
XLA Modules:
  0.0 383.3 jit_solution(3946964250232299482)
XLA Ops:
  0.6 0.7 convert_element_type.9
  1.3 0.7 convert_element_type.10
  2.0 0.7 pad_maximum_fusion.1
  2.6 0.1 copy.30
  2.8 0.6 convert_element_type.11.gains
  3.4 0.1 broadcast_in_dim.2
  3.5 0.3 multiply_cosine_fusion
  3.8 0.7 pad_maximum_fusion.table
  4.5 175.9 %shard_map.212 = (bf16[4,2,128,2048]{3,2,1,0:T(8,128)(2,1)}, bf16[2,2,4,2,64,640]{5,4,3,2,1,0:T(8,128)(2,1)}, f32[4,2,128,128]{3,2,1,0:T(8,128)}, bf16[4,2,128,2...) custom-call(bf16[128,2048]{1,0:T(8,128)(2,1)} %tokens.3, ...), custom_call_target="tpu_custom_call" | custom-call | tf_op jit(solution)/shard_map/pallas_call | solution.py:345
  180.4 103.9 %shard_map.213 = (f32[128,2048]{1,0:T(8,128)}, bf16[4,2,128,2048]{3,2,1,0:T(8,128)(2,1)}, bf16[128,2048]{1,0:T(8,128)(2,1)}, bf16[2,2,2,4,64,1408]{5,4,3,2,1,0:T(8,128)(2,1)}, bf16[2,2,176,2048]{3,2,1,0:T(8,128)(2,1)}) custom-call(bf16[4,2,128,2048]{3,2,1,0:T(8,128)(2,1)} %get-tuple-element.44.n2g, bf16[4,2,128,2048]{3,2,1,0:T(8,128)(2,1)} %get-tuple-element.45.cotg, ...), custom_call_target="tpu_custom_call" | custom-call | tf_op jit(solution)/shard_map/pallas_call | solution.py:345
  284.3 89.1 %shard_map.214 = (f32[128,2048]{1,0:T(8,128)}, bf16[64,5632]{1,0:T(8,128)(2,1)}, bf16[64,5632]{1,0:T(8,128)(2,1)}, bf16[2,2,176,2048]{3,2,1,0:T(8,128)(2,1)}, bf...) custom-call(bf16[4,2,128,2048]{3,2,1,0:T(8,128)(2,1)} %get-tuple-element.50.dag, ...), custom_call_target="tpu_custom_call" | custom-call | tf_op jit(solution)/shard_map/pallas_call | solution.py:345
  373.4 0.0 copy-start
  373.4 7.2 %shard_map.215 = (f32[128,2048]{1,0:T(8,128)}, f32[64,2048]{1,0:T(8,128)}, f32[64,256]{1,0:T(8,128)}, f32[64,256]{1,0:T(8,128)}, f32[64,2048]{1,0:T(8,128)}, /*i...) custom-call(f32[128,2048]{1,0:T(8,128)} %get-tuple-element.61.dn1, ...), custom_call_target="tpu_custom_call" | custom-call | tf_op jit(solution)/shard_map/pallas_call | solution.py:1214
  380.5 1.5 slice_reduce_fusion
  382.1 0.0 copy-done
  382.1 0.8 copy.32
  (1 shorter events, 0.0 us)
Async XLA Ops:
  373.4 8.7 %copy-start = (bf16[128,2048]{1,0:T(8,128)(2,1)S(1)}, bf16[128,2048]{1,0:T(8,128)(2,1)}, u32[]{:S(2)}) copy-start(bf16[128,2048]{1,0:T(8,128)(2,1)} %get-tuple-element.92) | copy-start | bytes 1572868

commit v7 on v6

--- a/solution.py
+++ b/solution.py
@@ -2,6 +2,7 @@
 
 import jax
 import jax.numpy as jnp
+import numpy as np
 from jax import lax
 from jax.experimental import pallas as pl
 from jax.experimental.pallas import tpu as pltpu
@@ -382,6 +383,12 @@
     return lax.dot_general(a, b, (((0,), (0,)), ((), ())), preferred_element_type=F32)
 
 
+def column(row):
+    count = row.shape[1]
+    down = lax.broadcasted_iota(jnp.int32, (count, count), 0)
+    return jnp.sum(jnp.where(down == lanes((count, count)), row, 0.0), axis=1, keepdims=True)
+
+
 def rope_lanes(tab):
     at = lanes(tab.shape)
     cos = jnp.where(at < 32, tab, 0.0)
@@ -418,9 +425,10 @@
 
 
 def forward_kernel(
-    dims, tokens, table, gains, w_query, w_key, w_value, w_out_t, w_gate, w_up, down, cot,
-    n1_out, w_out, tab, q, kk, vv, stat, ob, mid, n2g, cotg, w_mlp, w_dn,
-    n1g, w_attn, n1, blocks, mlp_blocks, mlp_t, kv, vt, part, held, came, n2,
+    dims, tokens, positions, starts, gain_a, gain_m, frequency, w_query, w_key, w_value, w_out_t, w_gate, w_up,
+    down, cot,
+    gains, n1_out, w_out, tab, q, kk, vv, stat, ob, mid, n2g, cotg, w_mlp, w_dn,
+    n1g, w_attn, table, n1, blocks, mlp_blocks, mlp_t, kv, vt, part, held, came, n2,
     gs, gr, gl, ts, tr, ss, sr, ds, dr, ws, wr, us, ur, ys, yr, rs, rr, rxs, rxr, cs, cr, cl, ns, nr, nl, ms, mr, local,
 ):
     nx, nc, nz, ny = dims
@@ -470,8 +478,14 @@
         inverse = lax.rsqrt(jnp.mean(value * value, axis=-1, keepdims=True) + EPSILON)
         n1[at, :] = (value * inverse).astype(BF)
 
+    first_lanes = lanes((own, 128)) < 64
+    gains[...] = jnp.where(first_lanes, column(gain_a[...].astype(F32)), column(gain_m[...].astype(F32)))
     by_rows(rows, norm)
     by_rows(own, pack)
+    angle = column(positions[...].astype(F32)) * frequency[...]
+    at = lanes(angle.shape)
+    doc = jnp.broadcast_to(column(starts[...].astype(F32)), angle.shape)
+    table[...] = jnp.where(at < 32, jnp.cos(angle), jnp.where(at < 64, jnp.sin(angle), doc))
     met()
     swap.start()
     tabs.start()
@@ -489,7 +503,7 @@
             copy.start()
 
     def pack_mlp(at):
-        gain = gains[at, 1:2]
+        gain = gains[at, 64:65]
         for k, weight in enumerate((w_gate, w_up)):
             for t in range(nz * nc):
                 for i in range(nx):
@@ -607,7 +621,9 @@
         copy.wait_send()
 
 
-def forward_call(dims, tokens, table, gains, w_query, w_key, w_value, w_out_t, w_gate, w_up, down, cot):
+def forward_call(
+    dims, tokens, positions, starts, gain_a, gain_m, w_query, w_key, w_value, w_out_t, w_gate, w_up, down, cot
+):
     nx, nc, nz, ny = dims
     rows, width = tokens.shape
     own = w_query.shape[0]
@@ -617,14 +633,21 @@
     mlp_cols = 2 * w_gate.shape[1] // (nz * nc)
     keys = nz * ny * rows
     team_rows = (nz, nc, rows, width)
+    half = HEAD_DIM // 2
+    exponents = np.tile(np.arange(half), 128 // half)[None, :] * (-2.0 / HEAD_DIM)
+    frequency = jnp.asarray(10000.0**exponents, F32)
     return call(
         functools.partial(forward_kernel, dims),
-        (tokens, table, gains, w_query, w_key, w_value, w_out_t, w_gate, w_up, down, cot),
-        (VM,) * 9 + (pl.ANY, VM),
+        (
+            tokens, positions, starts, gain_a, gain_m, frequency, w_query, w_key, w_value, w_out_t, w_gate, w_up,
+            down, cot,
+        ),
+        (VM,) * 12 + (pl.ANY, VM),
         [
+            ((own, 128), F32),
             (team_rows, BF),
             ((nx, nc, nz, ny, own, cols), BF),
-            ((nz, nc) + table.shape, F32),
+            ((nz, nc, rows, 128), F32),
             ((nz, nc, rows, qcols), BF),
             ((nc, keys, 128), BF),
             ((nc, keys, 128), BF),
@@ -636,10 +659,11 @@
             ((nx, nc, nz, ny, own, mlp_cols), BF),
             ((nx, ny) + down.shape, BF),
         ],
-        (pl.ANY,) * 2 + (VM,) * 7 + (pl.ANY,) * 4,
+        (VM,) + (pl.ANY,) * 2 + (VM,) * 7 + (pl.ANY,) * 4,
         [
             VM(team_rows, BF),
             VM((nx, nc, nz, ny, own, cols), BF),
+            VM((rows, 128), F32),
             VM((rows, width), BF),
             VM((nz, nc, own, cols), BF),
             VM((nz, nc, own, mlp_cols), BF),
@@ -777,8 +801,12 @@
         lax.fori_loop(0, 4, mlp_sum, 0)
         reduce2.start()
 
-    work = [functools.partial(forward_back, k) for k in range(1, nz)]
-    work += [functools.partial(mlp_grad, far) for far in reversed(range(nx))]
+    def other_blocks():
+        for k in range(2, nz):
+            forward_back(k)
+
+    forward_back(1)
+    work = [other_blocks] + [functools.partial(mlp_grad, far) for far in reversed(range(nx))]
     end = flow(reduce, None, None, work + [sum_all])
 
     def settle(at, total):
@@ -1155,7 +1183,7 @@
         down = down + came_dn[px, py].astype(F32)
     grad_down[...] = down
 
-    gain = gains[:, 1:2]
+    gain = gains[:, 64:65]
     both = 0.0
     for raw, weight, grad in ((raw_gate, w_gate, grad_gate), (raw_up, w_up, grad_up)):
         got = raw[...].astype(F32)
@@ -1226,22 +1254,9 @@
     attn_gain, w_gate, w_up, w_down, mlp_gain,
 ):
     dims = tuple(lax.axis_size(a) for a in ALL)
-    rows = tokens.shape[0]
-
-    gains = jnp.stack([attn_gain, mlp_gain], axis=1).astype(F32)
-    half = HEAD_DIM // 2
-    frequency = 10000.0 ** (-2.0 * jnp.arange(half, dtype=F32) / HEAD_DIM)
-    angles = positions.astype(F32)[:, None] * frequency[None, :]
-    table = jnp.concatenate(
-        [
-            jnp.cos(angles),
-            jnp.sin(angles),
-            jnp.broadcast_to(doc_start.astype(F32)[:, None], (rows, HEAD_DIM)),
-        ],
-        axis=-1,
-    )
-    n1g, w_attn, tab, q, kk, vv, stat, ob, mid, n2g, cotg, w_mlp, w_dn = forward_call(
-        dims, tokens, table, gains, w_query, w_key, w_value, w_out.T, w_gate, w_up, w_down, cotangent
+    gains, n1g, w_attn, tab, q, kk, vv, stat, ob, mid, n2g, cotg, w_mlp, w_dn = forward_call(
+        dims, tokens, positions[None], doc_start[None], attn_gain[None], mlp_gain[None],
+        w_query, w_key, w_value, w_out.T, w_gate, w_up, w_down, cotangent,
     )
     dx2, dag, output, came_mlp, grad_dn = mlp_call(dims, n2g, cotg, w_mlp, w_dn, mid, cotangent)
     dn1, raw_gate, raw_up, came_dn, own_o, own_p = backward_call(

time: 390 us -> 381 us (0.977)
  Pallas kernels: 376 us -> 371 us
    pallas_call x3, Pallas kernels: 369 us -> 364 us  [call(): pl.pallas_call(kernel, out_shape=[jax.ShapeDtypeStruct(s, t) for s, t in...]
where the time goes in v7:
time: 381 us; the launch traced here: 374 us
  Pallas kernels  371 us (97%)
    pallas_call x3, Pallas kernels, call(): pl.pallas_call(kernel, out_shape=[jax.ShapeDtypeStruct(s, t) for s, t in...  364 us

profile of v7, /device:TPU:31, one launch (start us, length us, event | category | flops | bytes accessed | tf_op | source)
XLA Modules:
  0.0 374.2 jit_solution(3838111825316389383)
XLA Ops:
  0.6 175.1 %shard_map.221 = (f32[64,128]{1,0:T(8,128)}, bf16[4,2,128,2048]{3,2,1,0:T(8,128)(2,1)}, bf16[2,2,4,2,64,640]{5,4,3,2,1,0:T(8,128)(2,1)}, f32[4,2,128,128]{3,2,1,...) custom-call(bf16[128,2048]{1,0:T(8,128)(2,1)} %tokens.3, ...), custom_call_target="tpu_custom_call" | custom-call | tf_op jit(solution)/shard_map/pallas_call | solution.py:346
  175.8 101.3 %shard_map.222 = (f32[128,2048]{1,0:T(8,128)}, bf16[4,2,128,2048]{3,2,1,0:T(8,128)(2,1)}, bf16[128,2048]{1,0:T(8,128)(2,1)}, bf16[2,2,2,4,64,1408]{5,4,3,2,1,0:T(8,128)(2,1)}, bf16[2,2,176,2048]{3,2,1,0:T(8,128)(2,1)}) custom-call(bf16[4,2,128,2048]{3,2,1,0:T(8,128)(2,1)} %get-tuple-element.45.n2g, bf16[4,2,128,2048]{3,2,1,0:T(8,128)(2,1)} %get-tuple-element.46.cotg, ...), custom_call_target="tpu_custom_call" | custom-call | tf_op jit(solution)/shard_map/pallas_call | solution.py:346
  277.1 87.1 %shard_map.223 = (f32[128,2048]{1,0:T(8,128)}, bf16[64,5632]{1,0:T(8,128)(2,1)}, bf16[64,5632]{1,0:T(8,128)(2,1)}, bf16[2,2,176,2048]{3,2,1,0:T(8,128)(2,1)}, bf...) custom-call(bf16[4,2,128,2048]{3,2,1,0:T(8,128)(2,1)} %get-tuple-element.51.dag, ...), custom_call_target="tpu_custom_call" | custom-call | tf_op jit(solution)/shard_map/pallas_call | solution.py:346
  364.2 0.0 copy-start
  364.2 7.2 %shard_map.224 = (f32[128,2048]{1,0:T(8,128)}, f32[64,2048]{1,0:T(8,128)}, f32[64,256]{1,0:T(8,128)}, f32[64,256]{1,0:T(8,128)}, f32[64,2048]{1,0:T(8,128)}, /*i...) custom-call(f32[128,2048]{1,0:T(8,128)} %get-tuple-element.62.dn1, ...), custom_call_target="tpu_custom_call" | custom-call | tf_op jit(solution)/shard_map/pallas_call | solution.py:1242
  371.4 1.5 slice_reduce_fusion
  372.9 0.0 copy-done
  372.9 0.8 copy.26
Async XLA Ops:
  364.2 8.7 %copy-start = (bf16[128,2048]{1,0:T(8,128)(2,1)S(1)}, bf16[128,2048]{1,0:T(8,128)(2,1)}, u32[]{:S(2)}) copy-start(bf16[128,2048]{1,0:T(8,128)(2,1)} %get-tuple-element.92) | copy-start | bytes 1572868

commit v8 on v7

--- a/solution.py
+++ b/solution.py
@@ -873,12 +873,12 @@
 
 
 def backward_kernel(
-    dims, dag, w, tab, q, kk, vv, stat, ob, came_mlp, grad_dn, n1g,
+    dims, dag, w_in, tab_in, q_in, kk_in, vv_in, stat_in, ob_in, came_mlp, grad_dn, n1g,
     dn1, raw_gate, raw_up, came_dn, own_o, own_p,
-    do, kt, dk, dv, out, near, dqkv, part, team, stage, mlp_sum, mlp_g,
+    w, tab, q, kk, vv, stat, ob, do, kt, dk, dv, out, near, dqkv, part, team, stage, mlp_sum, mlp_g,
     grad_o, came_o, sums_o, grad_p, came_p, sums_p,
     held, came,
-    loads, us, ur, ys, yr, ws, wr, rs, rr, rxs, rxr, ds, dr, ss, sr, es, er, fs, fr, local,
+    ins, loads, us, ur, ys, yr, ws, wr, rs, rr, rxs, rxr, ds, dr, ss, sr, es, er, fs, fr, local,
 ):
     nx, nc, nz, ny = dims
     x, c, z, y = place()
@@ -889,7 +889,8 @@
     keys_span = ny * rows
     fetch_dag = pltpu.make_async_copy(dag, team, loads.at[2])
     fetch = pltpu.make_async_copy(n1g, team, loads.at[2])
-    fetch_dag.start()
+    pairs_in = zip((w_in, kk_in, q_in, tab_in, stat_in, vv_in, ob_in), (w, kk, q, tab, stat, vv, ob))
+    fetch_rest = [pltpu.make_async_copy(a, b, ins.at[i]) for i, (a, b) in enumerate(pairs_in)]
     mlp_swap = Swap(
         lambda pz, pc: mlp_sum.at[pz, pc], lambda pz, pc: mlp_g.at[pz, pc], us, ur, local.at[0], nz, nc
     )
@@ -911,15 +912,10 @@
         return pltpu.make_async_copy(came_mlp.at[:, :, pc, pz], stage.at[i % 2], loads.at[i % 2])
 
     load(0).start()
+    fetch_dag.start()
+    for copy in fetch_rest:
+        copy.start()
     met = greet(*dims, cross=True)
-
-    def turned(i, carry):
-        pc, pz = i // nz, lax.rem(i, nz)
-        at = pl.ds(pl.multiple_of(pz * keys_span, keys_span), keys_span)
-        kt[pc, :, at] = kk[pc, at, :].astype(F32).T.astype(BF)
-        return carry
-
-    lax.fori_loop(0, nc * nz, turned, 0)
     early = 2 * (nx * ny - 1) // 3
     for i, copy in enumerate(list(mlp_swap.copies()) + [mlp_swap.own()]):
         if i + 1 < len(steps):
@@ -940,6 +936,16 @@
             dn.own().start()
         copy.start()
     fetch_dag.wait()
+    for copy in fetch_rest:
+        copy.wait()
+
+    def turned(i, carry):
+        pc, pz = i // nz, lax.rem(i, nz)
+        at = pl.ds(pl.multiple_of(pz * keys_span, keys_span), keys_span)
+        kt[pc, :, at] = kk[pc, at, :].astype(F32).T.astype(BF)
+        return carry
+
+    lax.fori_loop(0, nc * nz, turned, 0)
 
     def project(i, carry):
         weights = w[..., qcols + 128 :].reshape(width, qcols)
@@ -1125,7 +1131,7 @@
     return call(
         functools.partial(backward_kernel, dims),
         (dag, w, tab, q, kk, vv, stat, ob, came_mlp, grad_dn, n1g),
-        (pl.ANY,) + (VM,) * 7 + (pl.ANY,) * 3,
+        (pl.ANY,) * 11,
         [
             ((rows, width), F32),
             ((own, mlp_cols // 2 * nz * nc), BF),
@@ -1135,7 +1141,8 @@
             ((nz, nc, own, qcols + 128), BF),
         ],
         (VM,) * 3 + (pl.ANY,) * 3,
-        [
+        [VM(a.shape, a.dtype) for a in (w, tab, q, kk, vv, stat, ob)]
+        + [
             VM((nz, nc, rows, qcols), BF),
             VM((nc, 128, keys), BF),
             VM((nc, keys, 128), F32),
@@ -1155,7 +1162,7 @@
             for shape in ((nx, nc, nz, ny), (nx, ny, nc, nz), (nz, nc))
         ]
         + Reduce.buffers(nz, rows, width)
-        + [DMA((3,))]
+        + [DMA((7,)), DMA((3,))]
         + [DMA((members,))] * 2
         + [DMA((near,))] * 2
         + [DMA((peers,))] * 2
@@ -1167,11 +1174,12 @@
 
 
 def final_kernel(
-    dims, dn1, tokens, dx2, raw_gate, raw_up, came_dn, own_o, own_p, gains, w_query, w_key, w_value, w_gate, w_up,
-    input_grad, grad_query, grad_key, grad_value, grad_out_t, grad_gate, grad_up, grad_down, grad_gain,
+    dims, low, dn1, tokens, dx2, raw_gate, raw_up, came_dn, own_o, own_p, gains, w_query, w_key, w_value, w_gate, w_up,
+    output, input_grad, grad_query, grad_key, grad_value, grad_out_t, grad_gate, grad_up, grad_down, grad_gain,
 ):
     nx, nc, nz, ny = dims
     team = nz * nc
+    output[...] = low[...]
     value = tokens[...].astype(F32)
     total = dn1[...]
     inverse = lax.rsqrt(jnp.mean(value * value, axis=-1, keepdims=True) + EPSILON)
@@ -1221,7 +1229,8 @@
 
 
 def final_call(
-    dims, dn1, tokens, dx2, raw_gate, raw_up, came_dn, own_o, own_p, gains, w_query, w_key, w_value, w_gate, w_up
+    dims, low, dn1, tokens, dx2, raw_gate, raw_up, came_dn, own_o, own_p, gains,
+    w_query, w_key, w_value, w_gate, w_up,
 ):
     own = w_query.shape[0]
     steps = max(own // ROWS, 1)
@@ -1233,16 +1242,16 @@
         return pl.BlockSpec(block, lambda i: tuple(i if k == axis else 0 for k in range(len(shape))))
 
     operands = (
-        dn1, tokens, dx2, raw_gate, raw_up, came_dn, own_o, own_p, gains, w_query, w_key, w_value, w_gate, w_up
+        low, dn1, tokens, dx2, raw_gate, raw_up, came_dn, own_o, own_p, gains, w_query, w_key, w_value, w_gate, w_up
     )
     outs = [
-        dn1.shape, w_query.shape, w_key.shape, w_value.shape, w_query.shape, w_gate.shape, w_up.shape,
+        low.shape, dn1.shape, w_query.shape, w_key.shape, w_value.shape, w_query.shape, w_gate.shape, w_up.shape,
         came_dn.shape[2:], (own, 128),
     ]
     return pl.pallas_call(
         functools.partial(final_kernel, dims),
         grid=(steps,),
-        out_shape=[jax.ShapeDtypeStruct(s, F32) for s in outs],
+        out_shape=[jax.ShapeDtypeStruct(s, BF if i == 0 else F32) for i, s in enumerate(outs)],
         in_specs=[rows_of(a.shape, len(a.shape) - 2) for a in operands],
         out_specs=[rows_of(s, 0) for s in outs],
         compiler_params=pltpu.CompilerParams(vmem_limit_bytes=60 << 20),
@@ -1263,9 +1272,9 @@
         dims, dag, w_attn, tab, q, kk, vv, stat, ob, came_mlp, grad_dn, n1g
     )
     (
-        input_grad, grad_query, grad_key, grad_value, grad_out_t, grad_gate, grad_up, grad_down, grad_gain
+        output, input_grad, grad_query, grad_key, grad_value, grad_out_t, grad_gate, grad_up, grad_down, grad_gain
     ) = final_call(
-        dims, dn1, tokens, dx2, raw_gate, raw_up, came_dn, own_o, own_p, gains,
+        dims, output, dn1, tokens, dx2, raw_gate, raw_up, came_dn, own_o, own_p, gains,
         w_query, w_key, w_value, w_gate, w_up,
     )
     return (

time: 381 us -> 380 us (level)
  no operation moved by 1% of the time
where the time goes in v8:
time: 380 us; the launch traced here: 372 us
  Pallas kernels  370 us (97%)
    pallas_call x3, Pallas kernels, call(): pl.pallas_call(kernel, out_shape=[jax.ShapeDtypeStruct(s, t) for s, t in...  362 us

profile of v8, /device:TPU:31, one launch (start us, length us, event | category | flops | bytes accessed | tf_op | source)
XLA Modules:
  0.0 372.3 jit_solution(15227024857307015714)
XLA Ops:
  0.6 175.2 %shard_map.221 = (f32[64,128]{1,0:T(8,128)}, bf16[4,2,128,2048]{3,2,1,0:T(8,128)(2,1)}, bf16[2,2,4,2,64,640]{5,4,3,2,1,0:T(8,128)(2,1)}, f32[4,2,128,128]{3,2,1,...) custom-call(bf16[128,2048]{1,0:T(8,128)(2,1)} %tokens.3, ...), custom_call_target="tpu_custom_call" | custom-call | tf_op jit(solution)/shard_map/pallas_call | solution.py:346
  175.8 101.3 %shard_map.222 = (f32[128,2048]{1,0:T(8,128)}, bf16[4,2,128,2048]{3,2,1,0:T(8,128)(2,1)}, bf16[128,2048]{1,0:T(8,128)(2,1)}, bf16[2,2,2,4,64,1408]{5,4,3,2,1,0:T(8,128)(2,1)}, bf16[2,2,176,2048]{3,2,1,0:T(8,128)(2,1)}) custom-call(bf16[4,2,128,2048]{3,2,1,0:T(8,128)(2,1)} %get-tuple-element.46.n2g, bf16[4,2,128,2048]{3,2,1,0:T(8,128)(2,1)} %get-tuple-element.47.cotg, ...), custom_call_target="tpu_custom_call" | custom-call | tf_op jit(solution)/shard_map/pallas_call | solution.py:346
  277.1 85.9 %shard_map.223 = (f32[128,2048]{1,0:T(8,128)}, bf16[64,5632]{1,0:T(8,128)(2,1)}, bf16[64,5632]{1,0:T(8,128)(2,1)}, bf16[2,2,176,2048]{3,2,1,0:T(8,128)(2,1)}, bf...) custom-call(bf16[4,2,128,2048]{3,2,1,0:T(8,128)(2,1)} %get-tuple-element.52.dag, ...), custom_call_target="tpu_custom_call" | custom-call | tf_op jit(solution)/shard_map/pallas_call | solution.py:346
  362.9 7.3 %shard_map.224 = (bf16[128,2048]{1,0:T(8,128)(2,1)}, f32[128,2048]{1,0:T(8,128)}, f32[64,2048]{1,0:T(8,128)}, f32[64,256]{1,0:T(8,128)}, f32[64,256]{1,0:T(8,128...) custom-call(bf16[128,2048]{1,0:T(8,128)(2,1)} %get-tuple-element.51., ...), custom_call_target="tpu_custom_call" | custom-call | tf_op jit(solution)/shard_map/pallas_call | solution.py:1251
  370.3 1.5 slice_reduce_fusion

commit v9 on v8

--- a/solution.py
+++ b/solution.py
@@ -1175,7 +1175,7 @@
 
 def final_kernel(
     dims, low, dn1, tokens, dx2, raw_gate, raw_up, came_dn, own_o, own_p, gains, w_query, w_key, w_value, w_gate, w_up,
-    output, input_grad, grad_query, grad_key, grad_value, grad_out_t, grad_gate, grad_up, grad_down, grad_gain,
+    output, input_grad, grad_query, grad_key, grad_value, grad_out_t, grad_gate, grad_up, grad_down, grad_gain_a, grad_gain_m,
 ):
     nx, nc, nz, ny = dims
     team = nz * nc
@@ -1224,8 +1224,12 @@
         grad_value[:, cols] = val * gain
         both = key * w_key[:, cols].astype(F32) + val * w_value[:, cols].astype(F32)
         dots = dots + jnp.sum(both, axis=-1, keepdims=True)
-    shape = grad_gain.shape
-    grad_gain[...] = jnp.where(lanes(shape) < 64, dots, dots_mlp)
+    shape = (dots.shape[0], grad_gain_a.shape[1])
+    step = pl.program_id(0)
+    mine = lanes(shape) == step * shape[0] + lax.broadcasted_iota(jnp.int32, shape, 0)
+    for target, column_of in ((grad_gain_a, dots), (grad_gain_m, dots_mlp)):
+        row = jnp.sum(jnp.where(mine, column_of, 0.0), axis=0, keepdims=True)
+        target[...] = jnp.where(step == 0, row, target[...] + row)
 
 
 def final_call(
@@ -1246,14 +1250,14 @@
     )
     outs = [
         low.shape, dn1.shape, w_query.shape, w_key.shape, w_value.shape, w_query.shape, w_gate.shape, w_up.shape,
-        came_dn.shape[2:], (own, 128),
+        came_dn.shape[2:], (1, own), (1, own),
     ]
     return pl.pallas_call(
         functools.partial(final_kernel, dims),
         grid=(steps,),
         out_shape=[jax.ShapeDtypeStruct(s, BF if i == 0 else F32) for i, s in enumerate(outs)],
         in_specs=[rows_of(a.shape, len(a.shape) - 2) for a in operands],
-        out_specs=[rows_of(s, 0) for s in outs],
+        out_specs=[rows_of(s, 0) for s in outs[:-2]] + [pl.BlockSpec((1, own), lambda i: (0, 0))] * 2,
         compiler_params=pltpu.CompilerParams(vmem_limit_bytes=60 << 20),
     )(*operands)
 
@@ -1272,14 +1276,15 @@
         dims, dag, w_attn, tab, q, kk, vv, stat, ob, came_mlp, grad_dn, n1g
     )
     (
-        output, input_grad, grad_query, grad_key, grad_value, grad_out_t, grad_gate, grad_up, grad_down, grad_gain
+        output, input_grad, grad_query, grad_key, grad_value, grad_out_t, grad_gate, grad_up, grad_down,
+        grad_gain_a, grad_gain_m,
     ) = final_call(
         dims, output, dn1, tokens, dx2, raw_gate, raw_up, came_dn, own_o, own_p, gains,
         w_query, w_key, w_value, w_gate, w_up,
     )
     return (
-        output, input_grad, grad_query, grad_key, grad_value, grad_out_t.T, grad_gain[:, 0],
-        grad_gate, grad_up, grad_down, grad_gain[:, 64],
+        output, input_grad, grad_query, grad_key, grad_value, grad_out_t.T, grad_gain_a[0],
+        grad_gate, grad_up, grad_down, grad_gain_m[0],
     )
 
 

time: 380 us -> 378 us (level)
  no operation moved by 1% of the time
where the time goes in v9:
time: 378 us; the launch traced here: 371 us
  Pallas kernels  370 us (98%)
    pallas_call x3, Pallas kernels, call(): pl.pallas_call(kernel, out_shape=[jax.ShapeDtypeStruct(s, t) for s, t in...  362 us

profile of v9, /device:TPU:31, one launch (start us, length us, event | category | flops | bytes accessed | tf_op | source)
XLA Modules:
  0.0 370.7 jit_solution(985746921338050211)
XLA Ops:
  0.6 175.2 %shard_map.221 = (f32[64,128]{1,0:T(8,128)}, bf16[4,2,128,2048]{3,2,1,0:T(8,128)(2,1)}, bf16[2,2,4,2,64,640]{5,4,3,2,1,0:T(8,128)(2,1)}, f32[4,2,128,128]{3,2,1,...) custom-call(bf16[128,2048]{1,0:T(8,128)(2,1)} %tokens.3, ...), custom_call_target="tpu_custom_call" | custom-call | tf_op jit(solution)/shard_map/pallas_call | solution.py:346
  175.8 101.3 %shard_map.222 = (f32[128,2048]{1,0:T(8,128)}, bf16[4,2,128,2048]{3,2,1,0:T(8,128)(2,1)}, bf16[128,2048]{1,0:T(8,128)(2,1)}, bf16[2,2,2,4,64,1408]{5,4,3,2,1,0:T(8,128)(2,1)}, bf16[2,2,176,2048]{3,2,1,0:T(8,128)(2,1)}) custom-call(bf16[4,2,128,2048]{3,2,1,0:T(8,128)(2,1)} %get-tuple-element.47.n2g, bf16[4,2,128,2048]{3,2,1,0:T(8,128)(2,1)} %get-tuple-element.48.cotg, ...), custom_call_target="tpu_custom_call" | custom-call | tf_op jit(solution)/shard_map/pallas_call | solution.py:346
  277.1 85.8 %shard_map.223 = (f32[128,2048]{1,0:T(8,128)}, bf16[64,5632]{1,0:T(8,128)(2,1)}, bf16[64,5632]{1,0:T(8,128)(2,1)}, bf16[2,2,176,2048]{3,2,1,0:T(8,128)(2,1)}, bf...) custom-call(bf16[4,2,128,2048]{3,2,1,0:T(8,128)(2,1)} %get-tuple-element.53.dag, ...), custom_call_target="tpu_custom_call" | custom-call | tf_op jit(solution)/shard_map/pallas_call | solution.py:346
  362.9 7.4 %shard_map.224 = (bf16[128,2048]{1,0:T(8,128)(2,1)}, f32[128,2048]{1,0:T(8,128)}, f32[64,2048]{1,0:T(8,128)}, f32[64,256]{1,0:T(8,128)}, f32[64,256]{1,0:T(8,128...) custom-call(bf16[128,2048]{1,0:T(8,128)(2,1)} %get-tuple-element.52., ...), custom_call_target="tpu_custom_call" | custom-call | tf_op jit(solution)/shard_map/pallas_call | solution.py:1255
